TPU v7x, 32 devices: a whole 2x2x4 slice. The times are simulated.
32 devices in a mesh: ctx: 8 (over y, x, core), head: 4 (over z).
Axes of the slice: x: 2, y: 2, z: 4, core: 2. Of those that a mesh axis runs over, the one named last changes fastest.
Arguments:
- queries: bfloat16 [2, 1536, 4096], P(None, 'ctx', 'head'), may hold values from -6 to 6
- key_rows: bfloat16 [2, 1536, 4096], P(None, 'ctx', 'head'), may hold values from -6 to 6
- value_rows: bfloat16 [2, 1536, 4096], P(None, 'ctx', 'head'), may hold values from -6 to 6
- out_weight: bfloat16 [4096, 4096], P('head'), may hold values from -0.09375 to 0.09375
- cotangent: bfloat16 [2, 1536, 4096], P(None, 'ctx', 'head'), may hold values from -6 to 6
Outputs:
- layer_output: bfloat16 [2, 1536, 4096], P(None, 'ctx', 'head')
- query_grad: bfloat16 [2, 1536, 4096], P(None, 'ctx', 'head')
- key_grad: bfloat16 [2, 1536, 4096], P(None, 'ctx', 'head')
- value_grad: bfloat16 [2, 1536, 4096], P(None, 'ctx', 'head')
- weight_grad: float32 [4096, 4096], P('head', 'ctx')
All inputs are finite; a program needn't handle non-finite values.
Results may differ from a plain program's by a relative error of at most 0.015.
Values may be sent and summed in bfloat16 or wider, within the bound.
A program may use at most 128 MiB of HBM per device.

v0:
```python
import jax
import jax.numpy as jnp
from jax import lax
from jax.sharding import PartitionSpec as P

DH = 128


epsilon = 1e-06


def entering(part, axis, combine, identity, reverse):
    count = lax.axis_size(axis)
    place = lax.axis_index(axis)
    ahead = count - 1 - place if reverse else place
    gathered = lax.all_gather(part, axis)
    state = jnp.zeros_like(part) + jnp.asarray(identity, part.dtype)

    def one(hop, state):
        source = count - 1 - hop if reverse else hop
        return combine(state, lax.dynamic_index_in_dim(gathered, source, 0, False))

    return lax.fori_loop(0, ahead, one, state)


def split_heads(array):
    length = array.shape[1]
    return array.reshape(2, length, array.shape[2] // DH, DH).transpose(0, 2, 1, 3)


def join_heads(array):
    length = array.shape[2]
    return array.transpose(0, 2, 1, 3).reshape(2, length, array.shape[1] * DH)


def rms_normalize(attended):
    return attended / jnp.sqrt(jnp.mean(attended * attended, axis=-1, keepdims=True) + epsilon)


def add_states(earlier, later):
    return earlier + later


def shards(queries, key_rows, value_rows, out_weight, cotangent):
    head_scale = DH ** (-0.5)
    length = queries.shape[1]
    rows_index = lax.broadcasted_iota(jnp.int32, (length, length), 0)
    cols_index = lax.broadcasted_iota(jnp.int32, (length, length), 1)
    lower = rows_index >= cols_index
    query_heads = split_heads(queries)
    key_heads = split_heads(key_rows)
    value_heads = split_heads(value_rows)
    raw = (
        jnp.einsum("bhtd,bhsd->bhts", query_heads, key_heads, preferred_element_type=jnp.float32)
        * head_scale
    )
    scores = jnp.where(lower, raw, 0.0).astype(jnp.bfloat16)
    local_state = jnp.einsum(
        "bhsd,bhse->bhde", key_heads, value_heads, preferred_element_type=jnp.float32
    )
    state = entering(local_state, "ctx", add_states, jnp.zeros_like(local_state), False)
    state_bf = state.astype(jnp.bfloat16)
    attended = jnp.einsum(
        "bhts,bhsd->bhtd", scores, value_heads, preferred_element_type=jnp.float32
    )
    attended = attended + head_scale * jnp.einsum(
        "bhtd,bhde->bhte", query_heads, state_bf, preferred_element_type=jnp.float32
    )
    normed_flat = join_heads(rms_normalize(attended).astype(jnp.bfloat16))
    partial_value = jnp.einsum(
        "btr,rc->btc", normed_flat, out_weight, preferred_element_type=jnp.float32
    )
    layer_output = lax.psum_scatter(
        partial_value.astype(jnp.bfloat16), "head", scatter_dimension=2, tiled=True
    )
    grad_all = lax.all_gather(cotangent, "head", axis=2, tiled=True)
    normed_grad = jnp.einsum(
        "btc,rc->btr", grad_all, out_weight, preferred_element_type=jnp.float32
    )
    weight_term = jnp.einsum(
        "btr,btc->rc", normed_flat, grad_all, preferred_element_type=jnp.float32
    )
    token_factor = (2 * length * lax.axis_size("ctx")) ** (-0.5)
    weight_grad = (
        lax.psum_scatter(
            weight_term.astype(jnp.bfloat16), "ctx", scatter_dimension=1, tiled=True
        ).astype(jnp.float32)
        * token_factor
    )
    pullback = jax.vjp(rms_normalize, attended)[1]
    attended_grad = pullback(split_heads(normed_grad))[0].astype(jnp.bfloat16)
    local_grad_state = jnp.einsum(
        "bhtd,bhte->bhde", query_heads, attended_grad, preferred_element_type=jnp.float32
    )
    grad_state = entering(
        local_grad_state, "ctx", add_states, jnp.zeros_like(local_grad_state), True
    )
    grad_state_bf = grad_state.astype(jnp.bfloat16)
    raw_grad = (
        jnp.einsum(
            "bhtd,bhsd->bhts", attended_grad, value_heads, preferred_element_type=jnp.float32
        )
        * head_scale
    )
    score_grad = jnp.where(lower, raw_grad, 0.0).astype(jnp.bfloat16)
    query_part = jnp.einsum(
        "bhts,bhsd->bhtd", score_grad, key_heads, preferred_element_type=jnp.float32
    )
    query_part = query_part + head_scale * jnp.einsum(
        "bhte,bhde->bhtd", attended_grad, state_bf, preferred_element_type=jnp.float32
    )
    key_part = jnp.einsum(
        "bhts,bhtd->bhsd", score_grad, query_heads, preferred_element_type=jnp.float32
    )
    key_part = key_part + head_scale * jnp.einsum(
        "bhse,bhde->bhsd", value_heads, grad_state_bf, preferred_element_type=jnp.float32
    )
    value_part = jnp.einsum(
        "bhts,bhte->bhse", scores, attended_grad, preferred_element_type=jnp.float32
    )
    value_part = value_part + head_scale * jnp.einsum(
        "bhsd,bhde->bhse", key_heads, grad_state_bf, preferred_element_type=jnp.float32
    )
    query_grad = join_heads(query_part.astype(jnp.bfloat16))
    key_grad = join_heads(key_part.astype(jnp.bfloat16))
    value_grad = join_heads(value_part.astype(jnp.bfloat16))
    return (layer_output, query_grad, key_grad, value_grad, weight_grad)


def solution(mesh):
    in_specs = (
        P(None, "ctx", "head"),
        P(None, "ctx", "head"),
        P(None, "ctx", "head"),
        P("head", None),
        P(None, "ctx", "head"),
    )
    out_specs = (
        P(None, "ctx", "head"),
        P(None, "ctx", "head"),
        P(None, "ctx", "head"),
        P(None, "ctx", "head"),
        P("head", "ctx"),
    )
    return jax.shard_map(shards, mesh=mesh, in_specs=in_specs, out_specs=out_specs, check_vma=False)
```

profile of v0, /device:TPU:0, one launch (start us, length us, event | category | flops | bytes accessed | tf_op | source)
XLA Modules:
  0.0 339.3 jit_solution(7701241001959293072)
XLA Ops:
  7.2 1.1 copy-done
  8.3 2.7 fusion.24
  11.1 0.7 all-gather.6.cloned.1.call-update
  11.9 0.3 copy-done.5
  12.1 0.2 copy-done.7
  12.4 1.7 select_convert_fusion.1
  14.1 54.2 %all-gather.8.cloned.1.call-done = f32[16,8,128,128]{3,2,1,0:T(8,128)} async-done(((f32[2,8,128,128]{3,2,1,0:T(8,128)}), f32[16,8,128,128]{3,2,1,0:T(8,128)}) %all-gather.8.cloned.1.call-update) | async-done | bytes 8388624 | tf_op jit(solution)/shard_map/all_gather | solution.py:16
  68.3 0.1 broadcast.69.clone
  68.4 1.6 convolution_multiply_fusion
  70.0 0.8 multiply_reduce_fusion
  70.9 1.1 copy-done.1
  72.0 1.4 fusion.28
  73.4 59.9 %all-gather.6.cloned.1.call-done = bf16[2,192,4096]{2,1,0:T(8,128)(2,1)} async-done(((bf16[2,192,1024]{2,1,0:T(8,128)(2,1)}), bf16[2,192,4096]{2,1,0:T(8,128)(2,1)}) %all-gather.6.cloned.1.call-update) | async-done | bytes 3145744 | tf_op jit(solution)/shard_map/all_gather | solution.py:76
  133.3 9.9 %bitcast_convert_fusion = bf16[1024,4096]{1,0:T(8,128)(2,1)} fusion(bf16[2,192,4096]{2,1,0:T(8,128)(2,1)} %all-gather.6.cloned.1.call-done, bf16[2,8,24,8,128]{4,3,2,1,0:T(8,128)(2,1)} %fusion.28), kind=kOutput, calls=%fused_computation.2 | convolution fusion | flops 3225419776 | bytes 12320768 | tf_op jit(solution)/shard_map/btr,btc->rc/dot_general | solution.py:80
  143.3 0.0 all-gather.10.cloned.1.call-start
  143.3 7.0 %fusion.16 = f32[2,24,8,8,128]{4,3,2,1,0:T(8,128)S(1)} fusion(bf16[2,192,4096]{2,1,0:T(8,128)(2,1)} %all-gather.6.cloned.1.call-done, bf16[1024,4096]{1,0:T(8,128)(2,1)} %param.12), kind=kOutput, calls=%fused_computation.28 | convolution fusion | flops 3221225472 | bytes 13107200 | tf_op jit(solution)/shard_map/btc,rc->btr/dot_general | solution.py:77
  150.3 1.1 fusion.11
  151.4 1.0 fusion.7
  152.5 0.9 copy-done.3
  153.3 0.5 convolution_bitcast_fusion
  153.8 1.4 copy.34
  155.2 0.2 reduce-scatter.3.cloned.1.call-start
  155.5 9.5 %fusion.4 = bf16[2,192,4096]{2,1,0:T(8,128)(2,1)} fusion(bf16[1024,4096]{1,0:T(8,128)(2,1)} %param.12, bf16[2,8,24,8,128]{4,3,2,1,0:T(8,128)(2,1)} %fusion.28), kind=kOutput, calls=%fused_computation.7 | convolution fusion | flops 3222798336 | bytes 12320768 | tf_op jit(solution)/shard_map/btr,rc->btc/dot_general | solution.py:70
  165.0 1.1 copy-done.4
  166.1 0.6 select_convert_fusion
  166.8 0.6 copy-done.6
  167.4 0.6 fusion.26
  167.9 0.5 fusion.19
  168.4 1.1 copy.111
  169.5 0.6 copy-done.11
  170.1 1.9 fusion.49
  172.1 2.0 fusion.27
  174.0 39.4 %reduce-scatter.5.cloned.1.call-done = bf16[1024,512]{1,0:T(8,128)(2,1)} async-done(((bf16[1024,4096]{1,0:T(8,128)(2,1)}), bf16[1024,512]{1,0:T(8,128)(2,1)}) %reduce-scatter.5.cloned.1.call-update) | async-done | bytes 1048592 | tf_op jit(solution)/shard_map/reduce_scatter | solution.py:85
  213.4 2.8 convert_multiply_fusion
  216.3 53.4 %all-gather.10.cloned.1.call-done = f32[16,8,128,128]{3,2,1,0:T(8,128)} async-done(((f32[2,8,128,128]{3,2,1,0:T(8,128)}), f32[16,8,128,128]{3,2,1,0:T(8,128)}) %all-gather.10.cloned.1.call-update) | async-done | bytes 8388624 | tf_op jit(solution)/shard_map/all_gather | solution.py:16
  269.7 0.1 broadcast.69
  269.8 10.7 %while.23 = (s32[]{:T(128)}, f32[2,8,128,128]{3,2,1,0:T(8,128)S(1)}, s32[]{:T(128)}, f32[8,2,8,128,128]{4,3,2,1,0:T(8,128)}, s32[]{:T(128)}, /*index=5*/s32[]{:T(128)}, s32[]{:T(128)}, s32[]{:T(128)}) while((s32[]{:T(128)}, f32[2,8,128,128]{3,2,1,0:T(8,128)S(1)}, s32[]{:T(128)}, f32[8,2,8,128,128]{4,3,2,1,0:T(8,128)}, s32[]{:T(128)}, ...), condition=%wide.region_6.7_spmd, body=%wide.region_5.6_spmd.sunk | while | flops 262150 | bytes 3145871 | solution.py:23
  269.8 1.5 bitcast_add_fusion.9
  271.3 1.5 bitcast_add_fusion.9
  272.9 1.5 bitcast_add_fusion.9
  274.4 1.5 bitcast_add_fusion.9
  275.9 1.5 bitcast_add_fusion.9
  277.4 1.6 bitcast_add_fusion.9
  279.0 1.5 bitcast_add_fusion.9
  280.6 2.0 fusion.20
  282.6 0.4 fusion.21
  283.0 1.4 copy_bitcast_fusion
  284.4 48.5 %reduce-scatter.3.cloned.1.call-done = bf16[2,192,1024]{2,1,0:T(8,128)(2,1)} async-done(((bf16[2,192,4096]{2,1,0:T(8,128)(2,1)}), bf16[2,192,1024]{2,1,0:T(8,128)(2,1)}) %reduce-scatter.3.cloned.1.call-update) | async-done | bytes 786448 | tf_op jit(solution)/shard_map/reduce_scatter | solution.py:73
  (29 shorter events, 0.3 us)
Async XLA Ops:
  7.2 1.1 copy-start
  7.2 61.1 %all-gather.8.cloned.1.call-start = ((), (), s32[]{:S(2)}) async-start(), calls=%async_computation.5 | async-start | bytes 9437184 | tf_op jit(solution)/shard_map/all_gather | solution.py:16
  11.0 1.1 copy-start.5
  11.0 1.4 copy-start.7
  11.0 122.3 %all-gather.6.cloned.1.call-start = ((), (), s32[]{:S(2)}) async-start(), calls=%async_computation.3 | async-start | bytes 3932160 | tf_op jit(solution)/shard_map/all_gather | solution.py:76
  11.8 201.6 %reduce-scatter.5.cloned.1.call-start = ((), (), s32[]{:S(2)}) async-start(), calls=%async_computation.4 | async-start | bytes 9437184 | tf_op jit(solution)/shard_map/reduce_scatter | solution.py:85
  68.4 1.6 copy-start.10
  70.9 1.2 copy-start.1
  143.3 126.4 %all-gather.10.cloned.1.call-start = ((), (), s32[]{:S(2)}) async-start(), calls=%async_computation.6 | async-start | bytes 9437184 | tf_op jit(solution)/shard_map/all_gather | solution.py:16
  143.3 7.0 %copy-start.2 = (f32[2,8,192,128]{3,2,1,0:T(8,128)S(1)}, f32[2,8,192,128]{3,2,1,0:T(8,128)}, u32[]{:S(2)}) copy-start(f32[2,8,192,128]{3,2,1,0:T(8,128)} %copy-done.1) | copy-start | bytes 4718596
  151.4 1.9 copy-start.8
  152.5 0.9 copy-start.3
  155.2 177.6 %reduce-scatter.3.cloned.1.call-start = ((), (), s32[]{:S(2)}) async-start(), calls=%async_computation.2 | async-start | bytes 3932160 | tf_op jit(solution)/shard_map/reduce_scatter | solution.py:73
  165.0 1.1 copy-start.4
  166.1 1.2 copy-start.6
  168.4 1.7 copy-start.11
  170.1 1.9 copy-start.9
  280.6 2.0 copy-start.12
Sparse Core Ops, SparseCore 0:
  11.1 57.0 all-gather.7
  69.8 63.4 all-gather.5
  143.4 69.9 reduce-scatter.4
  215.3 54.3 all-gather.9
  272.5 60.2 reduce-scatter.2
where the time goes:
time: 340 us; the launch traced here: 339 us
  waiting for transfers between devices  256 us (75%)
  matrix products  41.7 us (12%)
  other arithmetic  16.9 us (5%)
  between operations  14 us (4%)
  local copies, waits for them, and re-layouts  10 us (3%)
    all_gather x2, waiting for transfers between devices, entering(): gathered = lax.all_gather(part, axis)  108 us
    all_gather x1, waiting for transfers between devices, shards(): grad_all = lax.all_gather(cotangent, 'head', axis=2, tiled=True)  59.9 us
    reduce_scatter x1, waiting for transfers between devices, shards(): lax.psum_scatter(partial_value.astype(jnp.bfloat16), 'head', scatter_dime...  48.5 us
    reduce_scatter x1, waiting for transfers between devices, shards(): lax.psum_scatter(weight_term.astype(jnp.bfloat16), 'ctx', scatter_dimensi...  39.4 us
    add x7, other arithmetic, add_states(): return earlier + later  10.6 us
    dot_general x1, matrix products, shards(): jnp.einsum('btr,btc->rc', normed_flat, grad_all, preferred_element_type=j...  9.93 us
    dot_general x1, matrix products, shards(): jnp.einsum('btr,rc->btc', normed_flat, out_weight, preferred_element_type...  9.54 us
    dot_general x1, matrix products, shards(): jnp.einsum('btc,rc->btr', grad_all, out_weight, preferred_element_type=jn...  6.95 us
  transfers between devices with their start and end apart: 5, of which 5 were waited for; matrix products, arithmetic and copies ran while one was open for 15% of the time, Pallas kernels for 0%

commit v1 on v0

--- a/solution.py
+++ b/solution.py
@@ -9,18 +9,86 @@
 epsilon = 1e-06
 
 
-def entering(part, axis, combine, identity, reverse):
+def swap(array, axis, bit):
+    count = lax.axis_size(axis)
+    return lax.ppermute(array, axis, [(i, i ^ bit) for i in range(count)])
+
+
+def exclusive_scan(part, axis, reverse):
     count = lax.axis_size(axis)
     place = lax.axis_index(axis)
-    ahead = count - 1 - place if reverse else place
-    gathered = lax.all_gather(part, axis)
-    state = jnp.zeros_like(part) + jnp.asarray(identity, part.dtype)
-
-    def one(hop, state):
-        source = count - 1 - hop if reverse else hop
-        return combine(state, lax.dynamic_index_in_dim(gathered, source, 0, False))
-
-    return lax.fori_loop(0, ahead, one, state)
+    core = place % 2
+    other = swap(part.astype(jnp.bfloat16), axis, 1).astype(jnp.float32)
+    total = lax.dynamic_index_in_dim(part + other, core, 0, False)
+    before = jnp.zeros_like(total)
+    bit = 2
+    while bit < count:
+        came = swap(total.astype(jnp.bfloat16), axis, bit).astype(jnp.float32)
+        mine = (place // bit) % 2
+        takes = (mine == 0) if reverse else (mine == 1)
+        before = before + jnp.where(takes, came, 0.0)
+        total = total + came
+        bit *= 2
+    before = before.astype(jnp.bfloat16)
+    came = swap(before, axis, 1)
+    first = jnp.where(core == 0, before, came)
+    second = jnp.where(core == 0, came, before)
+    pairs = jnp.stack([first, second]).astype(jnp.float32)
+    takes = (core == 0) if reverse else (core == 1)
+    return pairs + jnp.where(takes, other, 0.0)
+
+
+def right_of(array, axis, first, last):
+    return lax.ppermute(array, axis, [(i, i + 1) for i in range(first, last)])
+
+
+def left_of(array, axis, first, last):
+    return lax.ppermute(array, axis, [(i, i - 1) for i in range(first, last)])
+
+
+def gather_line(block, axis):
+    count = lax.axis_size(axis)
+    place = lax.axis_index(axis)
+    from_left, from_right = block, block
+    lefts, rights = {}, {}
+    for step in range(1, count):
+        from_left = right_of(from_left, axis, step - 1, count - 1)
+        from_right = left_of(from_right, axis, 1, count - step + 1)
+        lefts[step], rights[step] = from_left, from_right
+    blocks = [block]
+    for offset in range(1, count):
+        blocks.append(
+            jnp.where(place + offset < count, rights[offset], lefts[count - offset])
+        )
+    return blocks
+
+
+def scatter_line(terms, axis):
+    count = lax.axis_size(axis)
+    rightward = leftward = None
+    for step in range(1, count):
+        to_right, to_left = terms[count - step], terms[step]
+        if rightward is not None:
+            to_right = to_right + rightward.astype(jnp.float32)
+            to_left = to_left + leftward.astype(jnp.float32)
+        rightward = right_of(to_right.astype(jnp.bfloat16), axis, 0, step)
+        leftward = left_of(to_left.astype(jnp.bfloat16), axis, count - step, count)
+    return terms[0] + rightward.astype(jnp.float32) + leftward.astype(jnp.float32)
+
+
+def halve(blocks, axis, bits):
+    for bit in bits:
+        sent = {
+            k: swap(block.astype(jnp.bfloat16), axis, bit)
+            for k, block in blocks.items()
+            if k & bit
+        }
+        blocks = {
+            k: block + sent[k | bit].astype(jnp.float32)
+            for k, block in blocks.items()
+            if not k & bit
+        }
+    return blocks
 
 
 def split_heads(array):
@@ -35,10 +103,6 @@
 
 def rms_normalize(attended):
     return attended / jnp.sqrt(jnp.mean(attended * attended, axis=-1, keepdims=True) + epsilon)
-
-
-def add_states(earlier, later):
-    return earlier + later
 
 
 def shards(queries, key_rows, value_rows, out_weight, cotangent):
@@ -58,7 +122,7 @@
     local_state = jnp.einsum(
         "bhsd,bhse->bhde", key_heads, value_heads, preferred_element_type=jnp.float32
     )
-    state = entering(local_state, "ctx", add_states, jnp.zeros_like(local_state), False)
+    state = exclusive_scan(local_state, "ctx", False)
     state_bf = state.astype(jnp.bfloat16)
     attended = jnp.einsum(
         "bhts,bhsd->bhtd", scores, value_heads, preferred_element_type=jnp.float32
@@ -67,34 +131,49 @@
         "bhtd,bhde->bhte", query_heads, state_bf, preferred_element_type=jnp.float32
     )
     normed_flat = join_heads(rms_normalize(attended).astype(jnp.bfloat16))
-    partial_value = jnp.einsum(
-        "btr,rc->btc", normed_flat, out_weight, preferred_element_type=jnp.float32
-    )
-    layer_output = lax.psum_scatter(
-        partial_value.astype(jnp.bfloat16), "head", scatter_dimension=2, tiled=True
-    )
-    grad_all = lax.all_gather(cotangent, "head", axis=2, tiled=True)
-    normed_grad = jnp.einsum(
-        "btc,rc->btr", grad_all, out_weight, preferred_element_type=jnp.float32
-    )
-    weight_term = jnp.einsum(
-        "btr,btc->rc", normed_flat, grad_all, preferred_element_type=jnp.float32
-    )
-    token_factor = (2 * length * lax.axis_size("ctx")) ** (-0.5)
-    weight_grad = (
-        lax.psum_scatter(
-            weight_term.astype(jnp.bfloat16), "ctx", scatter_dimension=1, tiled=True
-        ).astype(jnp.float32)
-        * token_factor
-    )
+    groups = lax.axis_size("head")
+    group = lax.axis_index("head")
+    width = cotangent.shape[2]
+    columns = [
+        lax.dynamic_slice_in_dim(out_weight, (group + o) % groups * width, width, 1)
+        for o in range(groups)
+    ]
+    grads = gather_line(cotangent, "head")
+    layer_output = scatter_line(
+        [
+            jnp.einsum("btr,rc->btc", normed_flat, part, preferred_element_type=jnp.float32)
+            for part in columns
+        ],
+        "head",
+    ).astype(jnp.bfloat16)
+    normed_grad = sum(
+        jnp.einsum("btc,rc->btr", grad, part, preferred_element_type=jnp.float32)
+        for grad, part in zip(grads, columns)
+    )
+    places = lax.axis_size("ctx")
+    place = lax.axis_index("ctx")
+    span = groups * width // places
+    grad_all = jnp.concatenate(grads, axis=2)
+    blocks = {}
+    for k in range(places):
+        start = ((place ^ k) * span - group * width) % (groups * width)
+        wanted = lax.dynamic_slice_in_dim(grad_all, start, span, 2)
+        blocks[k] = jnp.einsum(
+            "btr,btc->rc", normed_flat, wanted, preferred_element_type=jnp.float32
+        )
+    blocks = halve(blocks, "ctx", [1])
+    bits = [1 << i for i in range(1, places.bit_length() - 1)]
+    rows = normed_flat.shape[2] // 2
+    upper = halve({k: block[:rows] for k, block in blocks.items()}, "ctx", bits)
+    lower_rows = halve({k: block[rows:] for k, block in blocks.items()}, "ctx", bits[::-1])
+    token_factor = (2 * length * places) ** (-0.5)
+    weight_grad = jnp.concatenate([upper[0], lower_rows[0]], axis=0) * token_factor
     pullback = jax.vjp(rms_normalize, attended)[1]
     attended_grad = pullback(split_heads(normed_grad))[0].astype(jnp.bfloat16)
     local_grad_state = jnp.einsum(
         "bhtd,bhte->bhde", query_heads, attended_grad, preferred_element_type=jnp.float32
     )
-    grad_state = entering(
-        local_grad_state, "ctx", add_states, jnp.zeros_like(local_grad_state), True
-    )
+    grad_state = exclusive_scan(local_grad_state, "ctx", True)
     grad_state_bf = grad_state.astype(jnp.bfloat16)
     raw_grad = (
         jnp.einsum(

time: 340 us -> 163 us (0.48)
  waiting for transfers between devices: 256 us -> 74.9 us
  starting transfers between devices: 0.38 us -> 44.3 us
  matrix products: 41.7 us -> 25.5 us
  between operations: 14 us -> 1.31 us
  other arithmetic: 16.9 us -> 10.9 us
  local copies, waits for them, and re-layouts: 10 us -> 5.17 us
    all_gather x3 -> x0, waiting for transfers between devices: 168 us -> none  [the longest x2 108 us: entering(): gathered = lax.all_gather(part, axis)]
    reduce_scatter x2 -> x0, waiting for transfers between devices: 87.8 us -> none  [the longest x1 48.5 us: shards(): lax.psum_scatter(partial_value.astype(jnp.bfloat16), 'head', scatter_dime...]
    ppermute x0 -> x30, waiting for transfers between devices: none -> 74.9 us  [the longest x18 46.1 us: swap(): return lax.ppermute(array, axis, [(i, i ^ bit) for i in range(count)])]
    ppermute x0 -> x30, starting transfers between devices: none -> 44.3 us  [the longest x6 21.8 us: right_of(): return lax.ppermute(array, axis, [(i, i + 1) for i in range(first, last)])]
    add x7 -> x1, other arithmetic: 10.6 us -> 0.43 us  [halve(): block + sent[k | bit].astype(jnp.float32)]
    dot_general x3 -> x16, matrix products: 26.4 us -> 16.5 us  [the longest x8 6.61 us: shards(): jnp.einsum('btr,btc->rc', normed_flat, wanted, preferred_element_type=jnp...]
    convert_element_type x0 -> x14, other arithmetic: none -> 4.44 us  [the longest x4 1.52 us: exclusive_scan(): came = swap(total.astype(jnp.bfloat16), axis, bit).astype(jnp.float32)]
    unnamed x26 -> x16, local copies, waits for them, and re-layouts: 5.97 us -> 2.48 us
  transfers between devices with their start and end apart: 5 -> 30, of which waited for: 5 -> 14; matrix products, arithmetic and copies ran while one was open for 15% -> 22% of each run, Pallas kernels for 0% -> 0%
where the time goes in v1:
time: 163 us; the launch traced here: 162 us
  waiting for transfers between devices  74.9 us (46%)
  starting transfers between devices  44.3 us (27%)
  matrix products  25.5 us (16%)
  other arithmetic  10.9 us (7%)
  local copies, waits for them, and re-layouts  5.17 us (3%)
    ppermute x18, waiting for transfers between devices, swap(): return lax.ppermute(array, axis, [(i, i ^ bit) for i in range(count)])  46.1 us
    ppermute x6, waiting for transfers between devices, left_of(): return lax.ppermute(array, axis, [(i, i - 1) for i in range(first, last)])  23.6 us
    ppermute x6, starting transfers between devices, right_of(): return lax.ppermute(array, axis, [(i, i + 1) for i in range(first, last)])  21.8 us
    ppermute x18, starting transfers between devices, swap(): return lax.ppermute(array, axis, [(i, i ^ bit) for i in range(count)])  16 us
    dot_general x8, matrix products, shards(): jnp.einsum('btr,btc->rc', normed_flat, wanted, preferred_element_type=jnp...  6.61 us
    ppermute x6, starting transfers between devices, left_of(): return lax.ppermute(array, axis, [(i, i - 1) for i in range(first, last)])  6.53 us
    dot_general x4, matrix products, shards(): jnp.einsum('btc,rc->btr', grad, part, preferred_element_type=jnp.float32)  5.94 us
    ppermute x6, waiting for transfers between devices, right_of(): return lax.ppermute(array, axis, [(i, i + 1) for i in range(first, last)])  5.12 us
  transfers between devices with their start and end apart: 30, of which 14 were waited for; matrix products, arithmetic and copies ran while one was open for 22% of the time, Pallas kernels for 0%

profile of v1, /device:TPU:0, one launch (start us, length us, event | category | flops | bytes accessed | tf_op | source)
XLA Modules:
  0.0 162.1 jit_solution(15476370149213732391)
XLA Ops:
  0.6 1.1 copy-done
  1.8 2.6 %fusion.124 = (bf16[2,8,128,128]{3,2,1,0:T(8,128)(2,1)S(1)}, f32[2,8,128,128]{3,2,1,0:T(8,128)}) fusion(bf16[2,192,1024]{2,1,0:T(8,128)(2,1)S(1)} %copy-done, bf16[2,192,1024]{2,1,0:T(8,128)(2,1)} %param.6), kind=kOutput, calls=%fused_computation.181 | convolution fusion | flops 100925440 | bytes 3145728 | tf_op jit(solution)/shard_map/bhsd,bhse->bhde/dot_general | solution.py:122
  4.8 1.5 collective-permute-done
  6.6 0.9 copy-done.4
  7.5 2.9 %collective-permute-start.1 = (bf16[8,128,128]{2,1,0:T(8,128)(2,1)S(1)}, bf16[8,128,128]{2,1,0:T(8,128)(2,1)S(1)}, u32[]{:S(2)}, u32[]{:S(2)}) collective-permute-start(bf16[8,128,128]{2,1,0:T(8,128)(2,1)S(1)} %fusion.91), channel_id=1, source_target_pairs={{0,8},{4,12},{8,0},{12,4},{16,24},{20,28},{24,16},{28,20},{1,9},{5... | collective-permute-start | bytes 786440 | tf_op jit(solution)/shard_map/ppermute | solution.py:14
  10.3 1.3 collective-permute-start.10
  11.6 5.5 %collective-permute-start.11 = (bf16[2,192,1024]{2,1,0:T(8,128)(2,1)}, bf16[2,192,1024]{2,1,0:T(8,128)(2,1)}, u32[]{:S(2)}, u32[]{:S(2)}) collective-permute-start(bf16[2,192,1024]{2,1,0:T(8,128)(2,1)} %param.9), channel_id=1, source_target_pairs={{0,1},{1,2},{2,3},{4,5},{5,6},{6,7},{8,9},{9,10},{10,11},{12,13},{... | collective-permute-start | bytes 2359304 | tf_op jit(solution)/shard_map/ppermute | solution.py:42
  17.1 1.3 fusion.65
  18.4 1.7 %collective-permute-start.2 = (bf16[8,128,128]{2,1,0:T(8,128)(2,1)S(1)}, bf16[8,128,128]{2,1,0:T(8,128)(2,1)S(1)}, u32[]{:S(2)}, u32[]{:S(2)}) collective-permute-start(bf16[8,128,128]{2,1,0:T(8,128)(2,1)S(1)} %fusion.65), channel_id=1, source_target_pairs={{0,16},{4,20},{8,24},{12,28},{16,0},{20,4},{24,8},{28,12},{1,17},{... | collective-permute-start | bytes 786440 | tf_op jit(solution)/shard_map/ppermute | solution.py:14
  20.7 5.6 %collective-permute-done.2 = bf16[8,128,128]{2,1,0:T(8,128)(2,1)S(1)} collective-permute-done((bf16[8,128,128]{2,1,0:T(8,128)(2,1)S(1)}, bf16[8,128,128]{2,1,0:T(8,128)(2,1)S(1)}, u32[]{:S(2)}, u32[]{:S(2)}) %collective-permute-start.2) | collective-permute-done | bytes 262176 | tf_op jit(solution)/shard_map/ppermute | solution.py:14
  26.4 2.8 %fusion.13 = f32[1024,2,192]{0,2,1:T(8,128)S(1)} fusion(bf16[2,192,1024]{2,1,0:T(8,128)(2,1)S(1)} %copy-done.5, bf16[1024,4096]{1,0:T(8,128)(2,1)} %param.8, s32[]{:T(128)S(6)} %select_n.223), kind=kOutput, calls=%fused_computation.26 | convolution fusion | flops 805306368 | bytes 4456452 | tf_op jit(solution)/shard_map/btc,rc->btr/dot_general | solution.py:150
  29.3 2.6 %collective-permute-done.10 = bf16[2,192,1024]{2,1,0:T(8,128)(2,1)} collective-permute-done((bf16[2,192,1024]{2,1,0:T(8,128)(2,1)}, bf16[2,192,1024]{2,1,0:T(8,128)(2,1)}, u32[]{:S(2)}, u32[]{:S(2)}) %collective-permute-start.10) | collective-permute-done | bytes 786464 | tf_op jit(solution)/shard_map/ppermute | solution.py:46
  31.8 1.3 collective-permute-start.14
  36.1 1.0 fusion.125
  37.1 7.5 %collective-permute-start.4 = (bf16[2,192,1024]{2,1,0:T(8,128)(2,1)S(1)}, bf16[2,192,1024]{2,1,0:T(8,128)(2,1)S(1)}, u32[]{:S(2)}, u32[]{:S(2)}) collective-permute-start(bf16[2,192,1024]{2,1,0:T(8,128)(2,1)S(1)} %get-tuple-element.22), channel_id=1, source_target_pairs={{0,1},{4,5},{8,9},{12,13},{16,17},{20,21},{24,25},{28,29}} | collective-permute-start | bytes 2359304 | tf_op jit(solution)/shard_map/ppermute | solution.py:42
  44.6 1.0 fusion.15
  45.5 1.0 fusion.11
  47.3 5.1 %collective-permute-done.14 = bf16[2,192,1024]{2,1,0:T(8,128)(2,1)S(1)} collective-permute-done((bf16[2,192,1024]{2,1,0:T(8,128)(2,1)}, bf16[2,192,1024]{2,1,0:T(8,128)(2,1)S(1)}, u32[]{:S(2)}, u32[]{:S(2)}) %collective-permute-start.14) | collective-permute-done | bytes 786464 | tf_op jit(solution)/shard_map/ppermute | solution.py:46
  52.4 1.3 collective-permute-start.15
  53.7 1.0 fusion.5
  54.8 5.1 %collective-permute-done.4 = bf16[2,192,1024]{2,1,0:T(8,128)(2,1)S(1)} collective-permute-done((bf16[2,192,1024]{2,1,0:T(8,128)(2,1)S(1)}, bf16[2,192,1024]{2,1,0:T(8,128)(2,1)S(1)}, u32[]{:S(2)}, u32[]{:S(2)}) %collective-permute-start.4) | collective-permute-done | bytes 786464 | tf_op jit(solution)/shard_map/ppermute | solution.py:42
  59.9 1.0 add_convert_fusion.5
  60.9 4.6 %collective-permute-start.5 = (bf16[2,192,1024]{2,1,0:T(8,128)(2,1)S(1)}, bf16[2,192,1024]{2,1,0:T(8,128)(2,1)S(1)}, u32[]{:S(2)}, u32[]{:S(2)}) collective-permute-start(bf16[2,192,1024]{2,1,0:T(8,128)(2,1)S(1)} %get-tuple-element.24), channel_id=1, source_target_pairs={{0,1},{1,2},{4,5},{5,6},{8,9},{9,10},{12,13},{13,14},{16,17},{17,1... | collective-permute-start | bytes 2359304 | tf_op jit(solution)/shard_map/ppermute | solution.py:42
  65.5 1.3 broadcast_select_fusion.2
  66.8 1.0 fusion.9
  67.8 5.0 %collective-permute-done.15 = bf16[2,192,1024]{2,1,0:T(8,128)(2,1)S(1)} collective-permute-done((bf16[2,192,1024]{2,1,0:T(8,128)(2,1)S(1)}, bf16[2,192,1024]{2,1,0:T(8,128)(2,1)S(1)}, u32[]{:S(2)}, u32[]{:S(2)}) %collective-permute-start.15) | collective-permute-done | bytes 786464 | tf_op jit(solution)/shard_map/ppermute | solution.py:46
  72.8 1.1 fusion.34
  74.0 1.1 fusion.29
  75.1 1.0 fusion.25
  79.3 1.1 copy.151
  87.0 7.8 %collective-permute-done.17 = bf16[8,128,128]{2,1,0:T(8,128)(2,1)S(1)} collective-permute-done((bf16[8,128,128]{2,1,0:T(8,128)(2,1)S(1)}, bf16[8,128,128]{2,1,0:T(8,128)(2,1)S(1)}, u32[]{:S(2)}, u32[]{:S(2)}) %collective-permute-start.17) | collective-permute-done | bytes 262176 | tf_op jit(solution)/shard_map/ppermute | solution.py:14
  95.6 1.6 collective-permute-start.18
  98.1 5.5 %collective-permute-done.18 = bf16[8,128,128]{2,1,0:T(8,128)(2,1)S(1)} collective-permute-done((bf16[8,128,128]{2,1,0:T(8,128)(2,1)S(1)}, bf16[8,128,128]{2,1,0:T(8,128)(2,1)S(1)}, u32[]{:S(2)}, u32[]{:S(2)}) %collective-permute-start.18) | collective-permute-done | bytes 262176 | tf_op jit(solution)/shard_map/ppermute | solution.py:14
  103.6 2.8 %collective-permute-start.6 = (bf16[2,192,1024]{2,1,0:T(8,128)(2,1)S(1)}, bf16[2,192,1024]{2,1,0:T(8,128)(2,1)S(1)}, u32[]{:S(2)}, u32[]{:S(2)}) collective-permute-start(bf16[2,192,1024]{2,1,0:T(8,128)(2,1)S(1)} %get-tuple-element.7), channel_id=1, source_target_pairs={{0,1},{1,2},{2,3},{4,5},{5,6},{6,7},{8,9},{9,10},{10,11},{12,13},{... | collective-permute-start | bytes 2359304 | tf_op jit(solution)/shard_map/ppermute | solution.py:42
  109.1 1.6 collective-permute-start.22
  111.5 1.6 collective-permute-start.28
  115.1 7.3 %collective-permute-done.25 = bf16[512,512]{1,0:T(8,128)(2,1)S(1)} collective-permute-done((bf16[512,512]{1,0:T(8,128)(2,1)S(1)}, bf16[512,512]{1,0:T(8,128)(2,1)S(1)}, u32[]{:S(2)}, u32[]{:S(2)}) %collective-permute-start.25) | collective-permute-done | bytes 524320 | tf_op jit(solution)/shard_map/ppermute | solution.py:14
  122.4 1.5 collective-permute-start.27
  124.1 2.3 %collective-permute-done.28 = bf16[512,512]{1,0:T(8,128)(2,1)S(1)} collective-permute-done((bf16[512,512]{1,0:T(8,128)(2,1)S(1)}, bf16[512,512]{1,0:T(8,128)(2,1)S(1)}, u32[]{:S(2)}, u32[]{:S(2)}) %collective-permute-start.28) | collective-permute-done | bytes 524320 | tf_op jit(solution)/shard_map/ppermute | solution.py:14
  126.4 1.5 collective-permute-start.26
  129.0 4.6 %collective-permute-done.22 = bf16[512,512]{1,0:T(8,128)(2,1)S(1)} collective-permute-done((bf16[512,512]{1,0:T(8,128)(2,1)S(1)}, bf16[512,512]{1,0:T(8,128)(2,1)S(1)}, u32[]{:S(2)}, u32[]{:S(2)}) %collective-permute-start.22) | collective-permute-done | bytes 524320 | tf_op jit(solution)/shard_map/ppermute | solution.py:14
  133.6 1.3 collective-permute-start.9
  134.9 1.4 copy_bitcast_fusion
  136.3 1.3 collective-permute-done.27
  137.6 10.2 %collective-permute-done.26 = bf16[512,512]{1,0:T(8,128)(2,1)S(1)} collective-permute-done((bf16[512,512]{1,0:T(8,128)(2,1)S(1)}, bf16[512,512]{1,0:T(8,128)(2,1)S(1)}, u32[]{:S(2)}, u32[]{:S(2)}) %collective-permute-start.26) | collective-permute-done | bytes 524320 | tf_op jit(solution)/shard_map/ppermute | solution.py:14
  148.2 1.6 maximum_multiply_fusion
  149.8 11.0 %collective-permute-done.9 = bf16[2,192,1024]{2,1,0:T(8,128)(2,1)S(1)} collective-permute-done((bf16[2,192,1024]{2,1,0:T(8,128)(2,1)S(1)}, bf16[2,192,1024]{2,1,0:T(8,128)(2,1)S(1)}, u32[]{:S(2)}, u32[]{:S(2)}) %collective-permute-start.9) | collective-permute-done | bytes 786464 | tf_op jit(solution)/shard_map/ppermute | solution.py:46
  160.8 1.3 add_convert_fusion.1
  (90 shorter events, 23.7 us)
Async XLA Ops:
  0.6 1.1 copy-start
  4.4 2.0 %collective-permute-start = (bf16[2,8,128,128]{3,2,1,0:T(8,128)(2,1)S(1)}, bf16[2,8,128,128]{3,2,1,0:T(8,128)(2,1)S(1)}, u32[]{:S(2)}, u32[]{:S(2)}) collective-permute-start(bf16[2,8,128,128]{3,2,1,0:T(8,128)(2,1)S(1)} %get-tuple-element.18), channel_id=1, source_target_pairs={{0,4},{4,0},{8,12},{12,8},{16,20},{20,16},{24,28},{28,24},{1,5},{5... | collective-permute-start | bytes 1572872 | tf_op jit(solution)/shard_map/ppermute | solution.py:14
  4.8 1.7 %copy-start.3 = (f32[2,8,128,128]{3,2,1,0:T(8,128)S(1)}, f32[2,8,128,128]{3,2,1,0:T(8,128)}, u32[]{:S(2)}) copy-start(f32[2,8,128,128]{3,2,1,0:T(8,128)} %get-tuple-element.19) | copy-start | bytes 3145732
  6.5 1.0 copy-start.4
  6.5 13.6 %copy-start.1 = (bf16[2,192,1024]{2,1,0:T(8,128)(2,1)S(1)}, bf16[2,192,1024]{2,1,0:T(8,128)(2,1)}, u32[]{:S(2)}) copy-start(bf16[2,192,1024]{2,1,0:T(8,128)(2,1)} %param.6) | copy-start | bytes 2359300
  6.5 13.6 %copy-start.2 = (bf16[2,192,1024]{2,1,0:T(8,128)(2,1)S(1)}, bf16[2,192,1024]{2,1,0:T(8,128)(2,1)}, u32[]{:S(2)}) copy-start(bf16[2,192,1024]{2,1,0:T(8,128)(2,1)} %param.5) | copy-start | bytes 2359300
  7.5 9.6 %collective-permute-start.1 = (bf16[8,128,128]{2,1,0:T(8,128)(2,1)S(1)}, bf16[8,128,128]{2,1,0:T(8,128)(2,1)S(1)}, u32[]{:S(2)}, u32[]{:S(2)}) collective-permute-start(bf16[8,128,128]{2,1,0:T(8,128)(2,1)S(1)} %fusion.91), channel_id=1, source_target_pairs={{0,8},{4,12},{8,0},{12,4},{16,24},{20,28},{24,16},{28,20},{1,9},{5... | collective-permute-start | bytes 786440 | tf_op jit(solution)/shard_map/ppermute | solution.py:14
  10.3 21.5 %collective-permute-start.10 = (bf16[2,192,1024]{2,1,0:T(8,128)(2,1)}, bf16[2,192,1024]{2,1,0:T(8,128)(2,1)}, u32[]{:S(2)}, u32[]{:S(2)}) collective-permute-start(bf16[2,192,1024]{2,1,0:T(8,128)(2,1)} %param.9), channel_id=1, source_target_pairs={{1,0},{2,1},{3,2},{5,4},{6,5},{7,6},{9,8},{10,9},{11,10},{13,12},{... | collective-permute-start | bytes 2359304 | tf_op jit(solution)/shard_map/ppermute | solution.py:46
  11.6 21.5 %collective-permute-start.11 = (bf16[2,192,1024]{2,1,0:T(8,128)(2,1)}, bf16[2,192,1024]{2,1,0:T(8,128)(2,1)}, u32[]{:S(2)}, u32[]{:S(2)}) collective-permute-start(bf16[2,192,1024]{2,1,0:T(8,128)(2,1)} %param.9), channel_id=1, source_target_pairs={{0,1},{1,2},{2,3},{4,5},{5,6},{6,7},{8,9},{9,10},{10,11},{12,13},{... | collective-permute-start | bytes 2359304 | tf_op jit(solution)/shard_map/ppermute | solution.py:42
  18.4 8.0 %copy-start.5 = (bf16[2,192,1024]{2,1,0:T(8,128)(2,1)S(1)}, bf16[2,192,1024]{2,1,0:T(8,128)(2,1)}, u32[]{:S(2)}) copy-start(bf16[2,192,1024]{2,1,0:T(8,128)(2,1)} %param.9) | copy-start | bytes 2359300
  18.4 7.8 %collective-permute-start.2 = (bf16[8,128,128]{2,1,0:T(8,128)(2,1)S(1)}, bf16[8,128,128]{2,1,0:T(8,128)(2,1)S(1)}, u32[]{:S(2)}, u32[]{:S(2)}) collective-permute-start(bf16[8,128,128]{2,1,0:T(8,128)(2,1)S(1)} %fusion.65), channel_id=1, source_target_pairs={{0,16},{4,20},{8,24},{12,28},{16,0},{20,4},{24,8},{28,12},{1,17},{... | collective-permute-start | bytes 786440 | tf_op jit(solution)/shard_map/ppermute | solution.py:14
  26.3 7.5 %collective-permute-start.3 = (bf16[8,128,128]{2,1,0:T(8,128)(2,1)S(1)}, bf16[8,128,128]{2,1,0:T(8,128)(2,1)S(1)}, u32[]{:S(2)}, u32[]{:S(2)}) collective-permute-start(bf16[8,128,128]{2,1,0:T(8,128)(2,1)S(1)} %fusion.64), channel_id=1, source_target_pairs={{0,4},{4,0},{8,12},{12,8},{16,20},{20,16},{24,28},{28,24},{1,5},{5... | collective-permute-start | bytes 786440 | tf_op jit(solution)/shard_map/ppermute | solution.py:14
  26.4 9.3 %slice-start = ((s8[8388608]{0:T(1024)(128)(4,1)}), s8[4194304]{0:T(1024)(128)(4,1)S(1)}, s32[]{:S(2)}) async-start(s8[8388608]{0:T(1024)(128)(4,1)} %bitcast.290), calls=%async_computation | async-start | bytes 8388608
  31.8 20.5 %collective-permute-start.14 = (bf16[2,192,1024]{2,1,0:T(8,128)(2,1)}, bf16[2,192,1024]{2,1,0:T(8,128)(2,1)S(1)}, u32[]{:S(2)}, u32[]{:S(2)}) collective-permute-start(bf16[2,192,1024]{2,1,0:T(8,128)(2,1)} %collective-permute-done.10), channel_id=1, source_target_pairs={{1,0},{2,1},{5,4},{6,5},{9,8},{10,9},{13,12},{14,13},{17,16},{18,1... | collective-permute-start | bytes 2359304 | tf_op jit(solution)/shard_map/ppermute | solution.py:46
  33.1 13.4 %collective-permute-start.12 = (bf16[2,192,1024]{2,1,0:T(8,128)(2,1)}, bf16[2,192,1024]{2,1,0:T(8,128)(2,1)S(1)}, u32[]{:S(2)}, u32[]{:S(2)}) collective-permute-start(bf16[2,192,1024]{2,1,0:T(8,128)(2,1)} %collective-permute-done.11), channel_id=1, source_target_pairs={{1,2},{2,3},{5,6},{6,7},{9,10},{10,11},{13,14},{14,15},{17,18},{18... | collective-permute-start | bytes 2359304 | tf_op jit(solution)/shard_map/ppermute | solution.py:42
  33.9 2.2 %slice-start.1 = ((s8[8388608]{0:T(1024)(128)(4,1)}), s8[4194304]{0:T(1024)(128)(4,1)S(1)}, s32[]{:S(2)}) async-start(s8[8388608]{0:T(1024)(128)(4,1)} %bitcast.290), calls=%async_computation.1 | async-start | bytes 8388608
  37.1 22.8 %collective-permute-start.4 = (bf16[2,192,1024]{2,1,0:T(8,128)(2,1)S(1)}, bf16[2,192,1024]{2,1,0:T(8,128)(2,1)S(1)}, u32[]{:S(2)}, u32[]{:S(2)}) collective-permute-start(bf16[2,192,1024]{2,1,0:T(8,128)(2,1)S(1)} %get-tuple-element.22), channel_id=1, source_target_pairs={{0,1},{4,5},{8,9},{12,13},{16,17},{20,21},{24,25},{28,29}} | collective-permute-start | bytes 2359304 | tf_op jit(solution)/shard_map/ppermute | solution.py:42
  46.5 18.9 %collective-permute-start.13 = (bf16[2,192,1024]{2,1,0:T(8,128)(2,1)S(1)}, bf16[2,192,1024]{2,1,0:T(8,128)(2,1)S(1)}, u32[]{:S(2)}, u32[]{:S(2)}) collective-permute-start(bf16[2,192,1024]{2,1,0:T(8,128)(2,1)S(1)} %collective-permute-done.12), channel_id=1, source_target_pairs={{2,3},{6,7},{10,11},{14,15},{18,19},{22,23},{26,27},{30,31}} | collective-permute-start | bytes 2359304 | tf_op jit(solution)/shard_map/ppermute | solution.py:42
  52.4 20.4 %collective-permute-start.15 = (bf16[2,192,1024]{2,1,0:T(8,128)(2,1)S(1)}, bf16[2,192,1024]{2,1,0:T(8,128)(2,1)S(1)}, u32[]{:S(2)}, u32[]{:S(2)}) collective-permute-start(bf16[2,192,1024]{2,1,0:T(8,128)(2,1)S(1)} %collective-permute-done.14), channel_id=1, source_target_pairs={{1,0},{5,4},{9,8},{13,12},{17,16},{21,20},{25,24},{29,28}} | collective-permute-start | bytes 2359304 | tf_op jit(solution)/shard_map/ppermute | solution.py:46
  60.9 25.1 %collective-permute-start.5 = (bf16[2,192,1024]{2,1,0:T(8,128)(2,1)S(1)}, bf16[2,192,1024]{2,1,0:T(8,128)(2,1)S(1)}, u32[]{:S(2)}, u32[]{:S(2)}) collective-permute-start(bf16[2,192,1024]{2,1,0:T(8,128)(2,1)S(1)} %get-tuple-element.24), channel_id=1, source_target_pairs={{0,1},{1,2},{4,5},{5,6},{8,9},{9,10},{12,13},{13,14},{16,17},{17,1... | collective-permute-start | bytes 2359304 | tf_op jit(solution)/shard_map/ppermute | solution.py:42
  80.4 5.3 %collective-permute-start.16 = (bf16[2,8,128,128]{3,2,1,0:T(8,128)(2,1)S(1)}, bf16[2,8,128,128]{3,2,1,0:T(8,128)(2,1)S(1)}, u32[]{:S(2)}, u32[]{:S(2)}) collective-permute-start(bf16[2,8,128,128]{3,2,1,0:T(8,128)(2,1)S(1)} %get-tuple-element.26), channel_id=1, source_target_pairs={{0,4},{4,0},{8,12},{12,8},{16,20},{20,16},{24,28},{28,24},{1,5},{5... | collective-permute-start | bytes 1572872 | tf_op jit(solution)/shard_map/ppermute | solution.py:14
  81.3 27.8 %collective-permute-start.20 = (bf16[1024,512]{1,0:T(8,128)(2,1)S(1)}, bf16[1024,512]{1,0:T(8,128)(2,1)S(1)}, u32[]{:S(2)}, u32[]{:S(2)}) collective-permute-start(bf16[1024,512]{1,0:T(8,128)(2,1)S(1)} %bitcast_convert_fusion.3), channel_id=1, source_target_pairs={{0,4},{4,0},{8,12},{12,8},{16,20},{20,16},{24,28},{28,24},{1,5},{5... | collective-permute-start | bytes 3145736 | tf_op jit(solution)/shard_map/ppermute | solution.py:14
  82.7 24.9 %collective-permute-start.23 = (bf16[1024,512]{1,0:T(8,128)(2,1)S(1)}, bf16[1024,512]{1,0:T(8,128)(2,1)S(1)}, u32[]{:S(2)}, u32[]{:S(2)}) collective-permute-start(bf16[1024,512]{1,0:T(8,128)(2,1)S(1)} %bitcast_convert_fusion.1), channel_id=1, source_target_pairs={{0,4},{4,0},{8,12},{12,8},{16,20},{20,16},{24,28},{28,24},{1,5},{5... | collective-permute-start | bytes 3145736 | tf_op jit(solution)/shard_map/ppermute | solution.py:14
  83.6 12.0 %collective-permute-start.21 = (bf16[1024,512]{1,0:T(8,128)(2,1)S(1)}, bf16[1024,512]{1,0:T(8,128)(2,1)S(1)}, u32[]{:S(2)}, u32[]{:S(2)}) collective-permute-start(bf16[1024,512]{1,0:T(8,128)(2,1)S(1)} %bitcast_convert_fusion.2), channel_id=1, source_target_pairs={{0,4},{4,0},{8,12},{12,8},{16,20},{20,16},{24,28},{28,24},{1,5},{5... | collective-permute-start | bytes 3145736 | tf_op jit(solution)/shard_map/ppermute | solution.py:14
  85.7 20.8 %collective-permute-start.24 = (bf16[1024,512]{1,0:T(8,128)(2,1)S(1)}, bf16[1024,512]{1,0:T(8,128)(2,1)S(1)}, u32[]{:S(2)}, u32[]{:S(2)}) collective-permute-start(bf16[1024,512]{1,0:T(8,128)(2,1)S(1)} %bitcast_convert_fusion), channel_id=1, source_target_pairs={{0,4},{4,0},{8,12},{12,8},{16,20},{20,16},{24,28},{28,24},{1,5},{5... | collective-permute-start | bytes 3145736 | tf_op jit(solution)/shard_map/ppermute | solution.py:14
  86.0 8.8 %collective-permute-start.17 = (bf16[8,128,128]{2,1,0:T(8,128)(2,1)S(1)}, bf16[8,128,128]{2,1,0:T(8,128)(2,1)S(1)}, u32[]{:S(2)}, u32[]{:S(2)}) collective-permute-start(bf16[8,128,128]{2,1,0:T(8,128)(2,1)S(1)} %fusion.92), channel_id=1, source_target_pairs={{0,8},{4,12},{8,0},{12,4},{16,24},{20,28},{24,16},{28,20},{1,9},{5... | collective-permute-start | bytes 786440 | tf_op jit(solution)/shard_map/ppermute | solution.py:14
  94.8 16.7 %collective-permute-start.7 = (bf16[2,192,1024]{2,1,0:T(8,128)(2,1)S(1)}, bf16[2,192,1024]{2,1,0:T(8,128)(2,1)S(1)}, u32[]{:S(2)}, u32[]{:S(2)}) collective-permute-start(bf16[2,192,1024]{2,1,0:T(8,128)(2,1)S(1)} %get-tuple-element.8), channel_id=1, source_target_pairs={{3,2},{7,6},{11,10},{15,14},{19,18},{23,22},{27,26},{31,30}} | collective-permute-start | bytes 2359304 | tf_op jit(solution)/shard_map/ppermute | solution.py:46
  95.6 8.0 %collective-permute-start.18 = (bf16[8,128,128]{2,1,0:T(8,128)(2,1)S(1)}, bf16[8,128,128]{2,1,0:T(8,128)(2,1)S(1)}, u32[]{:S(2)}, u32[]{:S(2)}) collective-permute-start(bf16[8,128,128]{2,1,0:T(8,128)(2,1)S(1)} %fusion.68), channel_id=1, source_target_pairs={{0,16},{4,20},{8,24},{12,28},{16,0},{20,4},{24,8},{28,12},{1,17},{... | collective-permute-start | bytes 786440 | tf_op jit(solution)/shard_map/ppermute | solution.py:14
  103.6 46.2 %collective-permute-start.6 = (bf16[2,192,1024]{2,1,0:T(8,128)(2,1)S(1)}, bf16[2,192,1024]{2,1,0:T(8,128)(2,1)S(1)}, u32[]{:S(2)}, u32[]{:S(2)}) collective-permute-start(bf16[2,192,1024]{2,1,0:T(8,128)(2,1)S(1)} %get-tuple-element.7), channel_id=1, source_target_pairs={{0,1},{1,2},{2,3},{4,5},{5,6},{6,7},{8,9},{9,10},{10,11},{12,13},{... | collective-permute-start | bytes 2359304 | tf_op jit(solution)/shard_map/ppermute | solution.py:42
  106.6 6.8 %collective-permute-start.19 = (bf16[8,128,128]{2,1,0:T(8,128)(2,1)S(1)}, bf16[8,128,128]{2,1,0:T(8,128)(2,1)S(1)}, u32[]{:S(2)}, u32[]{:S(2)}) collective-permute-start(bf16[8,128,128]{2,1,0:T(8,128)(2,1)S(1)} %fusion.67), channel_id=1, source_target_pairs={{0,4},{4,0},{8,12},{12,8},{16,20},{20,16},{24,28},{28,24},{1,5},{5... | collective-permute-start | bytes 786440 | tf_op jit(solution)/shard_map/ppermute | solution.py:14
  107.6 14.8 %collective-permute-start.25 = (bf16[512,512]{1,0:T(8,128)(2,1)S(1)}, bf16[512,512]{1,0:T(8,128)(2,1)S(1)}, u32[]{:S(2)}, u32[]{:S(2)}) collective-permute-start(bf16[512,512]{1,0:T(8,128)(2,1)S(1)} %get-tuple-element.9), channel_id=1, source_target_pairs={{0,8},{4,12},{8,0},{12,4},{16,24},{20,28},{24,16},{28,20},{1,9},{5... | collective-permute-start | bytes 1572872 | tf_op jit(solution)/shard_map/ppermute | solution.py:14
  109.1 24.5 %collective-permute-start.22 = (bf16[512,512]{1,0:T(8,128)(2,1)S(1)}, bf16[512,512]{1,0:T(8,128)(2,1)S(1)}, u32[]{:S(2)}, u32[]{:S(2)}) collective-permute-start(bf16[512,512]{1,0:T(8,128)(2,1)S(1)} %slice.59), channel_id=1, source_target_pairs={{0,8},{4,12},{8,0},{12,4},{16,24},{20,28},{24,16},{28,20},{1,9},{5... | collective-permute-start | bytes 1572872 | tf_op jit(solution)/shard_map/ppermute | solution.py:14
  111.5 14.9 %collective-permute-start.28 = (bf16[512,512]{1,0:T(8,128)(2,1)S(1)}, bf16[512,512]{1,0:T(8,128)(2,1)S(1)}, u32[]{:S(2)}, u32[]{:S(2)}) collective-permute-start(bf16[512,512]{1,0:T(8,128)(2,1)S(1)} %get-tuple-element.10), channel_id=1, source_target_pairs={{0,16},{4,20},{8,24},{12,28},{16,0},{20,4},{24,8},{28,12},{1,17},{... | collective-permute-start | bytes 1572872 | tf_op jit(solution)/shard_map/ppermute | solution.py:14
  113.4 14.7 %collective-permute-start.8 = (bf16[2,192,1024]{2,1,0:T(8,128)(2,1)S(1)}, bf16[2,192,1024]{2,1,0:T(8,128)(2,1)S(1)}, u32[]{:S(2)}, u32[]{:S(2)}) collective-permute-start(bf16[2,192,1024]{2,1,0:T(8,128)(2,1)S(1)} %add_convert_fusion.3), channel_id=1, source_target_pairs={{2,1},{3,2},{6,5},{7,6},{10,9},{11,10},{14,13},{15,14},{18,17},{19... | collective-permute-start | bytes 2359304 | tf_op jit(solution)/shard_map/ppermute | solution.py:46
  122.4 15.2 %collective-permute-start.27 = (bf16[512,512]{1,0:T(8,128)(2,1)S(1)}, bf16[512,512]{1,0:T(8,128)(2,1)S(1)}, u32[]{:S(2)}, u32[]{:S(2)}) collective-permute-start(bf16[512,512]{1,0:T(8,128)(2,1)S(1)} %slice.58), channel_id=1, source_target_pairs={{0,16},{4,20},{8,24},{12,28},{16,0},{20,4},{24,8},{28,12},{1,17},{... | collective-permute-start | bytes 1572872 | tf_op jit(solution)/shard_map/ppermute | solution.py:14
  126.4 21.4 %collective-permute-start.26 = (bf16[512,512]{1,0:T(8,128)(2,1)S(1)}, bf16[512,512]{1,0:T(8,128)(2,1)S(1)}, u32[]{:S(2)}, u32[]{:S(2)}) collective-permute-start(bf16[512,512]{1,0:T(8,128)(2,1)S(1)} %fusion.44), channel_id=1, source_target_pairs={{0,16},{4,20},{8,24},{12,28},{16,0},{20,4},{24,8},{28,12},{1,17},{... | collective-permute-start | bytes 1572872 | tf_op jit(solution)/shard_map/ppermute | solution.py:14
  128.1 19.7 %collective-permute-start.29 = (bf16[512,512]{1,0:T(8,128)(2,1)S(1)}, bf16[512,512]{1,0:T(8,128)(2,1)S(1)}, u32[]{:S(2)}, u32[]{:S(2)}) collective-permute-start(bf16[512,512]{1,0:T(8,128)(2,1)S(1)} %fusion.42), channel_id=1, source_target_pairs={{0,8},{4,12},{8,0},{12,4},{16,24},{20,28},{24,16},{28,20},{1,9},{5... | collective-permute-start | bytes 1572872 | tf_op jit(solution)/shard_map/ppermute | solution.py:14
  133.6 27.2 %collective-permute-start.9 = (bf16[2,192,1024]{2,1,0:T(8,128)(2,1)S(1)}, bf16[2,192,1024]{2,1,0:T(8,128)(2,1)S(1)}, u32[]{:S(2)}, u32[]{:S(2)}) collective-permute-start(bf16[2,192,1024]{2,1,0:T(8,128)(2,1)S(1)} %add_convert_fusion.2), channel_id=1, source_target_pairs={{1,0},{2,1},{3,2},{5,4},{6,5},{7,6},{9,8},{10,9},{11,10},{13,12},{... | collective-permute-start | bytes 2359304 | tf_op jit(solution)/shard_map/ppermute | solution.py:46

commit v2 on v1

--- a/solution.py
+++ b/solution.py
@@ -14,7 +14,7 @@
     return lax.ppermute(array, axis, [(i, i ^ bit) for i in range(count)])
 
 
-def exclusive_scan(part, axis, reverse):
+def exclusive_scan(part, axis, reverse, beside=()):
     count = lax.axis_size(axis)
     place = lax.axis_index(axis)
     core = place % 2
@@ -29,13 +29,13 @@
         before = before + jnp.where(takes, came, 0.0)
         total = total + came
         bit *= 2
-    before = before.astype(jnp.bfloat16)
+    before, beside = lax.optimization_barrier((before.astype(jnp.bfloat16), beside))
     came = swap(before, axis, 1)
     first = jnp.where(core == 0, before, came)
     second = jnp.where(core == 0, came, before)
     pairs = jnp.stack([first, second]).astype(jnp.float32)
     takes = (core == 0) if reverse else (core == 1)
-    return pairs + jnp.where(takes, other, 0.0)
+    return pairs + jnp.where(takes, other, 0.0), beside
 
 
 def right_of(array, axis, first, last):
@@ -46,34 +46,58 @@
     return lax.ppermute(array, axis, [(i, i - 1) for i in range(first, last)])
 
 
-def gather_line(block, axis):
-    count = lax.axis_size(axis)
-    place = lax.axis_index(axis)
-    from_left, from_right = block, block
-    lefts, rights = {}, {}
-    for step in range(1, count):
-        from_left = right_of(from_left, axis, step - 1, count - 1)
-        from_right = left_of(from_right, axis, 1, count - step + 1)
-        lefts[step], rights[step] = from_left, from_right
-    blocks = [block]
-    for offset in range(1, count):
-        blocks.append(
-            jnp.where(place + offset < count, rights[offset], lefts[count - offset])
-        )
-    return blocks
-
-
-def scatter_line(terms, axis):
-    count = lax.axis_size(axis)
-    rightward = leftward = None
-    for step in range(1, count):
-        to_right, to_left = terms[count - step], terms[step]
-        if rightward is not None:
-            to_right = to_right + rightward.astype(jnp.float32)
-            to_left = to_left + leftward.astype(jnp.float32)
-        rightward = right_of(to_right.astype(jnp.bfloat16), axis, 0, step)
-        leftward = left_of(to_left.astype(jnp.bfloat16), axis, count - step, count)
-    return terms[0] + rightward.astype(jnp.float32) + leftward.astype(jnp.float32)
+def line_order(count):
+    table = []
+    for place in range(count):
+        entries = []
+        for block in range(count):
+            entries.append((abs(block - place), int(block > place), block))
+        table.append(sorted(entries))
+    return table
+
+
+def look_up(values, place):
+    out = jnp.int32(values[0])
+    for i, value in enumerate(values[1:], 1):
+        out = jnp.where(place == i, value, out)
+    return out
+
+
+def gather_step(came, axis, step):
+    count = lax.axis_size(axis)
+    return (
+        right_of(came[0], axis, step - 1, count - 1),
+        left_of(came[1], axis, 1, count - step + 1),
+    )
+
+
+def pick(arrived, rank, table, place):
+    choices = {}
+    for i, row in enumerate(table):
+        choices.setdefault(row[rank][:2], []).append(i)
+    out = None
+    for (distance, side), owners in choices.items():
+        block = arrived[distance][side]
+        if out is None:
+            out = block
+        else:
+            wanted = place == owners[0]
+            for owner in owners[1:]:
+                wanted = wanted | (place == owner)
+            out = jnp.where(wanted, block, out)
+    return out
+
+
+def scatter_step(terms, came, axis, step):
+    count = lax.axis_size(axis)
+    to_right, to_left = terms[count - step], terms[step]
+    if came is not None:
+        to_right = to_right + came[0].astype(jnp.float32)
+        to_left = to_left + came[1].astype(jnp.float32)
+    return (
+        right_of(to_right.astype(jnp.bfloat16), axis, 0, step),
+        left_of(to_left.astype(jnp.bfloat16), axis, count - step, count),
+    )
 
 
 def halve(blocks, axis, bits):
@@ -111,6 +135,10 @@
     rows_index = lax.broadcasted_iota(jnp.int32, (length, length), 0)
     cols_index = lax.broadcasted_iota(jnp.int32, (length, length), 1)
     lower = rows_index >= cols_index
+    groups = lax.axis_size("head")
+    group = lax.axis_index("head")
+    arrived = {0: (cotangent, cotangent)}
+    arrived[1] = gather_step(arrived[0], "head", 1)
     query_heads = split_heads(queries)
     key_heads = split_heads(key_rows)
     value_heads = split_heads(value_rows)
@@ -122,7 +150,9 @@
     local_state = jnp.einsum(
         "bhsd,bhse->bhde", key_heads, value_heads, preferred_element_type=jnp.float32
     )
-    state = exclusive_scan(local_state, "ctx", False)
+    state, arrived[1] = exclusive_scan(local_state, "ctx", False, arrived[1])
+    for step in range(2, groups):
+        arrived[step] = gather_step(arrived[step - 1], "head", step)
     state_bf = state.astype(jnp.bfloat16)
     attended = jnp.einsum(
         "bhts,bhsd->bhtd", scores, value_heads, preferred_element_type=jnp.float32
@@ -131,49 +161,78 @@
         "bhtd,bhde->bhte", query_heads, state_bf, preferred_element_type=jnp.float32
     )
     normed_flat = join_heads(rms_normalize(attended).astype(jnp.bfloat16))
-    groups = lax.axis_size("head")
-    group = lax.axis_index("head")
     width = cotangent.shape[2]
-    columns = [
-        lax.dynamic_slice_in_dim(out_weight, (group + o) % groups * width, width, 1)
+    terms = [
+        jnp.einsum(
+            "btr,rc->btc",
+            normed_flat,
+            lax.dynamic_slice_in_dim(out_weight, (group + o) % groups * width, width, 1),
+            preferred_element_type=jnp.float32,
+        )
         for o in range(groups)
     ]
-    grads = gather_line(cotangent, "head")
-    layer_output = scatter_line(
-        [
-            jnp.einsum("btr,rc->btc", normed_flat, part, preferred_element_type=jnp.float32)
-            for part in columns
-        ],
-        "head",
+    came_out = scatter_step(terms, None, "head", 1)
+    places = lax.axis_size("ctx")
+    core = lax.axis_index("ctx") % 2
+    span = groups * width // places
+    chips = places // 2
+    table = line_order(groups)
+    per = chips // groups
+    normed_grad = 0.0
+    pair_sums = []
+    for rank in range(groups):
+        block = look_up([row[rank][2] for row in table], group)
+        grad = pick(arrived, rank, table, group)
+        if rank == groups - 1:
+            grad, pair_sums, came_out = lax.optimization_barrier((grad, pair_sums, came_out))
+        columns = lax.dynamic_slice_in_dim(out_weight, block * width, width, 1)
+        normed_grad = normed_grad + jnp.einsum(
+            "btc,rc->btr", grad, columns, preferred_element_type=jnp.float32
+        )
+        for t in range(per):
+            theirs, ours = [
+                jnp.einsum(
+                    "btr,btc->rc",
+                    normed_flat,
+                    lax.dynamic_slice_in_dim(grad, (2 * t + side) * span, span, 2),
+                    preferred_element_type=jnp.float32,
+                )
+                for side in (1 - core, core)
+            ]
+            came = swap(theirs.astype(jnp.bfloat16), "ctx", 1)
+            pair_sums.append((ours + came.astype(jnp.float32)).astype(jnp.bfloat16))
+    pullback = jax.vjp(rms_normalize, attended)[1]
+    attended_grad = pullback(split_heads(normed_grad))[0].astype(jnp.bfloat16)
+    local_grad_state = jnp.einsum(
+        "bhtd,bhte->bhde", query_heads, attended_grad, preferred_element_type=jnp.float32
+    )
+    pair_sums = jnp.stack(pair_sums)
+    for step in range(2, groups - 1):
+        came_out = scatter_step(terms, came_out, "head", step)
+    grad_state, (pair_sums, came_out) = exclusive_scan(
+        local_grad_state, "ctx", True, (pair_sums, came_out)
+    )
+    came_out = scatter_step(terms, came_out, "head", groups - 1)
+    layer_output = (
+        terms[0] + came_out[0].astype(jnp.float32) + came_out[1].astype(jnp.float32)
     ).astype(jnp.bfloat16)
-    normed_grad = sum(
-        jnp.einsum("btc,rc->btr", grad, part, preferred_element_type=jnp.float32)
-        for grad, part in zip(grads, columns)
-    )
-    places = lax.axis_size("ctx")
-    place = lax.axis_index("ctx")
-    span = groups * width // places
-    grad_all = jnp.concatenate(grads, axis=2)
+    chip = lax.axis_index("ctx") // 2
+    positions = [[[e[2] for e in row].index(g) for row in table] for g in range(groups)]
     blocks = {}
-    for k in range(places):
-        start = ((place ^ k) * span - group * width) % (groups * width)
-        wanted = lax.dynamic_slice_in_dim(grad_all, start, span, 2)
-        blocks[k] = jnp.einsum(
-            "btr,btc->rc", normed_flat, wanted, preferred_element_type=jnp.float32
-        )
-    blocks = halve(blocks, "ctx", [1])
+    for k in range(chips):
+        wanted = chip ^ k
+        rank = jnp.int32(0)
+        for g in range(groups):
+            rank = jnp.where(wanted // per == g, look_up(positions[g], group), rank)
+        blocks[2 * k] = lax.dynamic_index_in_dim(
+            pair_sums, rank * per + wanted % per, 0, False
+        ).astype(jnp.float32)
     bits = [1 << i for i in range(1, places.bit_length() - 1)]
     rows = normed_flat.shape[2] // 2
     upper = halve({k: block[:rows] for k, block in blocks.items()}, "ctx", bits)
     lower_rows = halve({k: block[rows:] for k, block in blocks.items()}, "ctx", bits[::-1])
     token_factor = (2 * length * places) ** (-0.5)
     weight_grad = jnp.concatenate([upper[0], lower_rows[0]], axis=0) * token_factor
-    pullback = jax.vjp(rms_normalize, attended)[1]
-    attended_grad = pullback(split_heads(normed_grad))[0].astype(jnp.bfloat16)
-    local_grad_state = jnp.einsum(
-        "bhtd,bhte->bhde", query_heads, attended_grad, preferred_element_type=jnp.float32
-    )
-    grad_state = exclusive_scan(local_grad_state, "ctx", True)
     grad_state_bf = grad_state.astype(jnp.bfloat16)
     raw_grad = (
         jnp.einsum(

time: 163 us -> 168 us (1.031)
  waiting for transfers between devices: 74.9 us -> 83.9 us
  starting transfers between devices: 44.3 us -> 40.9 us
    ppermute x6, waiting for transfers between devices: 23.6 us -> 31.7 us  [left_of(): return lax.ppermute(array, axis, [(i, i - 1) for i in range(first, last)])]
    ppermute x6, starting transfers between devices: 21.8 us -> 18.2 us  [right_of(): return lax.ppermute(array, axis, [(i, i + 1) for i in range(first, last)])]
  transfers between devices with their start and end apart: 30 -> 30, of which waited for: 14 -> 13; matrix products, arithmetic and copies ran while one was open for 22% -> 17% of each run, Pallas kernels for 0% -> 0%
where the time goes in v2:
time: 168 us
  waiting for transfers between devices  83.9 us (50%)
  starting transfers between devices  40.9 us (24%)
  matrix products  24.7 us (15%)
  other arithmetic  11.5 us (7%)
  local copies, waits for them, and re-layouts  5.16 us (3%)
    ppermute x18, waiting for transfers between devices, swap(): return lax.ppermute(array, axis, [(i, i ^ bit) for i in range(count)])  47.5 us
    ppermute x6, waiting for transfers between devices, left_of(): return lax.ppermute(array, axis, [(i, i - 1) for i in range(first, last)])  31.7 us
    ppermute x6, starting transfers between devices, right_of(): return lax.ppermute(array, axis, [(i, i + 1) for i in range(first, last)])  18.2 us
    ppermute x18, starting transfers between devices, swap(): return lax.ppermute(array, axis, [(i, i ^ bit) for i in range(count)])  15.7 us
    ppermute x6, starting transfers between devices, left_of(): return lax.ppermute(array, axis, [(i, i - 1) for i in range(first, last)])  6.97 us
    dot_general x8, matrix products, shards(): jnp.einsum('btr,btc->rc', normed_flat, lax.dynamic_slice_in_dim(grad, (2...  5.97 us
    dot_general x4, matrix products, shards(): jnp.einsum('btc,rc->btr', grad, columns, preferred_element_type=jnp.float32)  5.77 us
    ppermute x6, waiting for transfers between devices, right_of(): return lax.ppermute(array, axis, [(i, i + 1) for i in range(first, last)])  4.71 us
  transfers between devices with their start and end apart: 30, of which 13 were waited for; matrix products, arithmetic and copies ran while one was open for 17% of the time, Pallas kernels for 0%

profile of v2, /device:TPU:0, one launch (start us, length us, event | category | flops | bytes accessed | tf_op | source)
XLA Modules:
  0.0 167.7 jit_solution(3744291444002654249)
XLA Ops:
  0.6 1.1 copy-done
  1.8 2.6 %fusion.129 = (bf16[2,8,128,128]{3,2,1,0:T(8,128)(2,1)S(1)}, f32[2,8,128,128]{3,2,1,0:T(8,128)}) fusion(bf16[2,192,1024]{2,1,0:T(8,128)(2,1)S(1)} %copy-done, bf16[2,192,1024]{2,1,0:T(8,128)(2,1)} %param.6), kind=kOutput, calls=%fused_computation.191 | convolution fusion | flops 100925440 | bytes 3145728 | tf_op jit(solution)/shard_map/bhsd,bhse->bhde/dot_general | solution.py:150
  4.8 1.5 collective-permute-done
  6.6 0.9 copy-done.4
  7.5 2.9 %collective-permute-start.1 = (bf16[8,128,128]{2,1,0:T(8,128)(2,1)S(1)}, bf16[8,128,128]{2,1,0:T(8,128)(2,1)S(1)}, u32[]{:S(2)}, u32[]{:S(2)}) collective-permute-start(bf16[8,128,128]{2,1,0:T(8,128)(2,1)S(1)} %fusion.95), channel_id=1, source_target_pairs={{0,8},{4,12},{8,0},{12,4},{16,24},{20,28},{24,16},{28,20},{1,9},{5... | collective-permute-start | bytes 786440 | tf_op jit(solution)/shard_map/ppermute | solution.py:14
  10.3 4.4 %collective-permute-start.3 = (bf16[2,192,1024]{2,1,0:T(8,128)(2,1)}, bf16[2,192,1024]{2,1,0:T(8,128)(2,1)}, u32[]{:S(2)}, u32[]{:S(2)}) collective-permute-start(bf16[2,192,1024]{2,1,0:T(8,128)(2,1)} %param.9), channel_id=1, source_target_pairs={{0,1},{1,2},{2,3},{4,5},{5,6},{6,7},{8,9},{9,10},{10,11},{12,13},{... | collective-permute-start | bytes 2359304 | tf_op jit(solution)/shard_map/ppermute | solution.py:42
  14.7 1.3 collective-permute-start.4
  16.9 1.3 fusion.69
  18.2 1.8 %collective-permute-start.2 = (bf16[8,128,128]{2,1,0:T(8,128)(2,1)S(1)}, bf16[8,128,128]{2,1,0:T(8,128)(2,1)S(1)}, u32[]{:S(2)}, u32[]{:S(2)}) collective-permute-start(bf16[8,128,128]{2,1,0:T(8,128)(2,1)S(1)} %fusion.69), channel_id=1, source_target_pairs={{0,16},{4,20},{8,24},{12,28},{16,0},{20,4},{24,8},{28,12},{1,17},{... | collective-permute-start | bytes 786440 | tf_op jit(solution)/shard_map/ppermute | solution.py:14
  20.7 5.4 %collective-permute-done.2 = bf16[8,128,128]{2,1,0:T(8,128)(2,1)S(1)} collective-permute-done((bf16[8,128,128]{2,1,0:T(8,128)(2,1)S(1)}, bf16[8,128,128]{2,1,0:T(8,128)(2,1)S(1)}, u32[]{:S(2)}, u32[]{:S(2)}) %collective-permute-start.2) | collective-permute-done | bytes 262176 | tf_op jit(solution)/shard_map/ppermute | solution.py:14
  26.2 4.7 %collective-permute-done.3 = bf16[2,192,1024]{2,1,0:T(8,128)(2,1)} collective-permute-done((bf16[2,192,1024]{2,1,0:T(8,128)(2,1)}, bf16[2,192,1024]{2,1,0:T(8,128)(2,1)}, u32[]{:S(2)}, u32[]{:S(2)}) %collective-permute-start.3) | collective-permute-done | bytes 786464 | tf_op jit(solution)/shard_map/ppermute | solution.py:42
  30.9 5.0 %collective-permute-done.4 = bf16[2,192,1024]{2,1,0:T(8,128)(2,1)} collective-permute-done((bf16[2,192,1024]{2,1,0:T(8,128)(2,1)}, bf16[2,192,1024]{2,1,0:T(8,128)(2,1)}, u32[]{:S(2)}, u32[]{:S(2)}) %collective-permute-start.4) | collective-permute-done | bytes 786464 | tf_op jit(solution)/shard_map/ppermute | solution.py:46
  35.9 2.6 %fusion.14 = f32[1024,2,192]{0,2,1:T(8,128)S(1)} fusion(bf16[2,192,1024]{2,1,0:T(8,128)(2,1)S(1)} %copy-done.5, bf16[1024,4096]{1,0:T(8,128)(2,1)} %param.8, s32[]{:T(128)S(6)} %select_n.387), kind=kOutput, calls=%fused_computation.27 | convolution fusion | flops 805306368 | bytes 4456452 | tf_op jit(solution)/shard_map/btc,rc->btr/dot_general | solution.py:189
  39.3 1.3 collective-permute-start.7
  41.1 0.8 multiply_reduce_fusion
  44.2 1.0 fusion.130
  45.2 6.1 %collective-permute-start.13 = (bf16[2,192,1024]{2,1,0:T(8,128)(2,1)S(1)}, bf16[2,192,1024]{2,1,0:T(8,128)(2,1)S(1)}, u32[]{:S(2)}, u32[]{:S(2)}) collective-permute-start(bf16[2,192,1024]{2,1,0:T(8,128)(2,1)S(1)} %get-tuple-element.55), channel_id=1, source_target_pairs={{0,1},{4,5},{8,9},{12,13},{16,17},{20,21},{24,25},{28,29}} | collective-permute-start | bytes 2359304 | tf_op jit(solution)/shard_map/ppermute | solution.py:42
  52.0 10.8 %collective-permute-done.7 = bf16[2,192,1024]{2,1,0:T(8,128)(2,1)S(1)} collective-permute-done((bf16[2,192,1024]{2,1,0:T(8,128)(2,1)}, bf16[2,192,1024]{2,1,0:T(8,128)(2,1)S(1)}, u32[]{:S(2)}, u32[]{:S(2)}) %collective-permute-start.7) | collective-permute-done | bytes 786464 | tf_op jit(solution)/shard_map/ppermute | solution.py:46
  62.9 1.3 collective-permute-start.9
  64.1 1.0 fusion.131
  65.1 0.9 collective-permute-start.14
  66.0 1.0 fusion
  67.0 1.0 fusion.18
  68.0 15.9 %collective-permute-done.9 = bf16[2,192,1024]{2,1,0:T(8,128)(2,1)S(1)} collective-permute-done((bf16[2,192,1024]{2,1,0:T(8,128)(2,1)S(1)}, bf16[2,192,1024]{2,1,0:T(8,128)(2,1)S(1)}, u32[]{:S(2)}, u32[]{:S(2)}) %collective-permute-start.9) | collective-permute-done | bytes 786464 | tf_op jit(solution)/shard_map/ppermute | solution.py:46
  83.9 1.4 select_select_fusion
  88.2 1.0 fusion.10
  89.2 1.0 fusion.12
  92.5 1.1 fusion.37
  93.6 1.1 fusion.32
  94.8 1.0 fusion.28
  97.9 1.7 %collective-permute-start.19 = (bf16[2,192,1024]{2,1,0:T(8,128)(2,1)S(1)}, bf16[2,192,1024]{2,1,0:T(8,128)(2,1)S(1)}, u32[]{:S(2)}, u32[]{:S(2)}) collective-permute-start(bf16[2,192,1024]{2,1,0:T(8,128)(2,1)S(1)} %get-tuple-element.40), channel_id=1, source_target_pairs={{0,1},{1,2},{4,5},{5,6},{8,9},{9,10},{12,13},{13,14},{16,17},{17,1... | collective-permute-start | bytes 2359304 | tf_op jit(solution)/shard_map/ppermute | solution.py:42
  99.7 0.9 collective-permute-start.20
  101.7 1.1 copy.151
  104.3 6.7 %collective-permute-done.16 = bf16[8,128,128]{2,1,0:T(8,128)(2,1)S(1)} collective-permute-done((bf16[8,128,128]{2,1,0:T(8,128)(2,1)S(1)}, bf16[8,128,128]{2,1,0:T(8,128)(2,1)S(1)}, u32[]{:S(2)}, u32[]{:S(2)}) %collective-permute-start.16) | collective-permute-done | bytes 262176 | tf_op jit(solution)/shard_map/ppermute | solution.py:14
  111.1 1.6 collective-permute-start.17
  113.5 4.9 %collective-permute-done.17 = bf16[8,128,128]{2,1,0:T(8,128)(2,1)S(1)} collective-permute-done((bf16[8,128,128]{2,1,0:T(8,128)(2,1)S(1)}, bf16[8,128,128]{2,1,0:T(8,128)(2,1)S(1)}, u32[]{:S(2)}, u32[]{:S(2)}) %collective-permute-start.17) | collective-permute-done | bytes 262176 | tf_op jit(solution)/shard_map/ppermute | solution.py:14
  120.1 1.3 collective-permute-start.22
  121.7 4.6 %collective-permute-start.21 = (bf16[2,192,1024]{2,1,0:T(8,128)(2,1)S(1)}, bf16[2,192,1024]{2,1,0:T(8,128)(2,1)S(1)}, u32[]{:S(2)}, u32[]{:S(2)}) collective-permute-start(bf16[2,192,1024]{2,1,0:T(8,128)(2,1)S(1)} %add_convert_fusion.3), channel_id=1, source_target_pairs={{0,1},{1,2},{2,3},{4,5},{5,6},{6,7},{8,9},{9,10},{10,11},{12,13},{... | collective-permute-start | bytes 2359304 | tf_op jit(solution)/shard_map/ppermute | solution.py:42
  127.1 1.5 collective-permute-start.28
  128.9 1.5 collective-permute-start.24
  131.5 9.8 %collective-permute-done.25 = bf16[512,512]{1,0:T(8,128)(2,1)S(1)} collective-permute-done((bf16[512,512]{1,0:T(8,128)(2,1)S(1)}, bf16[512,512]{1,0:T(8,128)(2,1)S(1)}, u32[]{:S(2)}, u32[]{:S(2)}) %collective-permute-start.25) | collective-permute-done | bytes 524320 | tf_op jit(solution)/shard_map/ppermute | solution.py:14
  141.3 1.5 collective-permute-start.27
  144.5 1.4 copy_bitcast_fusion
  145.9 1.3 add_convert_fusion.1
  147.2 5.4 %collective-permute-done.24 = bf16[512,512]{1,0:T(8,128)(2,1)S(1)} collective-permute-done((bf16[512,512]{1,0:T(8,128)(2,1)S(1)}, bf16[512,512]{1,0:T(8,128)(2,1)S(1)}, u32[]{:S(2)}, u32[]{:S(2)}) %collective-permute-start.24) | collective-permute-done | bytes 524320 | tf_op jit(solution)/shard_map/ppermute | solution.py:14
  152.5 3.6 %collective-permute-done.27 = bf16[512,512]{1,0:T(8,128)(2,1)S(1)} collective-permute-done((bf16[512,512]{1,0:T(8,128)(2,1)S(1)}, bf16[512,512]{1,0:T(8,128)(2,1)S(1)}, u32[]{:S(2)}, u32[]{:S(2)}) %collective-permute-start.27) | collective-permute-done | bytes 524320 | tf_op jit(solution)/shard_map/ppermute | solution.py:14
  156.2 9.5 %collective-permute-done.26 = bf16[512,512]{1,0:T(8,128)(2,1)S(1)} collective-permute-done((bf16[512,512]{1,0:T(8,128)(2,1)S(1)}, bf16[512,512]{1,0:T(8,128)(2,1)S(1)}, u32[]{:S(2)}, u32[]{:S(2)}) %collective-permute-start.26) | collective-permute-done | bytes 524320 | tf_op jit(solution)/shard_map/ppermute | solution.py:14
  166.1 1.6 maximum_multiply_fusion
  (86 shorter events, 23.2 us)
Async XLA Ops:
  0.6 1.1 copy-start
  4.4 2.0 %collective-permute-start = (bf16[2,8,128,128]{3,2,1,0:T(8,128)(2,1)S(1)}, bf16[2,8,128,128]{3,2,1,0:T(8,128)(2,1)S(1)}, u32[]{:S(2)}, u32[]{:S(2)}) collective-permute-start(bf16[2,8,128,128]{3,2,1,0:T(8,128)(2,1)S(1)} %get-tuple-element.51), channel_id=1, source_target_pairs={{0,4},{4,0},{8,12},{12,8},{16,20},{20,16},{24,28},{28,24},{1,5},{5... | collective-permute-start | bytes 1572872 | tf_op jit(solution)/shard_map/ppermute | solution.py:14
  4.8 1.7 copy-start.3
  6.5 1.0 copy-start.4
  6.5 13.6 %copy-start.1 = (bf16[2,192,1024]{2,1,0:T(8,128)(2,1)S(1)}, bf16[2,192,1024]{2,1,0:T(8,128)(2,1)}, u32[]{:S(2)}) copy-start(bf16[2,192,1024]{2,1,0:T(8,128)(2,1)} %param.6) | copy-start | bytes 2359300
  6.5 13.6 %copy-start.2 = (bf16[2,192,1024]{2,1,0:T(8,128)(2,1)S(1)}, bf16[2,192,1024]{2,1,0:T(8,128)(2,1)}, u32[]{:S(2)}) copy-start(bf16[2,192,1024]{2,1,0:T(8,128)(2,1)} %param.5) | copy-start | bytes 2359300
  7.5 9.5 %collective-permute-start.1 = (bf16[8,128,128]{2,1,0:T(8,128)(2,1)S(1)}, bf16[8,128,128]{2,1,0:T(8,128)(2,1)S(1)}, u32[]{:S(2)}, u32[]{:S(2)}) collective-permute-start(bf16[8,128,128]{2,1,0:T(8,128)(2,1)S(1)} %fusion.95), channel_id=1, source_target_pairs={{0,8},{4,12},{8,0},{12,4},{16,24},{20,28},{24,16},{28,20},{1,9},{5... | collective-permute-start | bytes 786440 | tf_op jit(solution)/shard_map/ppermute | solution.py:14
  10.3 20.6 %collective-permute-start.3 = (bf16[2,192,1024]{2,1,0:T(8,128)(2,1)}, bf16[2,192,1024]{2,1,0:T(8,128)(2,1)}, u32[]{:S(2)}, u32[]{:S(2)}) collective-permute-start(bf16[2,192,1024]{2,1,0:T(8,128)(2,1)} %param.9), channel_id=1, source_target_pairs={{0,1},{1,2},{2,3},{4,5},{5,6},{6,7},{8,9},{9,10},{10,11},{12,13},{... | collective-permute-start | bytes 2359304 | tf_op jit(solution)/shard_map/ppermute | solution.py:42
  14.7 21.2 %collective-permute-start.4 = (bf16[2,192,1024]{2,1,0:T(8,128)(2,1)}, bf16[2,192,1024]{2,1,0:T(8,128)(2,1)}, u32[]{:S(2)}, u32[]{:S(2)}) collective-permute-start(bf16[2,192,1024]{2,1,0:T(8,128)(2,1)} %param.9), channel_id=1, source_target_pairs={{1,0},{2,1},{3,2},{5,4},{6,5},{7,6},{9,8},{10,9},{11,10},{13,12},{... | collective-permute-start | bytes 2359304 | tf_op jit(solution)/shard_map/ppermute | solution.py:46
  18.2 17.7 %copy-start.5 = (bf16[2,192,1024]{2,1,0:T(8,128)(2,1)S(1)}, bf16[2,192,1024]{2,1,0:T(8,128)(2,1)}, u32[]{:S(2)}) copy-start(bf16[2,192,1024]{2,1,0:T(8,128)(2,1)} %param.9) | copy-start | bytes 2359300
  18.2 7.9 %collective-permute-start.2 = (bf16[8,128,128]{2,1,0:T(8,128)(2,1)S(1)}, bf16[8,128,128]{2,1,0:T(8,128)(2,1)S(1)}, u32[]{:S(2)}, u32[]{:S(2)}) collective-permute-start(bf16[8,128,128]{2,1,0:T(8,128)(2,1)S(1)} %fusion.69), channel_id=1, source_target_pairs={{0,16},{4,20},{8,24},{12,28},{16,0},{20,4},{24,8},{28,12},{1,17},{... | collective-permute-start | bytes 786440 | tf_op jit(solution)/shard_map/ppermute | solution.py:14
  35.9 4.7 %collective-permute-start.5 = (bf16[8,128,128]{2,1,0:T(8,128)(2,1)S(1)}, bf16[8,128,128]{2,1,0:T(8,128)(2,1)S(1)}, u32[]{:S(2)}, u32[]{:S(2)}) collective-permute-start(bf16[8,128,128]{2,1,0:T(8,128)(2,1)S(1)} %fusion.68), channel_id=1, source_target_pairs={{0,4},{4,0},{8,12},{12,8},{16,20},{20,16},{24,28},{28,24},{1,5},{5... | collective-permute-start | bytes 786440 | tf_op jit(solution)/shard_map/ppermute | solution.py:14
  38.6 12.7 %collective-permute-start.6 = (bf16[2,192,1024]{2,1,0:T(8,128)(2,1)}, bf16[2,192,1024]{2,1,0:T(8,128)(2,1)S(1)}, u32[]{:S(2)}, u32[]{:S(2)}) collective-permute-start(bf16[2,192,1024]{2,1,0:T(8,128)(2,1)} %collective-permute-done.3), channel_id=1, source_target_pairs={{1,2},{2,3},{5,6},{6,7},{9,10},{10,11},{13,14},{14,15},{17,18},{18... | collective-permute-start | bytes 2359304 | tf_op jit(solution)/shard_map/ppermute | solution.py:42
  39.3 23.6 %collective-permute-start.7 = (bf16[2,192,1024]{2,1,0:T(8,128)(2,1)}, bf16[2,192,1024]{2,1,0:T(8,128)(2,1)S(1)}, u32[]{:S(2)}, u32[]{:S(2)}) collective-permute-start(bf16[2,192,1024]{2,1,0:T(8,128)(2,1)} %collective-permute-done.4), channel_id=1, source_target_pairs={{1,0},{2,1},{5,4},{6,5},{9,8},{10,9},{13,12},{14,13},{17,16},{18,1... | collective-permute-start | bytes 2359304 | tf_op jit(solution)/shard_map/ppermute | solution.py:46
  40.7 3.1 %slice-start = ((s8[8388608]{0:T(1024)(128)(4,1)}), s8[4194304]{0:T(1024)(128)(4,1)S(1)}, s32[]{:S(2)}) async-start(s8[8388608]{0:T(1024)(128)(4,1)} %bitcast.337), calls=%async_computation | async-start | bytes 8388608
  41.0 3.2 %slice-start.1 = ((s8[8388608]{0:T(1024)(128)(4,1)}), s8[4194304]{0:T(1024)(128)(4,1)S(1)}, s32[]{:S(2)}) async-start(s8[8388608]{0:T(1024)(128)(4,1)} %bitcast.337), calls=%async_computation.1 | async-start | bytes 8388608
  43.2 44.2 %collective-permute-start.10 = (bf16[1024,512]{1,0:T(8,128)(2,1)S(1)}, bf16[1024,512]{1,0:T(8,128)(2,1)S(1)}, u32[]{:S(2)}, u32[]{:S(2)}) collective-permute-start(bf16[1024,512]{1,0:T(8,128)(2,1)S(1)} %bitcast_convert_fusion.3), channel_id=1, source_target_pairs={{0,4},{4,0},{8,12},{12,8},{16,20},{20,16},{24,28},{28,24},{1,5},{5... | collective-permute-start | bytes 3145736 | tf_op jit(solution)/shard_map/ppermute | solution.py:14
  45.2 46.5 %collective-permute-start.13 = (bf16[2,192,1024]{2,1,0:T(8,128)(2,1)S(1)}, bf16[2,192,1024]{2,1,0:T(8,128)(2,1)S(1)}, u32[]{:S(2)}, u32[]{:S(2)}) collective-permute-start(bf16[2,192,1024]{2,1,0:T(8,128)(2,1)S(1)} %get-tuple-element.55), channel_id=1, source_target_pairs={{0,1},{4,5},{8,9},{12,13},{16,17},{20,21},{24,25},{28,29}} | collective-permute-start | bytes 2359304 | tf_op jit(solution)/shard_map/ppermute | solution.py:42
  51.3 16.7 %collective-permute-start.8 = (bf16[2,192,1024]{2,1,0:T(8,128)(2,1)S(1)}, bf16[2,192,1024]{2,1,0:T(8,128)(2,1)S(1)}, u32[]{:S(2)}, u32[]{:S(2)}) collective-permute-start(bf16[2,192,1024]{2,1,0:T(8,128)(2,1)S(1)} %collective-permute-done.6), channel_id=1, source_target_pairs={{2,3},{6,7},{10,11},{14,15},{18,19},{22,23},{26,27},{30,31}} | collective-permute-start | bytes 2359304 | tf_op jit(solution)/shard_map/ppermute | solution.py:42
  62.9 21.1 %collective-permute-start.9 = (bf16[2,192,1024]{2,1,0:T(8,128)(2,1)S(1)}, bf16[2,192,1024]{2,1,0:T(8,128)(2,1)S(1)}, u32[]{:S(2)}, u32[]{:S(2)}) collective-permute-start(bf16[2,192,1024]{2,1,0:T(8,128)(2,1)S(1)} %collective-permute-done.7), channel_id=1, source_target_pairs={{1,0},{5,4},{9,8},{13,12},{17,16},{21,20},{25,24},{29,28}} | collective-permute-start | bytes 2359304 | tf_op jit(solution)/shard_map/ppermute | solution.py:46
  65.1 26.6 %collective-permute-start.14 = (bf16[2,192,1024]{2,1,0:T(8,128)(2,1)S(1)}, bf16[2,192,1024]{2,1,0:T(8,128)(2,1)S(1)}, u32[]{:S(2)}, u32[]{:S(2)}) collective-permute-start(bf16[2,192,1024]{2,1,0:T(8,128)(2,1)S(1)} %get-tuple-element.57), channel_id=1, source_target_pairs={{3,2},{7,6},{11,10},{15,14},{19,18},{23,22},{27,26},{31,30}} | collective-permute-start | bytes 2359304 | tf_op jit(solution)/shard_map/ppermute | solution.py:46
  86.0 4.2 %collective-permute-start.11 = (bf16[1024,512]{1,0:T(8,128)(2,1)S(1)}, bf16[1024,512]{1,0:T(8,128)(2,1)S(1)}, u32[]{:S(2)}, u32[]{:S(2)}) collective-permute-start(bf16[1024,512]{1,0:T(8,128)(2,1)S(1)} %bitcast_convert_fusion.2), channel_id=1, source_target_pairs={{0,4},{4,0},{8,12},{12,8},{16,20},{20,16},{24,28},{28,24},{1,5},{5... | collective-permute-start | bytes 3145736 | tf_op jit(solution)/shard_map/ppermute | solution.py:14
  86.9 4.1 %collective-permute-start.12 = (bf16[1024,512]{1,0:T(8,128)(2,1)S(1)}, bf16[1024,512]{1,0:T(8,128)(2,1)S(1)}, u32[]{:S(2)}, u32[]{:S(2)}) collective-permute-start(bf16[1024,512]{1,0:T(8,128)(2,1)S(1)} %bitcast_convert_fusion.1), channel_id=1, source_target_pairs={{0,4},{4,0},{8,12},{12,8},{16,20},{20,16},{24,28},{28,24},{1,5},{5... | collective-permute-start | bytes 3145736 | tf_op jit(solution)/shard_map/ppermute | solution.py:14
  96.9 5.9 %collective-permute-start.15 = (bf16[2,8,128,128]{3,2,1,0:T(8,128)(2,1)S(1)}, bf16[2,8,128,128]{3,2,1,0:T(8,128)(2,1)S(1)}, u32[]{:S(2)}, u32[]{:S(2)}) collective-permute-start(bf16[2,8,128,128]{3,2,1,0:T(8,128)(2,1)S(1)} %get-tuple-element.59), channel_id=1, source_target_pairs={{0,4},{4,0},{8,12},{12,8},{16,20},{20,16},{24,28},{28,24},{1,5},{5... | collective-permute-start | bytes 1572872 | tf_op jit(solution)/shard_map/ppermute | solution.py:14
  97.0 21.5 %collective-permute-start.18 = (bf16[1024,512]{1,0:T(8,128)(2,1)S(1)}, bf16[1024,512]{1,0:T(8,128)(2,1)S(1)}, u32[]{:S(2)}, u32[]{:S(2)}) collective-permute-start(bf16[1024,512]{1,0:T(8,128)(2,1)S(1)} %bitcast_convert_fusion), channel_id=1, source_target_pairs={{0,4},{4,0},{8,12},{12,8},{16,20},{20,16},{24,28},{28,24},{1,5},{5... | collective-permute-start | bytes 3145736 | tf_op jit(solution)/shard_map/ppermute | solution.py:14
  97.9 21.9 %collective-permute-start.19 = (bf16[2,192,1024]{2,1,0:T(8,128)(2,1)S(1)}, bf16[2,192,1024]{2,1,0:T(8,128)(2,1)S(1)}, u32[]{:S(2)}, u32[]{:S(2)}) collective-permute-start(bf16[2,192,1024]{2,1,0:T(8,128)(2,1)S(1)} %get-tuple-element.40), channel_id=1, source_target_pairs={{0,1},{1,2},{4,5},{5,6},{8,9},{9,10},{12,13},{13,14},{16,17},{17,1... | collective-permute-start | bytes 2359304 | tf_op jit(solution)/shard_map/ppermute | solution.py:42
  99.7 20.1 %collective-permute-start.20 = (bf16[2,192,1024]{2,1,0:T(8,128)(2,1)S(1)}, bf16[2,192,1024]{2,1,0:T(8,128)(2,1)S(1)}, u32[]{:S(2)}, u32[]{:S(2)}) collective-permute-start(bf16[2,192,1024]{2,1,0:T(8,128)(2,1)S(1)} %get-tuple-element.39), channel_id=1, source_target_pairs={{2,1},{3,2},{6,5},{7,6},{10,9},{11,10},{14,13},{15,14},{18,17},{19... | collective-permute-start | bytes 2359304 | tf_op jit(solution)/shard_map/ppermute | solution.py:46
  103.0 8.1 %collective-permute-start.16 = (bf16[8,128,128]{2,1,0:T(8,128)(2,1)S(1)}, bf16[8,128,128]{2,1,0:T(8,128)(2,1)S(1)}, u32[]{:S(2)}, u32[]{:S(2)}) collective-permute-start(bf16[8,128,128]{2,1,0:T(8,128)(2,1)S(1)} %fusion.96), channel_id=1, source_target_pairs={{0,8},{4,12},{8,0},{12,4},{16,24},{20,28},{24,16},{28,20},{1,9},{5... | collective-permute-start | bytes 786440 | tf_op jit(solution)/shard_map/ppermute | solution.py:14
  111.1 7.2 %collective-permute-start.17 = (bf16[8,128,128]{2,1,0:T(8,128)(2,1)S(1)}, bf16[8,128,128]{2,1,0:T(8,128)(2,1)S(1)}, u32[]{:S(2)}, u32[]{:S(2)}) collective-permute-start(bf16[8,128,128]{2,1,0:T(8,128)(2,1)S(1)} %fusion.72), channel_id=1, source_target_pairs={{0,16},{4,20},{8,24},{12,28},{16,0},{20,4},{24,8},{28,12},{1,17},{... | collective-permute-start | bytes 786440 | tf_op jit(solution)/shard_map/ppermute | solution.py:14
  120.1 23.6 %collective-permute-start.22 = (bf16[2,192,1024]{2,1,0:T(8,128)(2,1)S(1)}, bf16[2,192,1024]{2,1,0:T(8,128)(2,1)S(1)}, u32[]{:S(2)}, u32[]{:S(2)}) collective-permute-start(bf16[2,192,1024]{2,1,0:T(8,128)(2,1)S(1)} %add_convert_fusion.2), channel_id=1, source_target_pairs={{1,0},{2,1},{3,2},{5,4},{6,5},{7,6},{9,8},{10,9},{11,10},{13,12},{... | collective-permute-start | bytes 2359304 | tf_op jit(solution)/shard_map/ppermute | solution.py:46
  121.7 24.2 %collective-permute-start.21 = (bf16[2,192,1024]{2,1,0:T(8,128)(2,1)S(1)}, bf16[2,192,1024]{2,1,0:T(8,128)(2,1)S(1)}, u32[]{:S(2)}, u32[]{:S(2)}) collective-permute-start(bf16[2,192,1024]{2,1,0:T(8,128)(2,1)S(1)} %add_convert_fusion.3), channel_id=1, source_target_pairs={{0,1},{1,2},{2,3},{4,5},{5,6},{6,7},{8,9},{9,10},{10,11},{12,13},{... | collective-permute-start | bytes 2359304 | tf_op jit(solution)/shard_map/ppermute | solution.py:42
  126.3 2.6 %collective-permute-start.23 = (bf16[8,128,128]{2,1,0:T(8,128)(2,1)S(1)}, bf16[8,128,128]{2,1,0:T(8,128)(2,1)S(1)}, u32[]{:S(2)}, u32[]{:S(2)}) collective-permute-start(bf16[8,128,128]{2,1,0:T(8,128)(2,1)S(1)} %fusion.71), channel_id=1, source_target_pairs={{0,4},{4,0},{8,12},{12,8},{16,20},{20,16},{24,28},{28,24},{1,5},{5... | collective-permute-start | bytes 786440 | tf_op jit(solution)/shard_map/ppermute | solution.py:14
  126.5 14.8 %collective-permute-start.25 = (bf16[512,512]{1,0:T(8,128)(2,1)S(1)}, bf16[512,512]{1,0:T(8,128)(2,1)S(1)}, u32[]{:S(2)}, u32[]{:S(2)}) collective-permute-start(bf16[512,512]{1,0:T(8,128)(2,1)S(1)} %get-tuple-element.32), channel_id=1, source_target_pairs={{0,8},{4,12},{8,0},{12,4},{16,24},{20,28},{24,16},{28,20},{1,9},{5... | collective-permute-start | bytes 1572872 | tf_op jit(solution)/shard_map/ppermute | solution.py:14
  127.1 15.7 %collective-permute-start.28 = (bf16[512,512]{1,0:T(8,128)(2,1)S(1)}, bf16[512,512]{1,0:T(8,128)(2,1)S(1)}, u32[]{:S(2)}, u32[]{:S(2)}) collective-permute-start(bf16[512,512]{1,0:T(8,128)(2,1)S(1)} %get-tuple-element.33), channel_id=1, source_target_pairs={{0,16},{4,20},{8,24},{12,28},{16,0},{20,4},{24,8},{28,12},{1,17},{... | collective-permute-start | bytes 1572872 | tf_op jit(solution)/shard_map/ppermute | solution.py:14
  128.9 23.6 %collective-permute-start.24 = (bf16[512,512]{1,0:T(8,128)(2,1)S(1)}, bf16[512,512]{1,0:T(8,128)(2,1)S(1)}, u32[]{:S(2)}, u32[]{:S(2)}) collective-permute-start(bf16[512,512]{1,0:T(8,128)(2,1)S(1)} %get-tuple-element.31), channel_id=1, source_target_pairs={{0,8},{4,12},{8,0},{12,4},{16,24},{20,28},{24,16},{28,20},{1,9},{5... | collective-permute-start | bytes 1572872 | tf_op jit(solution)/shard_map/ppermute | solution.py:14
  141.3 14.9 %collective-permute-start.27 = (bf16[512,512]{1,0:T(8,128)(2,1)S(1)}, bf16[512,512]{1,0:T(8,128)(2,1)S(1)}, u32[]{:S(2)}, u32[]{:S(2)}) collective-permute-start(bf16[512,512]{1,0:T(8,128)(2,1)S(1)} %get-tuple-element.34), channel_id=1, source_target_pairs={{0,16},{4,20},{8,24},{12,28},{16,0},{20,4},{24,8},{28,12},{1,17},{... | collective-permute-start | bytes 1572872 | tf_op jit(solution)/shard_map/ppermute | solution.py:14
  143.1 22.5 %collective-permute-start.26 = (bf16[512,512]{1,0:T(8,128)(2,1)S(1)}, bf16[512,512]{1,0:T(8,128)(2,1)S(1)}, u32[]{:S(2)}, u32[]{:S(2)}) collective-permute-start(bf16[512,512]{1,0:T(8,128)(2,1)S(1)} %get-tuple-element.35), channel_id=1, source_target_pairs={{0,16},{4,20},{8,24},{12,28},{16,0},{20,4},{24,8},{28,12},{1,17},{... | collective-permute-start | bytes 1572872 | tf_op jit(solution)/shard_map/ppermute | solution.py:14
  143.7 21.9 %collective-permute-start.29 = (bf16[512,512]{1,0:T(8,128)(2,1)S(1)}, bf16[512,512]{1,0:T(8,128)(2,1)S(1)}, u32[]{:S(2)}, u32[]{:S(2)}) collective-permute-start(bf16[512,512]{1,0:T(8,128)(2,1)S(1)} %get-tuple-element.36), channel_id=1, source_target_pairs={{0,8},{4,12},{8,0},{12,4},{16,24},{20,28},{24,16},{28,20},{1,9},{5... | collective-permute-start | bytes 1572872 | tf_op jit(solution)/shard_map/ppermute | solution.py:14

commit v3 on v2

--- a/solution.py
+++ b/solution.py
@@ -150,7 +150,7 @@
     local_state = jnp.einsum(
         "bhsd,bhse->bhde", key_heads, value_heads, preferred_element_type=jnp.float32
     )
-    state, arrived[1] = exclusive_scan(local_state, "ctx", False, arrived[1])
+    state, _ = exclusive_scan(local_state, "ctx", False)
     for step in range(2, groups):
         arrived[step] = gather_step(arrived[step - 1], "head", step)
     state_bf = state.astype(jnp.bfloat16)
@@ -182,9 +182,11 @@
     pair_sums = []
     for rank in range(groups):
         block = look_up([row[rank][2] for row in table], group)
+        if rank == groups - 1:
+            arrived, pair_sums, came_out = lax.optimization_barrier(
+                (arrived, pair_sums, came_out)
+            )
         grad = pick(arrived, rank, table, group)
-        if rank == groups - 1:
-            grad, pair_sums, came_out = lax.optimization_barrier((grad, pair_sums, came_out))
         columns = lax.dynamic_slice_in_dim(out_weight, block * width, width, 1)
         normed_grad = normed_grad + jnp.einsum(
             "btc,rc->btr", grad, columns, preferred_element_type=jnp.float32
@@ -207,15 +209,6 @@
         "bhtd,bhte->bhde", query_heads, attended_grad, preferred_element_type=jnp.float32
     )
     pair_sums = jnp.stack(pair_sums)
-    for step in range(2, groups - 1):
-        came_out = scatter_step(terms, came_out, "head", step)
-    grad_state, (pair_sums, came_out) = exclusive_scan(
-        local_grad_state, "ctx", True, (pair_sums, came_out)
-    )
-    came_out = scatter_step(terms, came_out, "head", groups - 1)
-    layer_output = (
-        terms[0] + came_out[0].astype(jnp.float32) + came_out[1].astype(jnp.float32)
-    ).astype(jnp.bfloat16)
     chip = lax.axis_index("ctx") // 2
     positions = [[[e[2] for e in row].index(g) for row in table] for g in range(groups)]
     blocks = {}
@@ -229,10 +222,21 @@
         ).astype(jnp.float32)
     bits = [1 << i for i in range(1, places.bit_length() - 1)]
     rows = normed_flat.shape[2] // 2
-    upper = halve({k: block[:rows] for k, block in blocks.items()}, "ctx", bits)
-    lower_rows = halve({k: block[rows:] for k, block in blocks.items()}, "ctx", bits[::-1])
+    upper = halve({k: block[:rows] for k, block in blocks.items()}, "ctx", bits[:1])
+    downer = halve({k: block[rows:] for k, block in blocks.items()}, "ctx", bits[::-1][:1])
+    for step in range(2, groups - 1):
+        came_out = scatter_step(terms, came_out, "head", step)
+    grad_state, (upper, downer, came_out) = exclusive_scan(
+        local_grad_state, "ctx", True, (upper, downer, came_out)
+    )
+    upper = halve(upper, "ctx", bits[1:])
+    downer = halve(downer, "ctx", bits[::-1][1:])
     token_factor = (2 * length * places) ** (-0.5)
-    weight_grad = jnp.concatenate([upper[0], lower_rows[0]], axis=0) * token_factor
+    weight_grad = jnp.concatenate([upper[0], downer[0]], axis=0) * token_factor
+    came_out = scatter_step(terms, came_out, "head", groups - 1)
+    layer_output = (
+        terms[0] + came_out[0].astype(jnp.float32) + came_out[1].astype(jnp.float32)
+    ).astype(jnp.bfloat16)
     grad_state_bf = grad_state.astype(jnp.bfloat16)
     raw_grad = (
         jnp.einsum(

time: 168 us -> 161 us (0.958)
  starting transfers between devices: 40.9 us -> 35.2 us
  waiting for transfers between devices: 83.9 us -> 81.1 us
    ppermute x18, waiting for transfers between devices: 47.5 us -> 38.6 us  [swap(): return lax.ppermute(array, axis, [(i, i ^ bit) for i in range(count)])]
    ppermute x6, starting transfers between devices: 18.2 us -> 13.6 us  [right_of(): return lax.ppermute(array, axis, [(i, i + 1) for i in range(first, last)])]
    ppermute x6, waiting for transfers between devices: 4.71 us -> 8.93 us  [right_of(): return lax.ppermute(array, axis, [(i, i + 1) for i in range(first, last)])]
    ppermute x6, waiting for transfers between devices: 31.7 us -> 33.5 us  [left_of(): return lax.ppermute(array, axis, [(i, i - 1) for i in range(first, last)])]
  transfers between devices with their start and end apart: 30 -> 30, of which waited for: 13 -> 18; matrix products, arithmetic and copies ran while one was open for 17% -> 19% of each run, Pallas kernels for 0% -> 0%
where the time goes in v3:
time: 161 us; the launch traced here: 160 us
  waiting for transfers between devices  81.1 us (50%)
  starting transfers between devices  35.2 us (22%)
  matrix products  24.6 us (15%)
  other arithmetic  12 us (7%)
  local copies, waits for them, and re-layouts  5.67 us (4%)
    ppermute x18, waiting for transfers between devices, swap(): return lax.ppermute(array, axis, [(i, i ^ bit) for i in range(count)])  38.6 us
    ppermute x6, waiting for transfers between devices, left_of(): return lax.ppermute(array, axis, [(i, i - 1) for i in range(first, last)])  33.5 us
    ppermute x18, starting transfers between devices, swap(): return lax.ppermute(array, axis, [(i, i ^ bit) for i in range(count)])  14.9 us
    ppermute x6, starting transfers between devices, right_of(): return lax.ppermute(array, axis, [(i, i + 1) for i in range(first, last)])  13.6 us
    ppermute x6, waiting for transfers between devices, right_of(): return lax.ppermute(array, axis, [(i, i + 1) for i in range(first, last)])  8.93 us
    ppermute x6, starting transfers between devices, left_of(): return lax.ppermute(array, axis, [(i, i - 1) for i in range(first, last)])  6.75 us
    dot_general x8, matrix products, shards(): jnp.einsum('btr,btc->rc', normed_flat, lax.dynamic_slice_in_dim(grad, (2...  5.96 us
    dot_general x4, matrix products, shards(): jnp.einsum('btc,rc->btr', grad, columns, preferred_element_type=jnp.float32)  5.77 us
  transfers between devices with their start and end apart: 30, of which 18 were waited for; matrix products, arithmetic and copies ran while one was open for 19% of the time, Pallas kernels for 0%

profile of v3, /device:TPU:0, one launch (start us, length us, event | category | flops | bytes accessed | tf_op | source)
XLA Modules:
  0.0 160.3 jit_solution(3710345912407609049)
XLA Ops:
  0.6 1.1 copy-done
  1.8 2.6 %fusion.125 = (bf16[2,8,128,128]{3,2,1,0:T(8,128)(2,1)S(1)}, f32[2,8,128,128]{3,2,1,0:T(8,128)}) fusion(bf16[2,192,1024]{2,1,0:T(8,128)(2,1)S(1)} %copy-done, bf16[2,192,1024]{2,1,0:T(8,128)(2,1)} %param.6), kind=kOutput, calls=%fused_computation.189 | convolution fusion | flops 100925440 | bytes 3145728 | tf_op jit(solution)/shard_map/bhsd,bhse->bhde/dot_general | solution.py:150
  4.8 1.5 collective-permute-done
  7.5 2.9 %collective-permute-start.1 = (bf16[8,128,128]{2,1,0:T(8,128)(2,1)S(1)}, bf16[8,128,128]{2,1,0:T(8,128)(2,1)S(1)}, u32[]{:S(2)}, u32[]{:S(2)}) collective-permute-start(bf16[8,128,128]{2,1,0:T(8,128)(2,1)S(1)} %fusion.93), channel_id=1, source_target_pairs={{0,8},{4,12},{8,0},{12,4},{16,24},{20,28},{24,16},{28,20},{1,9},{5... | collective-permute-start | bytes 786440 | tf_op jit(solution)/shard_map/ppermute | solution.py:14
  10.3 4.4 %collective-permute-start.4 = (bf16[2,192,1024]{2,1,0:T(8,128)(2,1)}, bf16[2,192,1024]{2,1,0:T(8,128)(2,1)}, u32[]{:S(2)}, u32[]{:S(2)}) collective-permute-start(bf16[2,192,1024]{2,1,0:T(8,128)(2,1)} %param.9), channel_id=1, source_target_pairs={{0,1},{1,2},{2,3},{4,5},{5,6},{6,7},{8,9},{9,10},{10,11},{12,13},{... | collective-permute-start | bytes 2359304 | tf_op jit(solution)/shard_map/ppermute | solution.py:42
  14.7 1.3 collective-permute-start.5
  16.9 1.3 fusion.67
  18.2 1.8 %collective-permute-start.2 = (bf16[8,128,128]{2,1,0:T(8,128)(2,1)S(1)}, bf16[8,128,128]{2,1,0:T(8,128)(2,1)S(1)}, u32[]{:S(2)}, u32[]{:S(2)}) collective-permute-start(bf16[8,128,128]{2,1,0:T(8,128)(2,1)S(1)} %fusion.67), channel_id=1, source_target_pairs={{0,16},{4,20},{8,24},{12,28},{16,0},{20,4},{24,8},{28,12},{1,17},{... | collective-permute-start | bytes 786440 | tf_op jit(solution)/shard_map/ppermute | solution.py:14
  20.7 5.4 %collective-permute-done.2 = bf16[8,128,128]{2,1,0:T(8,128)(2,1)S(1)} collective-permute-done((bf16[8,128,128]{2,1,0:T(8,128)(2,1)S(1)}, bf16[8,128,128]{2,1,0:T(8,128)(2,1)S(1)}, u32[]{:S(2)}, u32[]{:S(2)}) %collective-permute-start.2) | collective-permute-done | bytes 262176 | tf_op jit(solution)/shard_map/ppermute | solution.py:14
  26.3 2.7 %fusion.14 = f32[1024,2,192]{0,2,1:T(8,128)S(1)} fusion(bf16[2,192,1024]{2,1,0:T(8,128)(2,1)S(1)} %copy-done.5, bf16[1024,4096]{1,0:T(8,128)(2,1)} %param.8, s32[]{:T(128)S(6)} %select_n.387), kind=kOutput, calls=%fused_computation.27 | convolution fusion | flops 805306368 | bytes 4456452 | tf_op jit(solution)/shard_map/btc,rc->btr/dot_general | solution.py:191
  29.0 1.9 %collective-permute-done.4 = bf16[2,192,1024]{2,1,0:T(8,128)(2,1)} collective-permute-done((bf16[2,192,1024]{2,1,0:T(8,128)(2,1)}, bf16[2,192,1024]{2,1,0:T(8,128)(2,1)}, u32[]{:S(2)}, u32[]{:S(2)}) %collective-permute-start.4) | collective-permute-done | bytes 786464 | tf_op jit(solution)/shard_map/ppermute | solution.py:42
  31.6 4.3 %collective-permute-done.5 = bf16[2,192,1024]{2,1,0:T(8,128)(2,1)} collective-permute-done((bf16[2,192,1024]{2,1,0:T(8,128)(2,1)}, bf16[2,192,1024]{2,1,0:T(8,128)(2,1)}, u32[]{:S(2)}, u32[]{:S(2)}) %collective-permute-start.5) | collective-permute-done | bytes 786464 | tf_op jit(solution)/shard_map/ppermute | solution.py:46
  35.9 1.3 collective-permute-start.7
  40.8 1.0 fusion.127
  42.5 1.0 fusion.126
  43.5 4.6 %collective-permute-start.13 = (bf16[2,192,1024]{2,1,0:T(8,128)(2,1)S(1)}, bf16[2,192,1024]{2,1,0:T(8,128)(2,1)S(1)}, u32[]{:S(2)}, u32[]{:S(2)}) collective-permute-start(bf16[2,192,1024]{2,1,0:T(8,128)(2,1)S(1)} %get-tuple-element.60), channel_id=1, source_target_pairs={{0,1},{4,5},{8,9},{12,13},{16,17},{20,21},{24,25},{28,29}} | collective-permute-start | bytes 2359304 | tf_op jit(solution)/shard_map/ppermute | solution.py:42
  48.1 1.0 fusion
  49.1 7.0 %collective-permute-done.7 = bf16[2,192,1024]{2,1,0:T(8,128)(2,1)S(1)} collective-permute-done((bf16[2,192,1024]{2,1,0:T(8,128)(2,1)}, bf16[2,192,1024]{2,1,0:T(8,128)(2,1)S(1)}, u32[]{:S(2)}, u32[]{:S(2)}) %collective-permute-start.7) | collective-permute-done | bytes 786464 | tf_op jit(solution)/shard_map/ppermute | solution.py:46
  56.1 1.4 broadcast_select_fusion
  58.3 1.0 fusion.18
  60.6 1.0 fusion.12
  61.7 1.0 fusion.10
  63.4 1.5 collective-permute-start.9
  67.2 17.6 %collective-permute-done.9 = bf16[2,192,1024]{2,1,0:T(8,128)(2,1)S(1)} collective-permute-done((bf16[2,192,1024]{2,1,0:T(8,128)(2,1)S(1)}, bf16[2,192,1024]{2,1,0:T(8,128)(2,1)S(1)}, u32[]{:S(2)}, u32[]{:S(2)}) %collective-permute-start.9) | collective-permute-done | bytes 786464 | tf_op jit(solution)/shard_map/ppermute | solution.py:46
  85.8 1.1 fusion.37
  86.9 1.1 fusion.32
  88.0 1.0 fusion.28
  92.7 1.1 collective-permute-done.15
  96.1 1.6 collective-permute-start.20
  98.2 1.5 collective-permute-start.23
  100.4 2.8 %collective-permute-done.16 = bf16[8,128,128]{2,1,0:T(8,128)(2,1)S(1)} collective-permute-done((bf16[8,128,128]{2,1,0:T(8,128)(2,1)S(1)}, bf16[8,128,128]{2,1,0:T(8,128)(2,1)S(1)}, u32[]{:S(2)}, u32[]{:S(2)}) %collective-permute-start.16) | collective-permute-done | bytes 262176 | tf_op jit(solution)/shard_map/ppermute | solution.py:14
  103.3 1.6 collective-permute-start.17
  105.8 1.1 copy.151
  106.9 5.6 %collective-permute-done.17 = bf16[8,128,128]{2,1,0:T(8,128)(2,1)S(1)} collective-permute-done((bf16[8,128,128]{2,1,0:T(8,128)(2,1)S(1)}, bf16[8,128,128]{2,1,0:T(8,128)(2,1)S(1)}, u32[]{:S(2)}, u32[]{:S(2)}) %collective-permute-start.17) | collective-permute-done | bytes 262176 | tf_op jit(solution)/shard_map/ppermute | solution.py:14
  113.1 1.3 collective-permute-done.20
  114.4 1.5 collective-permute-start.21
  116.3 7.5 %collective-permute-done.22 = bf16[512,512]{1,0:T(8,128)(2,1)S(1)} collective-permute-done((bf16[512,512]{1,0:T(8,128)(2,1)S(1)}, bf16[512,512]{1,0:T(8,128)(2,1)S(1)}, u32[]{:S(2)}, u32[]{:S(2)}) %collective-permute-start.22) | collective-permute-done | bytes 524320 | tf_op jit(solution)/shard_map/ppermute | solution.py:14
  124.8 7.7 %collective-permute-done.21 = bf16[512,512]{1,0:T(8,128)(2,1)S(1)} collective-permute-done((bf16[512,512]{1,0:T(8,128)(2,1)S(1)}, bf16[512,512]{1,0:T(8,128)(2,1)S(1)}, u32[]{:S(2)}, u32[]{:S(2)}) %collective-permute-start.21) | collective-permute-done | bytes 524320 | tf_op jit(solution)/shard_map/ppermute | solution.py:14
  132.9 1.6 collective-permute-start.28
  135.3 1.7 %collective-permute-start.25 = (bf16[2,192,1024]{2,1,0:T(8,128)(2,1)S(1)}, bf16[2,192,1024]{2,1,0:T(8,128)(2,1)S(1)}, u32[]{:S(2)}, u32[]{:S(2)}) collective-permute-start(bf16[2,192,1024]{2,1,0:T(8,128)(2,1)S(1)} %add_convert_fusion.3), channel_id=1, source_target_pairs={{0,1},{1,2},{2,3},{4,5},{5,6},{6,7},{8,9},{9,10},{10,11},{12,13},{... | collective-permute-start | bytes 2359304 | tf_op jit(solution)/shard_map/ppermute | solution.py:42
  137.3 1.3 collective-permute-start.26
  139.6 1.4 copy_bitcast_fusion
  141.0 3.3 %collective-permute-done.28 = bf16[512,512]{1,0:T(8,128)(2,1)S(1)} collective-permute-done((bf16[512,512]{1,0:T(8,128)(2,1)S(1)}, bf16[512,512]{1,0:T(8,128)(2,1)S(1)}, u32[]{:S(2)}, u32[]{:S(2)}) %collective-permute-start.28) | collective-permute-done | bytes 524320 | tf_op jit(solution)/shard_map/ppermute | solution.py:14
  144.5 1.1 collective-permute-done.29
  145.8 1.6 maximum_multiply_fusion
  147.4 7.0 %collective-permute-done.25 = bf16[2,192,1024]{2,1,0:T(8,128)(2,1)S(1)} collective-permute-done((bf16[2,192,1024]{2,1,0:T(8,128)(2,1)S(1)}, bf16[2,192,1024]{2,1,0:T(8,128)(2,1)S(1)}, u32[]{:S(2)}, u32[]{:S(2)}) %collective-permute-start.25) | collective-permute-done | bytes 786464 | tf_op jit(solution)/shard_map/ppermute | solution.py:42
  154.3 4.6 %collective-permute-done.26 = bf16[2,192,1024]{2,1,0:T(8,128)(2,1)S(1)} collective-permute-done((bf16[2,192,1024]{2,1,0:T(8,128)(2,1)S(1)}, bf16[2,192,1024]{2,1,0:T(8,128)(2,1)S(1)}, u32[]{:S(2)}, u32[]{:S(2)}) %collective-permute-start.26) | collective-permute-done | bytes 786464 | tf_op jit(solution)/shard_map/ppermute | solution.py:46
  159.0 1.3 add_convert_fusion.1
  (89 shorter events, 27.0 us)
Async XLA Ops:
  0.6 1.1 copy-start
  4.4 2.0 %collective-permute-start = (bf16[2,8,128,128]{3,2,1,0:T(8,128)(2,1)S(1)}, bf16[2,8,128,128]{3,2,1,0:T(8,128)(2,1)S(1)}, u32[]{:S(2)}, u32[]{:S(2)}) collective-permute-start(bf16[2,8,128,128]{3,2,1,0:T(8,128)(2,1)S(1)} %get-tuple-element.56), channel_id=1, source_target_pairs={{0,4},{4,0},{8,12},{12,8},{16,20},{20,16},{24,28},{28,24},{1,5},{5... | collective-permute-start | bytes 1572872 | tf_op jit(solution)/shard_map/ppermute | solution.py:14
  4.8 1.7 %copy-start.3 = (f32[2,8,128,128]{3,2,1,0:T(8,128)S(1)}, f32[2,8,128,128]{3,2,1,0:T(8,128)}, u32[]{:S(2)}) copy-start(f32[2,8,128,128]{3,2,1,0:T(8,128)} %get-tuple-element.57) | copy-start | bytes 3145732
  6.5 1.0 copy-start.4
  6.5 13.6 %copy-start.1 = (bf16[2,192,1024]{2,1,0:T(8,128)(2,1)S(1)}, bf16[2,192,1024]{2,1,0:T(8,128)(2,1)}, u32[]{:S(2)}) copy-start(bf16[2,192,1024]{2,1,0:T(8,128)(2,1)} %param.6) | copy-start | bytes 2359300
  6.5 13.6 %copy-start.2 = (bf16[2,192,1024]{2,1,0:T(8,128)(2,1)S(1)}, bf16[2,192,1024]{2,1,0:T(8,128)(2,1)}, u32[]{:S(2)}) copy-start(bf16[2,192,1024]{2,1,0:T(8,128)(2,1)} %param.5) | copy-start | bytes 2359300
  7.5 9.5 %collective-permute-start.1 = (bf16[8,128,128]{2,1,0:T(8,128)(2,1)S(1)}, bf16[8,128,128]{2,1,0:T(8,128)(2,1)S(1)}, u32[]{:S(2)}, u32[]{:S(2)}) collective-permute-start(bf16[8,128,128]{2,1,0:T(8,128)(2,1)S(1)} %fusion.93), channel_id=1, source_target_pairs={{0,8},{4,12},{8,0},{12,4},{16,24},{20,28},{24,16},{28,20},{1,9},{5... | collective-permute-start | bytes 786440 | tf_op jit(solution)/shard_map/ppermute | solution.py:14
  10.3 20.6 %collective-permute-start.4 = (bf16[2,192,1024]{2,1,0:T(8,128)(2,1)}, bf16[2,192,1024]{2,1,0:T(8,128)(2,1)}, u32[]{:S(2)}, u32[]{:S(2)}) collective-permute-start(bf16[2,192,1024]{2,1,0:T(8,128)(2,1)} %param.9), channel_id=1, source_target_pairs={{0,1},{1,2},{2,3},{4,5},{5,6},{6,7},{8,9},{9,10},{10,11},{12,13},{... | collective-permute-start | bytes 2359304 | tf_op jit(solution)/shard_map/ppermute | solution.py:42
  14.7 21.2 %collective-permute-start.5 = (bf16[2,192,1024]{2,1,0:T(8,128)(2,1)}, bf16[2,192,1024]{2,1,0:T(8,128)(2,1)}, u32[]{:S(2)}, u32[]{:S(2)}) collective-permute-start(bf16[2,192,1024]{2,1,0:T(8,128)(2,1)} %param.9), channel_id=1, source_target_pairs={{1,0},{2,1},{3,2},{5,4},{6,5},{7,6},{9,8},{10,9},{11,10},{13,12},{... | collective-permute-start | bytes 2359304 | tf_op jit(solution)/shard_map/ppermute | solution.py:46
  18.2 8.1 %copy-start.5 = (bf16[2,192,1024]{2,1,0:T(8,128)(2,1)S(1)}, bf16[2,192,1024]{2,1,0:T(8,128)(2,1)}, u32[]{:S(2)}) copy-start(bf16[2,192,1024]{2,1,0:T(8,128)(2,1)} %param.9) | copy-start | bytes 2359300
  18.2 7.9 %collective-permute-start.2 = (bf16[8,128,128]{2,1,0:T(8,128)(2,1)S(1)}, bf16[8,128,128]{2,1,0:T(8,128)(2,1)S(1)}, u32[]{:S(2)}, u32[]{:S(2)}) collective-permute-start(bf16[8,128,128]{2,1,0:T(8,128)(2,1)S(1)} %fusion.67), channel_id=1, source_target_pairs={{0,16},{4,20},{8,24},{12,28},{16,0},{20,4},{24,8},{28,12},{1,17},{... | collective-permute-start | bytes 786440 | tf_op jit(solution)/shard_map/ppermute | solution.py:14
  26.2 11.0 %collective-permute-start.3 = (bf16[8,128,128]{2,1,0:T(8,128)(2,1)S(1)}, bf16[8,128,128]{2,1,0:T(8,128)(2,1)S(1)}, u32[]{:S(2)}, u32[]{:S(2)}) collective-permute-start(bf16[8,128,128]{2,1,0:T(8,128)(2,1)S(1)} %fusion.66), channel_id=1, source_target_pairs={{0,4},{4,0},{8,12},{12,8},{16,20},{20,16},{24,28},{28,24},{1,5},{5... | collective-permute-start | bytes 786440 | tf_op jit(solution)/shard_map/ppermute | solution.py:14
  30.9 18.2 %collective-permute-start.6 = (bf16[2,192,1024]{2,1,0:T(8,128)(2,1)}, bf16[2,192,1024]{2,1,0:T(8,128)(2,1)S(1)}, u32[]{:S(2)}, u32[]{:S(2)}) collective-permute-start(bf16[2,192,1024]{2,1,0:T(8,128)(2,1)} %collective-permute-done.4), channel_id=1, source_target_pairs={{1,2},{2,3},{5,6},{6,7},{9,10},{10,11},{13,14},{14,15},{17,18},{18... | collective-permute-start | bytes 2359304 | tf_op jit(solution)/shard_map/ppermute | solution.py:42
  35.9 20.2 %collective-permute-start.7 = (bf16[2,192,1024]{2,1,0:T(8,128)(2,1)}, bf16[2,192,1024]{2,1,0:T(8,128)(2,1)S(1)}, u32[]{:S(2)}, u32[]{:S(2)}) collective-permute-start(bf16[2,192,1024]{2,1,0:T(8,128)(2,1)} %collective-permute-done.5), channel_id=1, source_target_pairs={{1,0},{2,1},{5,4},{6,5},{9,8},{10,9},{13,12},{14,13},{17,16},{18,1... | collective-permute-start | bytes 2359304 | tf_op jit(solution)/shard_map/ppermute | solution.py:46
  37.3 2.6 %slice-start = ((s8[8388608]{0:T(1024)(128)(4,1)}), s8[4194304]{0:T(1024)(128)(4,1)S(1)}, s32[]{:S(2)}) async-start(s8[8388608]{0:T(1024)(128)(4,1)} %bitcast.333), calls=%async_computation | async-start | bytes 8388608
  37.7 3.2 %slice-start.1 = ((s8[8388608]{0:T(1024)(128)(4,1)}), s8[4194304]{0:T(1024)(128)(4,1)S(1)}, s32[]{:S(2)}) async-start(s8[8388608]{0:T(1024)(128)(4,1)} %bitcast.333), calls=%async_computation.1 | async-start | bytes 8388608
  39.8 22.9 %collective-permute-start.10 = (bf16[1024,512]{1,0:T(8,128)(2,1)S(1)}, bf16[1024,512]{1,0:T(8,128)(2,1)S(1)}, u32[]{:S(2)}, u32[]{:S(2)}) collective-permute-start(bf16[1024,512]{1,0:T(8,128)(2,1)S(1)} %bitcast_convert_fusion.3), channel_id=1, source_target_pairs={{0,4},{4,0},{8,12},{12,8},{16,20},{20,16},{24,28},{28,24},{1,5},{5... | collective-permute-start | bytes 3145736 | tf_op jit(solution)/shard_map/ppermute | solution.py:14
  41.8 25.3 %collective-permute-start.14 = (bf16[2,192,1024]{2,1,0:T(8,128)(2,1)S(1)}, bf16[2,192,1024]{2,1,0:T(8,128)(2,1)S(1)}, u32[]{:S(2)}, u32[]{:S(2)}) collective-permute-start(bf16[2,192,1024]{2,1,0:T(8,128)(2,1)S(1)} %get-tuple-element.62), channel_id=1, source_target_pairs={{3,2},{7,6},{11,10},{15,14},{19,18},{23,22},{27,26},{31,30}} | collective-permute-start | bytes 2359304 | tf_op jit(solution)/shard_map/ppermute | solution.py:46
  43.5 23.6 %collective-permute-start.13 = (bf16[2,192,1024]{2,1,0:T(8,128)(2,1)S(1)}, bf16[2,192,1024]{2,1,0:T(8,128)(2,1)S(1)}, u32[]{:S(2)}, u32[]{:S(2)}) collective-permute-start(bf16[2,192,1024]{2,1,0:T(8,128)(2,1)S(1)} %get-tuple-element.60), channel_id=1, source_target_pairs={{0,1},{4,5},{8,9},{12,13},{16,17},{20,21},{24,25},{28,29}} | collective-permute-start | bytes 2359304 | tf_op jit(solution)/shard_map/ppermute | solution.py:42
  58.3 5.2 %collective-permute-start.12 = (bf16[1024,512]{1,0:T(8,128)(2,1)S(1)}, bf16[1024,512]{1,0:T(8,128)(2,1)S(1)}, u32[]{:S(2)}, u32[]{:S(2)}) collective-permute-start(bf16[1024,512]{1,0:T(8,128)(2,1)S(1)} %bitcast_convert_fusion.1), channel_id=1, source_target_pairs={{0,4},{4,0},{8,12},{12,8},{16,20},{20,16},{24,28},{28,24},{1,5},{5... | collective-permute-start | bytes 3145736 | tf_op jit(solution)/shard_map/ppermute | solution.py:14
  60.1 6.3 %collective-permute-start.11 = (bf16[1024,512]{1,0:T(8,128)(2,1)S(1)}, bf16[1024,512]{1,0:T(8,128)(2,1)S(1)}, u32[]{:S(2)}, u32[]{:S(2)}) collective-permute-start(bf16[1024,512]{1,0:T(8,128)(2,1)S(1)} %bitcast_convert_fusion.2), channel_id=1, source_target_pairs={{0,4},{4,0},{8,12},{12,8},{16,20},{20,16},{24,28},{28,24},{1,5},{5... | collective-permute-start | bytes 3145736 | tf_op jit(solution)/shard_map/ppermute | solution.py:14
  62.7 4.5 %collective-permute-start.8 = (bf16[2,192,1024]{2,1,0:T(8,128)(2,1)S(1)}, bf16[2,192,1024]{2,1,0:T(8,128)(2,1)S(1)}, u32[]{:S(2)}, u32[]{:S(2)}) collective-permute-start(bf16[2,192,1024]{2,1,0:T(8,128)(2,1)S(1)} %collective-permute-done.6), channel_id=1, source_target_pairs={{2,3},{6,7},{10,11},{14,15},{18,19},{22,23},{26,27},{30,31}} | collective-permute-start | bytes 2359304 | tf_op jit(solution)/shard_map/ppermute | solution.py:42
  63.4 21.4 %collective-permute-start.9 = (bf16[2,192,1024]{2,1,0:T(8,128)(2,1)S(1)}, bf16[2,192,1024]{2,1,0:T(8,128)(2,1)S(1)}, u32[]{:S(2)}, u32[]{:S(2)}) collective-permute-start(bf16[2,192,1024]{2,1,0:T(8,128)(2,1)S(1)} %collective-permute-done.7), channel_id=1, source_target_pairs={{1,0},{5,4},{9,8},{13,12},{17,16},{21,20},{25,24},{29,28}} | collective-permute-start | bytes 2359304 | tf_op jit(solution)/shard_map/ppermute | solution.py:46
  90.3 4.3 %collective-permute-start.18 = (bf16[1024,512]{1,0:T(8,128)(2,1)S(1)}, bf16[1024,512]{1,0:T(8,128)(2,1)S(1)}, u32[]{:S(2)}, u32[]{:S(2)}) collective-permute-start(bf16[1024,512]{1,0:T(8,128)(2,1)S(1)} %bitcast_convert_fusion), channel_id=1, source_target_pairs={{0,4},{4,0},{8,12},{12,8},{16,20},{20,16},{24,28},{28,24},{1,5},{5... | collective-permute-start | bytes 3145736 | tf_op jit(solution)/shard_map/ppermute | solution.py:14
  90.4 3.4 %collective-permute-start.15 = (bf16[2,8,128,128]{3,2,1,0:T(8,128)(2,1)S(1)}, bf16[2,8,128,128]{3,2,1,0:T(8,128)(2,1)S(1)}, u32[]{:S(2)}, u32[]{:S(2)}) collective-permute-start(bf16[2,8,128,128]{3,2,1,0:T(8,128)(2,1)S(1)} %get-tuple-element.64), channel_id=1, source_target_pairs={{0,4},{4,0},{8,12},{12,8},{16,20},{20,16},{24,28},{28,24},{1,5},{5... | collective-permute-start | bytes 1572872 | tf_op jit(solution)/shard_map/ppermute | solution.py:14
  94.0 9.2 %collective-permute-start.16 = (bf16[8,128,128]{2,1,0:T(8,128)(2,1)S(1)}, bf16[8,128,128]{2,1,0:T(8,128)(2,1)S(1)}, u32[]{:S(2)}, u32[]{:S(2)}) collective-permute-start(bf16[8,128,128]{2,1,0:T(8,128)(2,1)S(1)} %fusion.94), channel_id=1, source_target_pairs={{0,8},{4,12},{8,0},{12,4},{16,24},{20,28},{24,16},{28,20},{1,9},{5... | collective-permute-start | bytes 786440 | tf_op jit(solution)/shard_map/ppermute | solution.py:14
  96.1 18.3 %collective-permute-start.20 = (bf16[512,512]{1,0:T(8,128)(2,1)S(1)}, bf16[512,512]{1,0:T(8,128)(2,1)S(1)}, u32[]{:S(2)}, u32[]{:S(2)}) collective-permute-start(bf16[512,512]{1,0:T(8,128)(2,1)S(1)} %get-tuple-element.40), channel_id=1, source_target_pairs={{0,8},{4,12},{8,0},{12,4},{16,24},{20,28},{24,16},{28,20},{1,9},{5... | collective-permute-start | bytes 1572872 | tf_op jit(solution)/shard_map/ppermute | solution.py:14
  98.2 34.7 %collective-permute-start.23 = (bf16[2,192,1024]{2,1,0:T(8,128)(2,1)S(1)}, bf16[2,192,1024]{2,1,0:T(8,128)(2,1)S(1)}, u32[]{:S(2)}, u32[]{:S(2)}) collective-permute-start(bf16[2,192,1024]{2,1,0:T(8,128)(2,1)S(1)} %get-tuple-element.46), channel_id=1, source_target_pairs={{0,1},{1,2},{4,5},{5,6},{8,9},{9,10},{12,13},{13,14},{16,17},{17,1... | collective-permute-start | bytes 2359304 | tf_op jit(solution)/shard_map/ppermute | solution.py:42
  99.7 33.2 %collective-permute-start.24 = (bf16[2,192,1024]{2,1,0:T(8,128)(2,1)S(1)}, bf16[2,192,1024]{2,1,0:T(8,128)(2,1)S(1)}, u32[]{:S(2)}, u32[]{:S(2)}) collective-permute-start(bf16[2,192,1024]{2,1,0:T(8,128)(2,1)S(1)} %get-tuple-element.45), channel_id=1, source_target_pairs={{2,1},{3,2},{6,5},{7,6},{10,9},{11,10},{14,13},{15,14},{18,17},{19... | collective-permute-start | bytes 2359304 | tf_op jit(solution)/shard_map/ppermute | solution.py:46
  103.3 9.3 %collective-permute-start.17 = (bf16[8,128,128]{2,1,0:T(8,128)(2,1)S(1)}, bf16[8,128,128]{2,1,0:T(8,128)(2,1)S(1)}, u32[]{:S(2)}, u32[]{:S(2)}) collective-permute-start(bf16[8,128,128]{2,1,0:T(8,128)(2,1)S(1)} %fusion.70), channel_id=1, source_target_pairs={{0,16},{4,20},{8,24},{12,28},{16,0},{20,4},{24,8},{28,12},{1,17},{... | collective-permute-start | bytes 786440 | tf_op jit(solution)/shard_map/ppermute | solution.py:14
  104.8 19.0 %collective-permute-start.22 = (bf16[512,512]{1,0:T(8,128)(2,1)S(1)}, bf16[512,512]{1,0:T(8,128)(2,1)S(1)}, u32[]{:S(2)}, u32[]{:S(2)}) collective-permute-start(bf16[512,512]{1,0:T(8,128)(2,1)S(1)} %get-tuple-element.39), channel_id=1, source_target_pairs={{0,16},{4,20},{8,24},{12,28},{16,0},{20,4},{24,8},{28,12},{1,17},{... | collective-permute-start | bytes 1572872 | tf_op jit(solution)/shard_map/ppermute | solution.py:14
  112.6 12.3 %collective-permute-start.19 = (bf16[512,512]{1,0:T(8,128)(2,1)S(1)}, bf16[512,512]{1,0:T(8,128)(2,1)S(1)}, u32[]{:S(2)}, u32[]{:S(2)}) collective-permute-start(bf16[512,512]{1,0:T(8,128)(2,1)S(1)} %get-tuple-element.41), channel_id=1, source_target_pairs={{0,8},{4,12},{8,0},{12,4},{16,24},{20,28},{24,16},{28,20},{1,9},{5... | collective-permute-start | bytes 1572872 | tf_op jit(solution)/shard_map/ppermute | solution.py:14
  114.4 18.1 %collective-permute-start.21 = (bf16[512,512]{1,0:T(8,128)(2,1)S(1)}, bf16[512,512]{1,0:T(8,128)(2,1)S(1)}, u32[]{:S(2)}, u32[]{:S(2)}) collective-permute-start(bf16[512,512]{1,0:T(8,128)(2,1)S(1)} %get-tuple-element.42), channel_id=1, source_target_pairs={{0,16},{4,20},{8,24},{12,28},{16,0},{20,4},{24,8},{28,12},{1,17},{... | collective-permute-start | bytes 1572872 | tf_op jit(solution)/shard_map/ppermute | solution.py:14
  132.9 11.5 %collective-permute-start.28 = (bf16[512,512]{1,0:T(8,128)(2,1)S(1)}, bf16[512,512]{1,0:T(8,128)(2,1)S(1)}, u32[]{:S(2)}, u32[]{:S(2)}) collective-permute-start(bf16[512,512]{1,0:T(8,128)(2,1)S(1)} %get-tuple-element.34), channel_id=1, source_target_pairs={{0,16},{4,20},{8,24},{12,28},{16,0},{20,4},{24,8},{28,12},{1,17},{... | collective-permute-start | bytes 1572872 | tf_op jit(solution)/shard_map/ppermute | solution.py:14
  134.5 11.1 %collective-permute-start.29 = (bf16[512,512]{1,0:T(8,128)(2,1)S(1)}, bf16[512,512]{1,0:T(8,128)(2,1)S(1)}, u32[]{:S(2)}, u32[]{:S(2)}) collective-permute-start(bf16[512,512]{1,0:T(8,128)(2,1)S(1)} %get-tuple-element.36), channel_id=1, source_target_pairs={{0,8},{4,12},{8,0},{12,4},{16,24},{20,28},{24,16},{28,20},{1,9},{5... | collective-permute-start | bytes 1572872 | tf_op jit(solution)/shard_map/ppermute | solution.py:14
  135.0 3.6 %collective-permute-start.27 = (bf16[8,128,128]{2,1,0:T(8,128)(2,1)S(1)}, bf16[8,128,128]{2,1,0:T(8,128)(2,1)S(1)}, u32[]{:S(2)}, u32[]{:S(2)}) collective-permute-start(bf16[8,128,128]{2,1,0:T(8,128)(2,1)S(1)} %fusion.69), channel_id=1, source_target_pairs={{0,4},{4,0},{8,12},{12,8},{16,20},{20,16},{24,28},{28,24},{1,5},{5... | collective-permute-start | bytes 786440 | tf_op jit(solution)/shard_map/ppermute | solution.py:14
  135.3 19.0 %collective-permute-start.25 = (bf16[2,192,1024]{2,1,0:T(8,128)(2,1)S(1)}, bf16[2,192,1024]{2,1,0:T(8,128)(2,1)S(1)}, u32[]{:S(2)}, u32[]{:S(2)}) collective-permute-start(bf16[2,192,1024]{2,1,0:T(8,128)(2,1)S(1)} %add_convert_fusion.3), channel_id=1, source_target_pairs={{0,1},{1,2},{2,3},{4,5},{5,6},{6,7},{8,9},{9,10},{10,11},{12,13},{... | collective-permute-start | bytes 2359304 | tf_op jit(solution)/shard_map/ppermute | solution.py:42
  137.3 21.7 %collective-permute-start.26 = (bf16[2,192,1024]{2,1,0:T(8,128)(2,1)S(1)}, bf16[2,192,1024]{2,1,0:T(8,128)(2,1)S(1)}, u32[]{:S(2)}, u32[]{:S(2)}) collective-permute-start(bf16[2,192,1024]{2,1,0:T(8,128)(2,1)S(1)} %add_convert_fusion.2), channel_id=1, source_target_pairs={{1,0},{2,1},{3,2},{5,4},{6,5},{7,6},{9,8},{10,9},{11,10},{13,12},{... | collective-permute-start | bytes 2359304 | tf_op jit(solution)/shard_map/ppermute | solution.py:46

commit v4 on v3

--- a/solution.py
+++ b/solution.py
@@ -224,16 +224,16 @@
     rows = normed_flat.shape[2] // 2
     upper = halve({k: block[:rows] for k, block in blocks.items()}, "ctx", bits[:1])
     downer = halve({k: block[rows:] for k, block in blocks.items()}, "ctx", bits[::-1][:1])
-    for step in range(2, groups - 1):
+    for step in range(2, groups):
         came_out = scatter_step(terms, came_out, "head", step)
-    grad_state, (upper, downer, came_out) = exclusive_scan(
-        local_grad_state, "ctx", True, (upper, downer, came_out)
-    )
+    grad_state, (upper, downer) = exclusive_scan(
+        local_grad_state, "ctx", True, (upper, downer)
+    )
+    grad_state, came_out = lax.optimization_barrier((grad_state, came_out))
     upper = halve(upper, "ctx", bits[1:])
     downer = halve(downer, "ctx", bits[::-1][1:])
     token_factor = (2 * length * places) ** (-0.5)
     weight_grad = jnp.concatenate([upper[0], downer[0]], axis=0) * token_factor
-    came_out = scatter_step(terms, came_out, "head", groups - 1)
     layer_output = (
         terms[0] + came_out[0].astype(jnp.float32) + came_out[1].astype(jnp.float32)
     ).astype(jnp.bfloat16)

time: 161 us -> 155 us (0.963)
  waiting for transfers between devices: 81.1 us -> 67.6 us
  starting transfers between devices: 35.2 us -> 41.5 us
    ppermute x18, waiting for transfers between devices: 38.6 us -> 27.9 us  [swap(): return lax.ppermute(array, axis, [(i, i ^ bit) for i in range(count)])]
    ppermute x6, starting transfers between devices: 13.6 us -> 20.7 us  [right_of(): return lax.ppermute(array, axis, [(i, i + 1) for i in range(first, last)])]
    ppermute x6, waiting for transfers between devices: 33.5 us -> 29.4 us  [left_of(): return lax.ppermute(array, axis, [(i, i - 1) for i in range(first, last)])]
  transfers between devices with their start and end apart: 30 -> 30, of which waited for: 18 -> 16; matrix products, arithmetic and copies ran while one was open for 19% -> 19% of each run, Pallas kernels for 0% -> 0%
where the time goes in v4:
time: 155 us; the launch traced here: 153 us
  waiting for transfers between devices  67.6 us (44%)
  starting transfers between devices  41.5 us (27%)
  matrix products  24.7 us (16%)
  other arithmetic  12.1 us (8%)
  local copies, waits for them, and re-layouts  5.12 us (3%)
  between operations  1.59 us (1%)
    ppermute x6, waiting for transfers between devices, left_of(): return lax.ppermute(array, axis, [(i, i - 1) for i in range(first, last)])  29.4 us
    ppermute x18, waiting for transfers between devices, swap(): return lax.ppermute(array, axis, [(i, i ^ bit) for i in range(count)])  27.9 us
    ppermute x6, starting transfers between devices, right_of(): return lax.ppermute(array, axis, [(i, i + 1) for i in range(first, last)])  20.7 us
    ppermute x18, starting transfers between devices, swap(): return lax.ppermute(array, axis, [(i, i ^ bit) for i in range(count)])  14.1 us
    ppermute x6, waiting for transfers between devices, right_of(): return lax.ppermute(array, axis, [(i, i + 1) for i in range(first, last)])  10.3 us
    ppermute x6, starting transfers between devices, left_of(): return lax.ppermute(array, axis, [(i, i - 1) for i in range(first, last)])  6.74 us
    dot_general x8, matrix products, shards(): jnp.einsum('btr,btc->rc', normed_flat, lax.dynamic_slice_in_dim(grad, (2...  5.96 us
    dot_general x4, matrix products, shards(): jnp.einsum('btc,rc->btr', grad, columns, preferred_element_type=jnp.float32)  5.92 us
  transfers between devices with their start and end apart: 30, of which 16 were waited for; matrix products, arithmetic and copies ran while one was open for 19% of the time, Pallas kernels for 0%

profile of v4, /device:TPU:0, one launch (start us, length us, event | category | flops | bytes accessed | tf_op | source)
XLA Modules:
  0.0 152.7 jit_solution(1279070101121967720)
XLA Ops:
  0.6 1.1 copy-done
  1.8 2.6 %fusion.127 = (bf16[2,8,128,128]{3,2,1,0:T(8,128)(2,1)S(1)}, f32[2,8,128,128]{3,2,1,0:T(8,128)}) fusion(bf16[2,192,1024]{2,1,0:T(8,128)(2,1)S(1)} %copy-done, bf16[2,192,1024]{2,1,0:T(8,128)(2,1)} %param.6), kind=kOutput, calls=%fused_computation.191 | convolution fusion | flops 100925440 | bytes 3145728 | tf_op jit(solution)/shard_map/bhsd,bhse->bhde/dot_general | solution.py:150
  4.8 1.5 %collective-permute-done = bf16[2,8,128,128]{3,2,1,0:T(8,128)(2,1)S(1)} collective-permute-done((bf16[2,8,128,128]{3,2,1,0:T(8,128)(2,1)S(1)}, bf16[2,8,128,128]{3,2,1,0:T(8,128)(2,1)S(1)}, u32[]{:S(2)}, u32[]{:S(2)}) %collective-permute-start) | collective-permute-done | bytes 524320 | tf_op jit(solution)/shard_map/ppermute | solution.py:14
  6.6 0.9 copy-done.4
  7.5 2.9 %collective-permute-start.1 = (bf16[8,128,128]{2,1,0:T(8,128)(2,1)S(1)}, bf16[8,128,128]{2,1,0:T(8,128)(2,1)S(1)}, u32[]{:S(2)}, u32[]{:S(2)}) collective-permute-start(bf16[8,128,128]{2,1,0:T(8,128)(2,1)S(1)} %fusion.95), channel_id=1, source_target_pairs={{0,8},{4,12},{8,0},{12,4},{16,24},{20,28},{24,16},{28,20},{1,9},{5... | collective-permute-start | bytes 786440 | tf_op jit(solution)/shard_map/ppermute | solution.py:14
  10.3 4.4 %collective-permute-start.4 = (bf16[2,192,1024]{2,1,0:T(8,128)(2,1)}, bf16[2,192,1024]{2,1,0:T(8,128)(2,1)}, u32[]{:S(2)}, u32[]{:S(2)}) collective-permute-start(bf16[2,192,1024]{2,1,0:T(8,128)(2,1)} %param.9), channel_id=1, source_target_pairs={{0,1},{1,2},{2,3},{4,5},{5,6},{6,7},{8,9},{9,10},{10,11},{12,13},{... | collective-permute-start | bytes 2359304 | tf_op jit(solution)/shard_map/ppermute | solution.py:42
  14.7 1.3 collective-permute-start.5
  16.9 1.3 fusion.67
  18.2 1.8 %collective-permute-start.2 = (bf16[8,128,128]{2,1,0:T(8,128)(2,1)S(1)}, bf16[8,128,128]{2,1,0:T(8,128)(2,1)S(1)}, u32[]{:S(2)}, u32[]{:S(2)}) collective-permute-start(bf16[8,128,128]{2,1,0:T(8,128)(2,1)S(1)} %fusion.67), channel_id=1, source_target_pairs={{0,16},{4,20},{8,24},{12,28},{16,0},{20,4},{24,8},{28,12},{1,17},{... | collective-permute-start | bytes 786440 | tf_op jit(solution)/shard_map/ppermute | solution.py:14
  20.7 5.4 %collective-permute-done.2 = bf16[8,128,128]{2,1,0:T(8,128)(2,1)S(1)} collective-permute-done((bf16[8,128,128]{2,1,0:T(8,128)(2,1)S(1)}, bf16[8,128,128]{2,1,0:T(8,128)(2,1)S(1)}, u32[]{:S(2)}, u32[]{:S(2)}) %collective-permute-start.2) | collective-permute-done | bytes 262176 | tf_op jit(solution)/shard_map/ppermute | solution.py:14
  26.3 2.8 %fusion.16 = f32[1024,2,192]{0,2,1:T(8,128)S(1)} fusion(bf16[2,192,1024]{2,1,0:T(8,128)(2,1)S(1)} %copy-done.5, bf16[1024,4096]{1,0:T(8,128)(2,1)} %param.8, s32[]{:T(128)S(6)} %select_n.385), kind=kOutput, calls=%fused_computation.29 | convolution fusion | flops 805306368 | bytes 4456452 | tf_op jit(solution)/shard_map/btc,rc->btr/dot_general | solution.py:191
  29.1 1.8 %collective-permute-done.4 = bf16[2,192,1024]{2,1,0:T(8,128)(2,1)} collective-permute-done((bf16[2,192,1024]{2,1,0:T(8,128)(2,1)}, bf16[2,192,1024]{2,1,0:T(8,128)(2,1)}, u32[]{:S(2)}, u32[]{:S(2)}) %collective-permute-start.4) | collective-permute-done | bytes 786464 | tf_op jit(solution)/shard_map/ppermute | solution.py:42
  31.6 4.3 %collective-permute-done.5 = bf16[2,192,1024]{2,1,0:T(8,128)(2,1)} collective-permute-done((bf16[2,192,1024]{2,1,0:T(8,128)(2,1)}, bf16[2,192,1024]{2,1,0:T(8,128)(2,1)}, u32[]{:S(2)}, u32[]{:S(2)}) %collective-permute-start.5) | collective-permute-done | bytes 786464 | tf_op jit(solution)/shard_map/ppermute | solution.py:46
  35.9 1.3 collective-permute-start.7
  37.7 0.8 multiply_reduce_fusion
  39.5 1.0 fusion.128
  40.5 4.6 %collective-permute-start.13 = (bf16[2,192,1024]{2,1,0:T(8,128)(2,1)S(1)}, bf16[2,192,1024]{2,1,0:T(8,128)(2,1)S(1)}, u32[]{:S(2)}, u32[]{:S(2)}) collective-permute-start(bf16[2,192,1024]{2,1,0:T(8,128)(2,1)S(1)} %get-tuple-element.62), channel_id=1, source_target_pairs={{0,1},{4,5},{8,9},{12,13},{16,17},{20,21},{24,25},{28,29}} | collective-permute-start | bytes 2359304 | tf_op jit(solution)/shard_map/ppermute | solution.py:42
  45.1 1.0 fusion.129
  47.6 1.0 fusion
  48.6 7.5 %collective-permute-done.7 = bf16[2,192,1024]{2,1,0:T(8,128)(2,1)S(1)} collective-permute-done((bf16[2,192,1024]{2,1,0:T(8,128)(2,1)}, bf16[2,192,1024]{2,1,0:T(8,128)(2,1)S(1)}, u32[]{:S(2)}, u32[]{:S(2)}) %collective-permute-start.7) | collective-permute-done | bytes 786464 | tf_op jit(solution)/shard_map/ppermute | solution.py:46
  56.1 1.4 broadcast_select_fusion
  58.3 1.0 fusion.18
  60.6 1.0 fusion.14
  61.7 1.0 fusion.12
  63.4 1.5 collective-permute-start.9
  67.2 17.6 %collective-permute-done.9 = bf16[2,192,1024]{2,1,0:T(8,128)(2,1)S(1)} collective-permute-done((bf16[2,192,1024]{2,1,0:T(8,128)(2,1)S(1)}, bf16[2,192,1024]{2,1,0:T(8,128)(2,1)S(1)}, u32[]{:S(2)}, u32[]{:S(2)}) %collective-permute-start.9) | collective-permute-done | bytes 786464 | tf_op jit(solution)/shard_map/ppermute | solution.py:46
  85.8 1.1 fusion.37
  86.9 1.1 fusion.32
  88.0 1.0 fusion.28
  91.9 2.1 %collective-permute-start.24 = (bf16[2,192,1024]{2,1,0:T(8,128)(2,1)S(1)}, bf16[2,192,1024]{2,1,0:T(8,128)(2,1)S(1)}, u32[]{:S(2)}, u32[]{:S(2)}) collective-permute-start(bf16[2,192,1024]{2,1,0:T(8,128)(2,1)S(1)} %get-tuple-element.48), channel_id=1, source_target_pairs={{0,1},{1,2},{4,5},{5,6},{8,9},{9,10},{12,13},{13,14},{16,17},{17,1... | collective-permute-start | bytes 2359304 | tf_op jit(solution)/shard_map/ppermute | solution.py:42
  95.1 1.1 copy.151
  97.0 0.8 fusion.63
  97.7 6.7 %collective-permute-done.16 = bf16[8,128,128]{2,1,0:T(8,128)(2,1)S(1)} collective-permute-done((bf16[8,128,128]{2,1,0:T(8,128)(2,1)S(1)}, bf16[8,128,128]{2,1,0:T(8,128)(2,1)S(1)}, u32[]{:S(2)}, u32[]{:S(2)}) %collective-permute-start.16) | collective-permute-done | bytes 262176 | tf_op jit(solution)/shard_map/ppermute | solution.py:14
  104.5 1.6 %collective-permute-start.17 = (bf16[8,128,128]{2,1,0:T(8,128)(2,1)S(1)}, bf16[8,128,128]{2,1,0:T(8,128)(2,1)S(1)}, u32[]{:S(2)}, u32[]{:S(2)}) collective-permute-start(bf16[8,128,128]{2,1,0:T(8,128)(2,1)S(1)} %fusion.70), channel_id=1, source_target_pairs={{0,16},{4,20},{8,24},{12,28},{16,0},{20,4},{24,8},{28,12},{1,17},{... | collective-permute-start | bytes 786440 | tf_op jit(solution)/shard_map/ppermute | solution.py:14
  109.0 2.0 %collective-permute-done.24 = bf16[2,192,1024]{2,1,0:T(8,128)(2,1)S(1)} collective-permute-done((bf16[2,192,1024]{2,1,0:T(8,128)(2,1)S(1)}, bf16[2,192,1024]{2,1,0:T(8,128)(2,1)S(1)}, u32[]{:S(2)}, u32[]{:S(2)}) %collective-permute-start.24) | collective-permute-done | bytes 786464 | tf_op jit(solution)/shard_map/ppermute | solution.py:42
  111.8 1.5 collective-permute-start.21
  113.8 1.3 collective-permute-start.27
  115.2 7.6 %collective-permute-done.20 = bf16[512,512]{1,0:T(8,128)(2,1)S(1)} collective-permute-done((bf16[512,512]{1,0:T(8,128)(2,1)S(1)}, bf16[512,512]{1,0:T(8,128)(2,1)S(1)}, u32[]{:S(2)}, u32[]{:S(2)}) %collective-permute-start.20) | collective-permute-done | bytes 524320 | tf_op jit(solution)/shard_map/ppermute | solution.py:14
  122.8 8.2 %collective-permute-start.25 = (bf16[2,192,1024]{2,1,0:T(8,128)(2,1)S(1)}, bf16[2,192,1024]{2,1,0:T(8,128)(2,1)S(1)}, u32[]{:S(2)}, u32[]{:S(2)}) collective-permute-start(bf16[2,192,1024]{2,1,0:T(8,128)(2,1)S(1)} %add_convert_fusion.4), channel_id=1, source_target_pairs={{0,1},{1,2},{2,3},{4,5},{5,6},{6,7},{8,9},{9,10},{10,11},{12,13},{... | collective-permute-start | bytes 2359304 | tf_op jit(solution)/shard_map/ppermute | solution.py:42
  131.7 2.5 %collective-permute-done.21 = bf16[512,512]{1,0:T(8,128)(2,1)S(1)} collective-permute-done((bf16[512,512]{1,0:T(8,128)(2,1)S(1)}, bf16[512,512]{1,0:T(8,128)(2,1)S(1)}, u32[]{:S(2)}, u32[]{:S(2)}) %collective-permute-start.21) | collective-permute-done | bytes 524320 | tf_op jit(solution)/shard_map/ppermute | solution.py:14
  134.6 0.8 fusion.131
  135.3 1.6 %collective-permute-start.28 = (bf16[512,512]{1,0:T(8,128)(2,1)S(1)}, bf16[512,512]{1,0:T(8,128)(2,1)S(1)}, u32[]{:S(2)}, u32[]{:S(2)}) collective-permute-start(bf16[512,512]{1,0:T(8,128)(2,1)S(1)} %get-tuple-element.36), channel_id=1, source_target_pairs={{0,16},{4,20},{8,24},{12,28},{16,0},{20,4},{24,8},{28,12},{1,17},{... | collective-permute-start | bytes 1572872 | tf_op jit(solution)/shard_map/ppermute | solution.py:14
  137.7 6.6 %collective-permute-done.25 = bf16[2,192,1024]{2,1,0:T(8,128)(2,1)S(1)} collective-permute-done((bf16[2,192,1024]{2,1,0:T(8,128)(2,1)S(1)}, bf16[2,192,1024]{2,1,0:T(8,128)(2,1)S(1)}, u32[]{:S(2)}, u32[]{:S(2)}) %collective-permute-start.25) | collective-permute-done | bytes 786464 | tf_op jit(solution)/shard_map/ppermute | solution.py:42
  144.7 1.3 add_convert_fusion.1
  146.4 1.4 copy_bitcast_fusion
  147.8 1.9 %collective-permute-done.28 = bf16[512,512]{1,0:T(8,128)(2,1)S(1)} collective-permute-done((bf16[512,512]{1,0:T(8,128)(2,1)S(1)}, bf16[512,512]{1,0:T(8,128)(2,1)S(1)}, u32[]{:S(2)}, u32[]{:S(2)}) %collective-permute-start.28) | collective-permute-done | bytes 524320 | tf_op jit(solution)/shard_map/ppermute | solution.py:14
  149.9 1.1 collective-permute-done.29
  151.1 1.6 %maximum_multiply_fusion = f32[1024,512]{1,0:T(8,128)} fusion(f32[512,512]{1,0:T(8,128)S(1)} %convert_add_fusion.2, f32[512,512]{1,0:T(8,128)S(1)} %convert_add_fusion.3), kind=kLoop, calls=%fused_computation.4 | loop fusion | flops 1048576 | bytes 4194304 | tf_op jit(solution)/shard_map/mul | solution.py:236
  (90 shorter events, 23.8 us)
Async XLA Ops:
  0.6 1.1 copy-start
  4.4 2.0 %collective-permute-start = (bf16[2,8,128,128]{3,2,1,0:T(8,128)(2,1)S(1)}, bf16[2,8,128,128]{3,2,1,0:T(8,128)(2,1)S(1)}, u32[]{:S(2)}, u32[]{:S(2)}) collective-permute-start(bf16[2,8,128,128]{3,2,1,0:T(8,128)(2,1)S(1)} %get-tuple-element.58), channel_id=1, source_target_pairs={{0,4},{4,0},{8,12},{12,8},{16,20},{20,16},{24,28},{28,24},{1,5},{5... | collective-permute-start | bytes 1572872 | tf_op jit(solution)/shard_map/ppermute | solution.py:14
  4.8 1.7 %copy-start.3 = (f32[2,8,128,128]{3,2,1,0:T(8,128)S(1)}, f32[2,8,128,128]{3,2,1,0:T(8,128)}, u32[]{:S(2)}) copy-start(f32[2,8,128,128]{3,2,1,0:T(8,128)} %get-tuple-element.59) | copy-start | bytes 3145732
  6.5 1.0 copy-start.4
  6.5 13.6 %copy-start.1 = (bf16[2,192,1024]{2,1,0:T(8,128)(2,1)S(1)}, bf16[2,192,1024]{2,1,0:T(8,128)(2,1)}, u32[]{:S(2)}) copy-start(bf16[2,192,1024]{2,1,0:T(8,128)(2,1)} %param.6) | copy-start | bytes 2359300
  6.5 13.6 %copy-start.2 = (bf16[2,192,1024]{2,1,0:T(8,128)(2,1)S(1)}, bf16[2,192,1024]{2,1,0:T(8,128)(2,1)}, u32[]{:S(2)}) copy-start(bf16[2,192,1024]{2,1,0:T(8,128)(2,1)} %param.5) | copy-start | bytes 2359300
  7.5 9.5 %collective-permute-start.1 = (bf16[8,128,128]{2,1,0:T(8,128)(2,1)S(1)}, bf16[8,128,128]{2,1,0:T(8,128)(2,1)S(1)}, u32[]{:S(2)}, u32[]{:S(2)}) collective-permute-start(bf16[8,128,128]{2,1,0:T(8,128)(2,1)S(1)} %fusion.95), channel_id=1, source_target_pairs={{0,8},{4,12},{8,0},{12,4},{16,24},{20,28},{24,16},{28,20},{1,9},{5... | collective-permute-start | bytes 786440 | tf_op jit(solution)/shard_map/ppermute | solution.py:14
  10.3 20.6 %collective-permute-start.4 = (bf16[2,192,1024]{2,1,0:T(8,128)(2,1)}, bf16[2,192,1024]{2,1,0:T(8,128)(2,1)}, u32[]{:S(2)}, u32[]{:S(2)}) collective-permute-start(bf16[2,192,1024]{2,1,0:T(8,128)(2,1)} %param.9), channel_id=1, source_target_pairs={{0,1},{1,2},{2,3},{4,5},{5,6},{6,7},{8,9},{9,10},{10,11},{12,13},{... | collective-permute-start | bytes 2359304 | tf_op jit(solution)/shard_map/ppermute | solution.py:42
  14.7 21.2 %collective-permute-start.5 = (bf16[2,192,1024]{2,1,0:T(8,128)(2,1)}, bf16[2,192,1024]{2,1,0:T(8,128)(2,1)}, u32[]{:S(2)}, u32[]{:S(2)}) collective-permute-start(bf16[2,192,1024]{2,1,0:T(8,128)(2,1)} %param.9), channel_id=1, source_target_pairs={{1,0},{2,1},{3,2},{5,4},{6,5},{7,6},{9,8},{10,9},{11,10},{13,12},{... | collective-permute-start | bytes 2359304 | tf_op jit(solution)/shard_map/ppermute | solution.py:46
  18.2 8.1 %copy-start.5 = (bf16[2,192,1024]{2,1,0:T(8,128)(2,1)S(1)}, bf16[2,192,1024]{2,1,0:T(8,128)(2,1)}, u32[]{:S(2)}) copy-start(bf16[2,192,1024]{2,1,0:T(8,128)(2,1)} %param.9) | copy-start | bytes 2359300
  18.2 7.9 %collective-permute-start.2 = (bf16[8,128,128]{2,1,0:T(8,128)(2,1)S(1)}, bf16[8,128,128]{2,1,0:T(8,128)(2,1)S(1)}, u32[]{:S(2)}, u32[]{:S(2)}) collective-permute-start(bf16[8,128,128]{2,1,0:T(8,128)(2,1)S(1)} %fusion.67), channel_id=1, source_target_pairs={{0,16},{4,20},{8,24},{12,28},{16,0},{20,4},{24,8},{28,12},{1,17},{... | collective-permute-start | bytes 786440 | tf_op jit(solution)/shard_map/ppermute | solution.py:14
  26.2 11.0 %collective-permute-start.3 = (bf16[8,128,128]{2,1,0:T(8,128)(2,1)S(1)}, bf16[8,128,128]{2,1,0:T(8,128)(2,1)S(1)}, u32[]{:S(2)}, u32[]{:S(2)}) collective-permute-start(bf16[8,128,128]{2,1,0:T(8,128)(2,1)S(1)} %fusion.66), channel_id=1, source_target_pairs={{0,4},{4,0},{8,12},{12,8},{16,20},{20,16},{24,28},{28,24},{1,5},{5... | collective-permute-start | bytes 786440 | tf_op jit(solution)/shard_map/ppermute | solution.py:14
  26.3 12.7 %slice-start = ((s8[8388608]{0:T(1024)(128)(4,1)}), s8[4194304]{0:T(1024)(128)(4,1)S(1)}, s32[]{:S(2)}) async-start(s8[8388608]{0:T(1024)(128)(4,1)} %bitcast.335), calls=%async_computation | async-start | bytes 8388608
  30.9 17.7 %collective-permute-start.6 = (bf16[2,192,1024]{2,1,0:T(8,128)(2,1)}, bf16[2,192,1024]{2,1,0:T(8,128)(2,1)S(1)}, u32[]{:S(2)}, u32[]{:S(2)}) collective-permute-start(bf16[2,192,1024]{2,1,0:T(8,128)(2,1)} %collective-permute-done.4), channel_id=1, source_target_pairs={{1,2},{2,3},{5,6},{6,7},{9,10},{10,11},{13,14},{14,15},{17,18},{18... | collective-permute-start | bytes 2359304 | tf_op jit(solution)/shard_map/ppermute | solution.py:42
  35.9 20.2 %collective-permute-start.7 = (bf16[2,192,1024]{2,1,0:T(8,128)(2,1)}, bf16[2,192,1024]{2,1,0:T(8,128)(2,1)S(1)}, u32[]{:S(2)}, u32[]{:S(2)}) collective-permute-start(bf16[2,192,1024]{2,1,0:T(8,128)(2,1)} %collective-permute-done.5), channel_id=1, source_target_pairs={{1,0},{2,1},{5,4},{6,5},{9,8},{10,9},{13,12},{14,13},{17,16},{18,1... | collective-permute-start | bytes 2359304 | tf_op jit(solution)/shard_map/ppermute | solution.py:46
  37.3 2.2 %slice-start.1 = ((s8[8388608]{0:T(1024)(128)(4,1)}), s8[4194304]{0:T(1024)(128)(4,1)S(1)}, s32[]{:S(2)}) async-start(s8[8388608]{0:T(1024)(128)(4,1)} %bitcast.335), calls=%async_computation.1 | async-start | bytes 8388608
  40.5 26.7 %collective-permute-start.13 = (bf16[2,192,1024]{2,1,0:T(8,128)(2,1)S(1)}, bf16[2,192,1024]{2,1,0:T(8,128)(2,1)S(1)}, u32[]{:S(2)}, u32[]{:S(2)}) collective-permute-start(bf16[2,192,1024]{2,1,0:T(8,128)(2,1)S(1)} %get-tuple-element.62), channel_id=1, source_target_pairs={{0,1},{4,5},{8,9},{12,13},{16,17},{20,21},{24,25},{28,29}} | collective-permute-start | bytes 2359304 | tf_op jit(solution)/shard_map/ppermute | solution.py:42
  46.0 21.1 %collective-permute-start.14 = (bf16[2,192,1024]{2,1,0:T(8,128)(2,1)S(1)}, bf16[2,192,1024]{2,1,0:T(8,128)(2,1)S(1)}, u32[]{:S(2)}, u32[]{:S(2)}) collective-permute-start(bf16[2,192,1024]{2,1,0:T(8,128)(2,1)S(1)} %get-tuple-element.64), channel_id=1, source_target_pairs={{3,2},{7,6},{11,10},{15,14},{19,18},{23,22},{27,26},{31,30}} | collective-permute-start | bytes 2359304 | tf_op jit(solution)/shard_map/ppermute | solution.py:46
  47.5 15.2 %collective-permute-start.10 = (bf16[1024,512]{1,0:T(8,128)(2,1)S(1)}, bf16[1024,512]{1,0:T(8,128)(2,1)S(1)}, u32[]{:S(2)}, u32[]{:S(2)}) collective-permute-start(bf16[1024,512]{1,0:T(8,128)(2,1)S(1)} %bitcast_convert_fusion.3), channel_id=1, source_target_pairs={{0,4},{4,0},{8,12},{12,8},{16,20},{20,16},{24,28},{28,24},{1,5},{5... | collective-permute-start | bytes 3145736 | tf_op jit(solution)/shard_map/ppermute | solution.py:14
  58.3 5.2 %collective-permute-start.12 = (bf16[1024,512]{1,0:T(8,128)(2,1)S(1)}, bf16[1024,512]{1,0:T(8,128)(2,1)S(1)}, u32[]{:S(2)}, u32[]{:S(2)}) collective-permute-start(bf16[1024,512]{1,0:T(8,128)(2,1)S(1)} %bitcast_convert_fusion.1), channel_id=1, source_target_pairs={{0,4},{4,0},{8,12},{12,8},{16,20},{20,16},{24,28},{28,24},{1,5},{5... | collective-permute-start | bytes 3145736 | tf_op jit(solution)/shard_map/ppermute | solution.py:14
  60.1 6.3 %collective-permute-start.11 = (bf16[1024,512]{1,0:T(8,128)(2,1)S(1)}, bf16[1024,512]{1,0:T(8,128)(2,1)S(1)}, u32[]{:S(2)}, u32[]{:S(2)}) collective-permute-start(bf16[1024,512]{1,0:T(8,128)(2,1)S(1)} %bitcast_convert_fusion.2), channel_id=1, source_target_pairs={{0,4},{4,0},{8,12},{12,8},{16,20},{20,16},{24,28},{28,24},{1,5},{5... | collective-permute-start | bytes 3145736 | tf_op jit(solution)/shard_map/ppermute | solution.py:14
  62.7 4.5 %collective-permute-start.8 = (bf16[2,192,1024]{2,1,0:T(8,128)(2,1)S(1)}, bf16[2,192,1024]{2,1,0:T(8,128)(2,1)S(1)}, u32[]{:S(2)}, u32[]{:S(2)}) collective-permute-start(bf16[2,192,1024]{2,1,0:T(8,128)(2,1)S(1)} %collective-permute-done.6), channel_id=1, source_target_pairs={{2,3},{6,7},{10,11},{14,15},{18,19},{22,23},{26,27},{30,31}} | collective-permute-start | bytes 2359304 | tf_op jit(solution)/shard_map/ppermute | solution.py:42
  63.4 21.4 %collective-permute-start.9 = (bf16[2,192,1024]{2,1,0:T(8,128)(2,1)S(1)}, bf16[2,192,1024]{2,1,0:T(8,128)(2,1)S(1)}, u32[]{:S(2)}, u32[]{:S(2)}) collective-permute-start(bf16[2,192,1024]{2,1,0:T(8,128)(2,1)S(1)} %collective-permute-done.7), channel_id=1, source_target_pairs={{1,0},{5,4},{9,8},{13,12},{17,16},{21,20},{25,24},{29,28}} | collective-permute-start | bytes 2359304 | tf_op jit(solution)/shard_map/ppermute | solution.py:46
  90.2 16.2 %collective-permute-start.18 = (bf16[1024,512]{1,0:T(8,128)(2,1)S(1)}, bf16[1024,512]{1,0:T(8,128)(2,1)S(1)}, u32[]{:S(2)}, u32[]{:S(2)}) collective-permute-start(bf16[1024,512]{1,0:T(8,128)(2,1)S(1)} %bitcast_convert_fusion), channel_id=1, source_target_pairs={{0,4},{4,0},{8,12},{12,8},{16,20},{20,16},{24,28},{28,24},{1,5},{5... | collective-permute-start | bytes 3145736 | tf_op jit(solution)/shard_map/ppermute | solution.py:14
  90.2 5.9 %collective-permute-start.15 = (bf16[2,8,128,128]{3,2,1,0:T(8,128)(2,1)S(1)}, bf16[2,8,128,128]{3,2,1,0:T(8,128)(2,1)S(1)}, u32[]{:S(2)}, u32[]{:S(2)}) collective-permute-start(bf16[2,8,128,128]{3,2,1,0:T(8,128)(2,1)S(1)} %get-tuple-element.66), channel_id=1, source_target_pairs={{0,4},{4,0},{8,12},{12,8},{16,20},{20,16},{24,28},{28,24},{1,5},{5... | collective-permute-start | bytes 1572872 | tf_op jit(solution)/shard_map/ppermute | solution.py:14
  91.2 14.9 %collective-permute-start.26 = (bf16[2,192,1024]{2,1,0:T(8,128)(2,1)S(1)}, bf16[2,192,1024]{2,1,0:T(8,128)(2,1)S(1)}, u32[]{:S(2)}, u32[]{:S(2)}) collective-permute-start(bf16[2,192,1024]{2,1,0:T(8,128)(2,1)S(1)} %get-tuple-element.47), channel_id=1, source_target_pairs={{2,1},{3,2},{6,5},{7,6},{10,9},{11,10},{14,13},{15,14},{18,17},{19... | collective-permute-start | bytes 2359304 | tf_op jit(solution)/shard_map/ppermute | solution.py:46
  91.9 19.1 %collective-permute-start.24 = (bf16[2,192,1024]{2,1,0:T(8,128)(2,1)S(1)}, bf16[2,192,1024]{2,1,0:T(8,128)(2,1)S(1)}, u32[]{:S(2)}, u32[]{:S(2)}) collective-permute-start(bf16[2,192,1024]{2,1,0:T(8,128)(2,1)S(1)} %get-tuple-element.48), channel_id=1, source_target_pairs={{0,1},{1,2},{4,5},{5,6},{8,9},{9,10},{12,13},{13,14},{16,17},{17,1... | collective-permute-start | bytes 2359304 | tf_op jit(solution)/shard_map/ppermute | solution.py:42
  96.3 8.1 %collective-permute-start.16 = (bf16[8,128,128]{2,1,0:T(8,128)(2,1)S(1)}, bf16[8,128,128]{2,1,0:T(8,128)(2,1)S(1)}, u32[]{:S(2)}, u32[]{:S(2)}) collective-permute-start(bf16[8,128,128]{2,1,0:T(8,128)(2,1)S(1)} %fusion.96), channel_id=1, source_target_pairs={{0,8},{4,12},{8,0},{12,4},{16,24},{20,28},{24,16},{28,20},{1,9},{5... | collective-permute-start | bytes 786440 | tf_op jit(solution)/shard_map/ppermute | solution.py:14
  104.5 9.3 %collective-permute-start.17 = (bf16[8,128,128]{2,1,0:T(8,128)(2,1)S(1)}, bf16[8,128,128]{2,1,0:T(8,128)(2,1)S(1)}, u32[]{:S(2)}, u32[]{:S(2)}) collective-permute-start(bf16[8,128,128]{2,1,0:T(8,128)(2,1)S(1)} %fusion.70), channel_id=1, source_target_pairs={{0,16},{4,20},{8,24},{12,28},{16,0},{20,4},{24,8},{28,12},{1,17},{... | collective-permute-start | bytes 786440 | tf_op jit(solution)/shard_map/ppermute | solution.py:14
  107.9 14.9 %collective-permute-start.20 = (bf16[512,512]{1,0:T(8,128)(2,1)S(1)}, bf16[512,512]{1,0:T(8,128)(2,1)S(1)}, u32[]{:S(2)}, u32[]{:S(2)}) collective-permute-start(bf16[512,512]{1,0:T(8,128)(2,1)S(1)} %get-tuple-element.42), channel_id=1, source_target_pairs={{0,8},{4,12},{8,0},{12,4},{16,24},{20,28},{24,16},{28,20},{1,9},{5... | collective-permute-start | bytes 1572872 | tf_op jit(solution)/shard_map/ppermute | solution.py:14
  108.5 22.5 %collective-permute-start.22 = (bf16[512,512]{1,0:T(8,128)(2,1)S(1)}, bf16[512,512]{1,0:T(8,128)(2,1)S(1)}, u32[]{:S(2)}, u32[]{:S(2)}) collective-permute-start(bf16[512,512]{1,0:T(8,128)(2,1)S(1)} %get-tuple-element.41), channel_id=1, source_target_pairs={{0,16},{4,20},{8,24},{12,28},{16,0},{20,4},{24,8},{28,12},{1,17},{... | collective-permute-start | bytes 1572872 | tf_op jit(solution)/shard_map/ppermute | solution.py:14
  111.2 20.4 %collective-permute-start.19 = (bf16[512,512]{1,0:T(8,128)(2,1)S(1)}, bf16[512,512]{1,0:T(8,128)(2,1)S(1)}, u32[]{:S(2)}, u32[]{:S(2)}) collective-permute-start(bf16[512,512]{1,0:T(8,128)(2,1)S(1)} %get-tuple-element.43), channel_id=1, source_target_pairs={{0,8},{4,12},{8,0},{12,4},{16,24},{20,28},{24,16},{28,20},{1,9},{5... | collective-permute-start | bytes 1572872 | tf_op jit(solution)/shard_map/ppermute | solution.py:14
  111.8 22.3 %collective-permute-start.21 = (bf16[512,512]{1,0:T(8,128)(2,1)S(1)}, bf16[512,512]{1,0:T(8,128)(2,1)S(1)}, u32[]{:S(2)}, u32[]{:S(2)}) collective-permute-start(bf16[512,512]{1,0:T(8,128)(2,1)S(1)} %get-tuple-element.44), channel_id=1, source_target_pairs={{0,16},{4,20},{8,24},{12,28},{16,0},{20,4},{24,8},{28,12},{1,17},{... | collective-permute-start | bytes 1572872 | tf_op jit(solution)/shard_map/ppermute | solution.py:14
  113.8 23.9 %collective-permute-start.27 = (bf16[2,192,1024]{2,1,0:T(8,128)(2,1)S(1)}, bf16[2,192,1024]{2,1,0:T(8,128)(2,1)S(1)}, u32[]{:S(2)}, u32[]{:S(2)}) collective-permute-start(bf16[2,192,1024]{2,1,0:T(8,128)(2,1)S(1)} %add_convert_fusion.2), channel_id=1, source_target_pairs={{1,0},{2,1},{3,2},{5,4},{6,5},{7,6},{9,8},{10,9},{11,10},{13,12},{... | collective-permute-start | bytes 2359304 | tf_op jit(solution)/shard_map/ppermute | solution.py:46
  122.8 21.4 %collective-permute-start.25 = (bf16[2,192,1024]{2,1,0:T(8,128)(2,1)S(1)}, bf16[2,192,1024]{2,1,0:T(8,128)(2,1)S(1)}, u32[]{:S(2)}, u32[]{:S(2)}) collective-permute-start(bf16[2,192,1024]{2,1,0:T(8,128)(2,1)S(1)} %add_convert_fusion.4), channel_id=1, source_target_pairs={{0,1},{1,2},{2,3},{4,5},{5,6},{6,7},{8,9},{9,10},{10,11},{12,13},{... | collective-permute-start | bytes 2359304 | tf_op jit(solution)/shard_map/ppermute | solution.py:42
  134.5 3.0 %collective-permute-start.23 = (bf16[8,128,128]{2,1,0:T(8,128)(2,1)S(1)}, bf16[8,128,128]{2,1,0:T(8,128)(2,1)S(1)}, u32[]{:S(2)}, u32[]{:S(2)}) collective-permute-start(bf16[8,128,128]{2,1,0:T(8,128)(2,1)S(1)} %fusion.69), channel_id=1, source_target_pairs={{0,4},{4,0},{8,12},{12,8},{16,20},{20,16},{24,28},{28,24},{1,5},{5... | collective-permute-start | bytes 786440 | tf_op jit(solution)/shard_map/ppermute | solution.py:14
  135.3 14.4 %collective-permute-start.28 = (bf16[512,512]{1,0:T(8,128)(2,1)S(1)}, bf16[512,512]{1,0:T(8,128)(2,1)S(1)}, u32[]{:S(2)}, u32[]{:S(2)}) collective-permute-start(bf16[512,512]{1,0:T(8,128)(2,1)S(1)} %get-tuple-element.36), channel_id=1, source_target_pairs={{0,16},{4,20},{8,24},{12,28},{16,0},{20,4},{24,8},{28,12},{1,17},{... | collective-permute-start | bytes 1572872 | tf_op jit(solution)/shard_map/ppermute | solution.py:14
  136.9 14.0 %collective-permute-start.29 = (bf16[512,512]{1,0:T(8,128)(2,1)S(1)}, bf16[512,512]{1,0:T(8,128)(2,1)S(1)}, u32[]{:S(2)}, u32[]{:S(2)}) collective-permute-start(bf16[512,512]{1,0:T(8,128)(2,1)S(1)} %get-tuple-element.38), channel_id=1, source_target_pairs={{0,8},{4,12},{8,0},{12,4},{16,24},{20,28},{24,16},{28,20},{1,9},{5... | collective-permute-start | bytes 1572872 | tf_op jit(solution)/shard_map/ppermute | solution.py:14

commit v5 on v4

--- a/solution.py
+++ b/solution.py
@@ -226,7 +226,7 @@
     downer = halve({k: block[rows:] for k, block in blocks.items()}, "ctx", bits[::-1][:1])
     for step in range(2, groups):
         came_out = scatter_step(terms, came_out, "head", step)
-    grad_state, (upper, downer) = exclusive_scan(
+    grad_state, _ = exclusive_scan(
         local_grad_state, "ctx", True, (upper, downer)
     )
     grad_state, came_out = lax.optimization_barrier((grad_state, came_out))

time: 155 us -> 152 us (0.981); the launches traced: 153 us -> 152 us
  starting transfers between devices: 41.5 us -> 38.6 us
  waiting for transfers between devices: 67.6 us -> 69.8 us
    ppermute x18, waiting for transfers between devices: 27.9 us -> 35.7 us  [swap(): return lax.ppermute(array, axis, [(i, i ^ bit) for i in range(count)])]
    ppermute x6, waiting for transfers between devices: 10.3 us -> 4.71 us  [right_of(): return lax.ppermute(array, axis, [(i, i + 1) for i in range(first, last)])]
    ppermute x6, starting transfers between devices: 20.7 us -> 17 us  [right_of(): return lax.ppermute(array, axis, [(i, i + 1) for i in range(first, last)])]
  transfers between devices with their start and end apart: 30 -> 30, of which waited for: 16 -> 12; matrix products, arithmetic and copies ran while one was open for 19% -> 18% of each run, Pallas kernels for 0% -> 0%
where the time goes in v5:
time: 152 us
  waiting for transfers between devices  69.8 us (46%)
  starting transfers between devices  38.6 us (25%)
  matrix products  24.8 us (16%)
  other arithmetic  11.8 us (8%)
  local copies, waits for them, and re-layouts  5.16 us (3%)
  between operations  1.6 us (1%)
    ppermute x18, waiting for transfers between devices, swap(): return lax.ppermute(array, axis, [(i, i ^ bit) for i in range(count)])  35.7 us
    ppermute x6, waiting for transfers between devices, left_of(): return lax.ppermute(array, axis, [(i, i - 1) for i in range(first, last)])  29.4 us
    ppermute x6, starting transfers between devices, right_of(): return lax.ppermute(array, axis, [(i, i + 1) for i in range(first, last)])  17 us
    ppermute x18, starting transfers between devices, swap(): return lax.ppermute(array, axis, [(i, i ^ bit) for i in range(count)])  14.8 us
    ppermute x6, starting transfers between devices, left_of(): return lax.ppermute(array, axis, [(i, i - 1) for i in range(first, last)])  6.75 us
    dot_general x8, matrix products, shards(): jnp.einsum('btr,btc->rc', normed_flat, lax.dynamic_slice_in_dim(grad, (2...  5.97 us
    dot_general x4, matrix products, shards(): jnp.einsum('btc,rc->btr', grad, columns, preferred_element_type=jnp.float32)  5.96 us
    ppermute x6, waiting for transfers between devices, right_of(): return lax.ppermute(array, axis, [(i, i + 1) for i in range(first, last)])  4.71 us
  transfers between devices with their start and end apart: 30, of which 12 were waited for; matrix products, arithmetic and copies ran while one was open for 18% of the time, Pallas kernels for 0%

profile of v5, /device:TPU:0, one launch (start us, length us, event | category | flops | bytes accessed | tf_op | source)
XLA Modules:
  0.0 151.7 jit_solution(15719327286414096571)
XLA Ops:
  0.6 1.1 copy-done
  1.8 2.6 %fusion.129 = (bf16[2,8,128,128]{3,2,1,0:T(8,128)(2,1)S(1)}, f32[2,8,128,128]{3,2,1,0:T(8,128)}) fusion(bf16[2,192,1024]{2,1,0:T(8,128)(2,1)S(1)} %copy-done, bf16[2,192,1024]{2,1,0:T(8,128)(2,1)} %param.6), kind=kOutput, calls=%fused_computation.191 | convolution fusion | flops 100925440 | bytes 3145728 | tf_op jit(solution)/shard_map/bhsd,bhse->bhde/dot_general | solution.py:150
  4.8 1.5 %collective-permute-done = bf16[2,8,128,128]{3,2,1,0:T(8,128)(2,1)S(1)} collective-permute-done((bf16[2,8,128,128]{3,2,1,0:T(8,128)(2,1)S(1)}, bf16[2,8,128,128]{3,2,1,0:T(8,128)(2,1)S(1)}, u32[]{:S(2)}, u32[]{:S(2)}) %collective-permute-start) | collective-permute-done | bytes 524320 | tf_op jit(solution)/shard_map/ppermute | solution.py:14
  6.6 0.9 copy-done.4
  7.5 2.9 %collective-permute-start.1 = (bf16[8,128,128]{2,1,0:T(8,128)(2,1)S(1)}, bf16[8,128,128]{2,1,0:T(8,128)(2,1)S(1)}, u32[]{:S(2)}, u32[]{:S(2)}) collective-permute-start(bf16[8,128,128]{2,1,0:T(8,128)(2,1)S(1)} %fusion.95), channel_id=1, source_target_pairs={{0,8},{4,12},{8,0},{12,4},{16,24},{20,28},{24,16},{28,20},{1,9},{5... | collective-permute-start | bytes 786440 | tf_op jit(solution)/shard_map/ppermute | solution.py:14
  10.3 4.4 %collective-permute-start.4 = (bf16[2,192,1024]{2,1,0:T(8,128)(2,1)}, bf16[2,192,1024]{2,1,0:T(8,128)(2,1)}, u32[]{:S(2)}, u32[]{:S(2)}) collective-permute-start(bf16[2,192,1024]{2,1,0:T(8,128)(2,1)} %param.9), channel_id=1, source_target_pairs={{0,1},{1,2},{2,3},{4,5},{5,6},{6,7},{8,9},{9,10},{10,11},{12,13},{... | collective-permute-start | bytes 2359304 | tf_op jit(solution)/shard_map/ppermute | solution.py:42
  14.7 1.3 collective-permute-start.5
  16.9 1.3 fusion.67
  18.2 1.8 %collective-permute-start.2 = (bf16[8,128,128]{2,1,0:T(8,128)(2,1)S(1)}, bf16[8,128,128]{2,1,0:T(8,128)(2,1)S(1)}, u32[]{:S(2)}, u32[]{:S(2)}) collective-permute-start(bf16[8,128,128]{2,1,0:T(8,128)(2,1)S(1)} %fusion.67), channel_id=1, source_target_pairs={{0,16},{4,20},{8,24},{12,28},{16,0},{20,4},{24,8},{28,12},{1,17},{... | collective-permute-start | bytes 786440 | tf_op jit(solution)/shard_map/ppermute | solution.py:14
  20.7 5.4 %collective-permute-done.2 = bf16[8,128,128]{2,1,0:T(8,128)(2,1)S(1)} collective-permute-done((bf16[8,128,128]{2,1,0:T(8,128)(2,1)S(1)}, bf16[8,128,128]{2,1,0:T(8,128)(2,1)S(1)}, u32[]{:S(2)}, u32[]{:S(2)}) %collective-permute-start.2) | collective-permute-done | bytes 262176 | tf_op jit(solution)/shard_map/ppermute | solution.py:14
  26.3 2.8 %fusion.16 = f32[1024,2,192]{0,2,1:T(8,128)S(1)} fusion(bf16[2,192,1024]{2,1,0:T(8,128)(2,1)S(1)} %copy-done.5, bf16[1024,4096]{1,0:T(8,128)(2,1)} %param.8, s32[]{:T(128)S(6)} %select_n.385), kind=kOutput, calls=%fused_computation.29 | convolution fusion | flops 805306368 | bytes 4456452 | tf_op jit(solution)/shard_map/btc,rc->btr/dot_general | solution.py:191
  29.1 1.8 %collective-permute-done.4 = bf16[2,192,1024]{2,1,0:T(8,128)(2,1)} collective-permute-done((bf16[2,192,1024]{2,1,0:T(8,128)(2,1)}, bf16[2,192,1024]{2,1,0:T(8,128)(2,1)}, u32[]{:S(2)}, u32[]{:S(2)}) %collective-permute-start.4) | collective-permute-done | bytes 786464 | tf_op jit(solution)/shard_map/ppermute | solution.py:42
  31.6 4.3 %collective-permute-done.5 = bf16[2,192,1024]{2,1,0:T(8,128)(2,1)} collective-permute-done((bf16[2,192,1024]{2,1,0:T(8,128)(2,1)}, bf16[2,192,1024]{2,1,0:T(8,128)(2,1)}, u32[]{:S(2)}, u32[]{:S(2)}) %collective-permute-start.5) | collective-permute-done | bytes 786464 | tf_op jit(solution)/shard_map/ppermute | solution.py:46
  35.9 1.3 collective-permute-start.7
  37.7 0.8 multiply_reduce_fusion
  39.5 1.0 fusion.130
  40.5 4.6 %collective-permute-start.13 = (bf16[2,192,1024]{2,1,0:T(8,128)(2,1)S(1)}, bf16[2,192,1024]{2,1,0:T(8,128)(2,1)S(1)}, u32[]{:S(2)}, u32[]{:S(2)}) collective-permute-start(bf16[2,192,1024]{2,1,0:T(8,128)(2,1)S(1)} %get-tuple-element.58), channel_id=1, source_target_pairs={{0,1},{4,5},{8,9},{12,13},{16,17},{20,21},{24,25},{28,29}} | collective-permute-start | bytes 2359304 | tf_op jit(solution)/shard_map/ppermute | solution.py:42
  45.1 1.0 fusion.131
  47.6 1.0 fusion
  48.6 7.5 %collective-permute-done.7 = bf16[2,192,1024]{2,1,0:T(8,128)(2,1)S(1)} collective-permute-done((bf16[2,192,1024]{2,1,0:T(8,128)(2,1)}, bf16[2,192,1024]{2,1,0:T(8,128)(2,1)S(1)}, u32[]{:S(2)}, u32[]{:S(2)}) %collective-permute-start.7) | collective-permute-done | bytes 786464 | tf_op jit(solution)/shard_map/ppermute | solution.py:46
  56.1 1.4 broadcast_select_fusion
  57.5 0.7 bitcast_convert_fusion.1
  58.3 1.0 fusion.18
  60.6 1.1 fusion.14
  61.7 1.0 fusion.12
  63.5 1.5 collective-permute-start.9
  66.5 0.8 fusion.10
  67.3 17.6 %collective-permute-done.9 = bf16[2,192,1024]{2,1,0:T(8,128)(2,1)S(1)} collective-permute-done((bf16[2,192,1024]{2,1,0:T(8,128)(2,1)S(1)}, bf16[2,192,1024]{2,1,0:T(8,128)(2,1)S(1)}, u32[]{:S(2)}, u32[]{:S(2)}) %collective-permute-start.9) | collective-permute-done | bytes 786464 | tf_op jit(solution)/shard_map/ppermute | solution.py:46
  85.7 1.1 fusion.37
  86.8 1.1 fusion.32
  88.0 1.0 fusion.28
  89.5 0.8 fusion.133
  91.5 2.1 %collective-permute-start.24 = (bf16[2,192,1024]{2,1,0:T(8,128)(2,1)S(1)}, bf16[2,192,1024]{2,1,0:T(8,128)(2,1)S(1)}, u32[]{:S(2)}, u32[]{:S(2)}) collective-permute-start(bf16[2,192,1024]{2,1,0:T(8,128)(2,1)S(1)} %get-tuple-element.44), channel_id=1, source_target_pairs={{0,1},{1,2},{4,5},{5,6},{8,9},{9,10},{12,13},{13,14},{16,17},{17,1... | collective-permute-start | bytes 2359304 | tf_op jit(solution)/shard_map/ppermute | solution.py:42
  98.1 1.6 %collective-permute-start.20 = (bf16[512,512]{1,0:T(8,128)(2,1)S(1)}, bf16[512,512]{1,0:T(8,128)(2,1)S(1)}, u32[]{:S(2)}, u32[]{:S(2)}) collective-permute-start(bf16[512,512]{1,0:T(8,128)(2,1)S(1)} %get-tuple-element.36), channel_id=1, source_target_pairs={{0,8},{4,12},{8,0},{12,4},{16,24},{20,28},{24,16},{28,20},{1,9},{5... | collective-permute-start | bytes 1572872 | tf_op jit(solution)/shard_map/ppermute | solution.py:14
  99.6 1.5 %collective-permute-start.22 = (bf16[512,512]{1,0:T(8,128)(2,1)S(1)}, bf16[512,512]{1,0:T(8,128)(2,1)S(1)}, u32[]{:S(2)}, u32[]{:S(2)}) collective-permute-start(bf16[512,512]{1,0:T(8,128)(2,1)S(1)} %get-tuple-element.38), channel_id=1, source_target_pairs={{0,16},{4,20},{8,24},{12,28},{16,0},{20,4},{24,8},{28,12},{1,17},{... | collective-permute-start | bytes 1572872 | tf_op jit(solution)/shard_map/ppermute | solution.py:14
  101.2 4.0 %collective-permute-done.16 = bf16[8,128,128]{2,1,0:T(8,128)(2,1)S(1)} collective-permute-done((bf16[8,128,128]{2,1,0:T(8,128)(2,1)S(1)}, bf16[8,128,128]{2,1,0:T(8,128)(2,1)S(1)}, u32[]{:S(2)}, u32[]{:S(2)}) %collective-permute-start.16) | collective-permute-done | bytes 262176 | tf_op jit(solution)/shard_map/ppermute | solution.py:14
  105.2 1.6 %collective-permute-start.17 = (bf16[8,128,128]{2,1,0:T(8,128)(2,1)S(1)}, bf16[8,128,128]{2,1,0:T(8,128)(2,1)S(1)}, u32[]{:S(2)}, u32[]{:S(2)}) collective-permute-start(bf16[8,128,128]{2,1,0:T(8,128)(2,1)S(1)} %fusion.70), channel_id=1, source_target_pairs={{0,16},{4,20},{8,24},{12,28},{16,0},{20,4},{24,8},{28,12},{1,17},{... | collective-permute-start | bytes 786440 | tf_op jit(solution)/shard_map/ppermute | solution.py:14
  107.7 8.7 %collective-permute-done.20 = bf16[512,512]{1,0:T(8,128)(2,1)S(1)} collective-permute-done((bf16[512,512]{1,0:T(8,128)(2,1)S(1)}, bf16[512,512]{1,0:T(8,128)(2,1)S(1)}, u32[]{:S(2)}, u32[]{:S(2)}) %collective-permute-start.20) | collective-permute-done | bytes 524320 | tf_op jit(solution)/shard_map/ppermute | solution.py:14
  116.4 1.5 %collective-permute-start.21 = (bf16[512,512]{1,0:T(8,128)(2,1)S(1)}, bf16[512,512]{1,0:T(8,128)(2,1)S(1)}, u32[]{:S(2)}, u32[]{:S(2)}) collective-permute-start(bf16[512,512]{1,0:T(8,128)(2,1)S(1)} %get-tuple-element.35), channel_id=1, source_target_pairs={{0,16},{4,20},{8,24},{12,28},{16,0},{20,4},{24,8},{28,12},{1,17},{... | collective-permute-start | bytes 1572872 | tf_op jit(solution)/shard_map/ppermute | solution.py:14
  120.0 1.3 collective-permute-start.27
  121.4 6.3 %collective-permute-done.19 = bf16[512,512]{1,0:T(8,128)(2,1)S(1)} collective-permute-done((bf16[512,512]{1,0:T(8,128)(2,1)S(1)}, bf16[512,512]{1,0:T(8,128)(2,1)S(1)}, u32[]{:S(2)}, u32[]{:S(2)}) %collective-permute-start.19) | collective-permute-done | bytes 524320 | tf_op jit(solution)/shard_map/ppermute | solution.py:14
  127.6 4.5 %collective-permute-start.25 = (bf16[2,192,1024]{2,1,0:T(8,128)(2,1)S(1)}, bf16[2,192,1024]{2,1,0:T(8,128)(2,1)S(1)}, u32[]{:S(2)}, u32[]{:S(2)}) collective-permute-start(bf16[2,192,1024]{2,1,0:T(8,128)(2,1)S(1)} %add_convert_fusion.4), channel_id=1, source_target_pairs={{0,1},{1,2},{2,3},{4,5},{5,6},{6,7},{8,9},{9,10},{10,11},{12,13},{... | collective-permute-start | bytes 2359304 | tf_op jit(solution)/shard_map/ppermute | solution.py:42
  132.2 9.1 %collective-permute-done.28 = bf16[512,512]{1,0:T(8,128)(2,1)S(1)} collective-permute-done((bf16[512,512]{1,0:T(8,128)(2,1)S(1)}, bf16[512,512]{1,0:T(8,128)(2,1)S(1)}, u32[]{:S(2)}, u32[]{:S(2)}) %collective-permute-start.28) | collective-permute-done | bytes 524320 | tf_op jit(solution)/shard_map/ppermute | solution.py:14
  142.3 1.1 copy.151
  143.4 1.6 %maximum_multiply_fusion = f32[1024,512]{1,0:T(8,128)} fusion(f32[512,512]{1,0:T(8,128)S(1)} %get-tuple-element.33, f32[512,512]{1,0:T(8,128)S(1)} %get-tuple-element.41), kind=kLoop, calls=%fused_computation.4 | loop fusion | flops 1048576 | bytes 4194304 | tf_op jit(solution)/shard_map/mul | solution.py:236
  145.3 2.9 %collective-permute-done.25 = bf16[2,192,1024]{2,1,0:T(8,128)(2,1)S(1)} collective-permute-done((bf16[2,192,1024]{2,1,0:T(8,128)(2,1)S(1)}, bf16[2,192,1024]{2,1,0:T(8,128)(2,1)S(1)}, u32[]{:S(2)}, u32[]{:S(2)}) %collective-permute-start.25) | collective-permute-done | bytes 786464 | tf_op jit(solution)/shard_map/ppermute | solution.py:42
  149.1 1.4 copy_bitcast_fusion
  150.4 1.3 add_convert_fusion.1
  (88 shorter events, 21.5 us)
Async XLA Ops:
  0.6 1.1 copy-start
  4.4 2.0 %collective-permute-start = (bf16[2,8,128,128]{3,2,1,0:T(8,128)(2,1)S(1)}, bf16[2,8,128,128]{3,2,1,0:T(8,128)(2,1)S(1)}, u32[]{:S(2)}, u32[]{:S(2)}) collective-permute-start(bf16[2,8,128,128]{3,2,1,0:T(8,128)(2,1)S(1)} %get-tuple-element.54), channel_id=1, source_target_pairs={{0,4},{4,0},{8,12},{12,8},{16,20},{20,16},{24,28},{28,24},{1,5},{5... | collective-permute-start | bytes 1572872 | tf_op jit(solution)/shard_map/ppermute | solution.py:14
  4.8 1.7 %copy-start.3 = (f32[2,8,128,128]{3,2,1,0:T(8,128)S(1)}, f32[2,8,128,128]{3,2,1,0:T(8,128)}, u32[]{:S(2)}) copy-start(f32[2,8,128,128]{3,2,1,0:T(8,128)} %get-tuple-element.55) | copy-start | bytes 3145732
  6.5 1.0 copy-start.4
  6.5 13.6 %copy-start.1 = (bf16[2,192,1024]{2,1,0:T(8,128)(2,1)S(1)}, bf16[2,192,1024]{2,1,0:T(8,128)(2,1)}, u32[]{:S(2)}) copy-start(bf16[2,192,1024]{2,1,0:T(8,128)(2,1)} %param.6) | copy-start | bytes 2359300
  6.5 13.6 %copy-start.2 = (bf16[2,192,1024]{2,1,0:T(8,128)(2,1)S(1)}, bf16[2,192,1024]{2,1,0:T(8,128)(2,1)}, u32[]{:S(2)}) copy-start(bf16[2,192,1024]{2,1,0:T(8,128)(2,1)} %param.5) | copy-start | bytes 2359300
  7.5 9.5 %collective-permute-start.1 = (bf16[8,128,128]{2,1,0:T(8,128)(2,1)S(1)}, bf16[8,128,128]{2,1,0:T(8,128)(2,1)S(1)}, u32[]{:S(2)}, u32[]{:S(2)}) collective-permute-start(bf16[8,128,128]{2,1,0:T(8,128)(2,1)S(1)} %fusion.95), channel_id=1, source_target_pairs={{0,8},{4,12},{8,0},{12,4},{16,24},{20,28},{24,16},{28,20},{1,9},{5... | collective-permute-start | bytes 786440 | tf_op jit(solution)/shard_map/ppermute | solution.py:14
  10.3 20.6 %collective-permute-start.4 = (bf16[2,192,1024]{2,1,0:T(8,128)(2,1)}, bf16[2,192,1024]{2,1,0:T(8,128)(2,1)}, u32[]{:S(2)}, u32[]{:S(2)}) collective-permute-start(bf16[2,192,1024]{2,1,0:T(8,128)(2,1)} %param.9), channel_id=1, source_target_pairs={{0,1},{1,2},{2,3},{4,5},{5,6},{6,7},{8,9},{9,10},{10,11},{12,13},{... | collective-permute-start | bytes 2359304 | tf_op jit(solution)/shard_map/ppermute | solution.py:42
  14.7 21.2 %collective-permute-start.5 = (bf16[2,192,1024]{2,1,0:T(8,128)(2,1)}, bf16[2,192,1024]{2,1,0:T(8,128)(2,1)}, u32[]{:S(2)}, u32[]{:S(2)}) collective-permute-start(bf16[2,192,1024]{2,1,0:T(8,128)(2,1)} %param.9), channel_id=1, source_target_pairs={{1,0},{2,1},{3,2},{5,4},{6,5},{7,6},{9,8},{10,9},{11,10},{13,12},{... | collective-permute-start | bytes 2359304 | tf_op jit(solution)/shard_map/ppermute | solution.py:46
  18.2 8.1 %copy-start.5 = (bf16[2,192,1024]{2,1,0:T(8,128)(2,1)S(1)}, bf16[2,192,1024]{2,1,0:T(8,128)(2,1)}, u32[]{:S(2)}) copy-start(bf16[2,192,1024]{2,1,0:T(8,128)(2,1)} %param.9) | copy-start | bytes 2359300
  18.2 7.9 %collective-permute-start.2 = (bf16[8,128,128]{2,1,0:T(8,128)(2,1)S(1)}, bf16[8,128,128]{2,1,0:T(8,128)(2,1)S(1)}, u32[]{:S(2)}, u32[]{:S(2)}) collective-permute-start(bf16[8,128,128]{2,1,0:T(8,128)(2,1)S(1)} %fusion.67), channel_id=1, source_target_pairs={{0,16},{4,20},{8,24},{12,28},{16,0},{20,4},{24,8},{28,12},{1,17},{... | collective-permute-start | bytes 786440 | tf_op jit(solution)/shard_map/ppermute | solution.py:14
  26.2 11.0 %collective-permute-start.3 = (bf16[8,128,128]{2,1,0:T(8,128)(2,1)S(1)}, bf16[8,128,128]{2,1,0:T(8,128)(2,1)S(1)}, u32[]{:S(2)}, u32[]{:S(2)}) collective-permute-start(bf16[8,128,128]{2,1,0:T(8,128)(2,1)S(1)} %fusion.66), channel_id=1, source_target_pairs={{0,4},{4,0},{8,12},{12,8},{16,20},{20,16},{24,28},{28,24},{1,5},{5... | collective-permute-start | bytes 786440 | tf_op jit(solution)/shard_map/ppermute | solution.py:14
  26.3 12.7 %slice-start = ((s8[8388608]{0:T(1024)(128)(4,1)}), s8[4194304]{0:T(1024)(128)(4,1)S(1)}, s32[]{:S(2)}) async-start(s8[8388608]{0:T(1024)(128)(4,1)} %bitcast.337), calls=%async_computation | async-start | bytes 8388608
  30.9 17.7 %collective-permute-start.6 = (bf16[2,192,1024]{2,1,0:T(8,128)(2,1)}, bf16[2,192,1024]{2,1,0:T(8,128)(2,1)S(1)}, u32[]{:S(2)}, u32[]{:S(2)}) collective-permute-start(bf16[2,192,1024]{2,1,0:T(8,128)(2,1)} %collective-permute-done.4), channel_id=1, source_target_pairs={{1,2},{2,3},{5,6},{6,7},{9,10},{10,11},{13,14},{14,15},{17,18},{18... | collective-permute-start | bytes 2359304 | tf_op jit(solution)/shard_map/ppermute | solution.py:42
  35.9 20.2 %collective-permute-start.7 = (bf16[2,192,1024]{2,1,0:T(8,128)(2,1)}, bf16[2,192,1024]{2,1,0:T(8,128)(2,1)S(1)}, u32[]{:S(2)}, u32[]{:S(2)}) collective-permute-start(bf16[2,192,1024]{2,1,0:T(8,128)(2,1)} %collective-permute-done.5), channel_id=1, source_target_pairs={{1,0},{2,1},{5,4},{6,5},{9,8},{10,9},{13,12},{14,13},{17,16},{18,1... | collective-permute-start | bytes 2359304 | tf_op jit(solution)/shard_map/ppermute | solution.py:46
  37.3 2.2 %slice-start.1 = ((s8[8388608]{0:T(1024)(128)(4,1)}), s8[4194304]{0:T(1024)(128)(4,1)S(1)}, s32[]{:S(2)}) async-start(s8[8388608]{0:T(1024)(128)(4,1)} %bitcast.337), calls=%async_computation.1 | async-start | bytes 8388608
  40.5 26.8 %collective-permute-start.13 = (bf16[2,192,1024]{2,1,0:T(8,128)(2,1)S(1)}, bf16[2,192,1024]{2,1,0:T(8,128)(2,1)S(1)}, u32[]{:S(2)}, u32[]{:S(2)}) collective-permute-start(bf16[2,192,1024]{2,1,0:T(8,128)(2,1)S(1)} %get-tuple-element.58), channel_id=1, source_target_pairs={{0,1},{4,5},{8,9},{12,13},{16,17},{20,21},{24,25},{28,29}} | collective-permute-start | bytes 2359304 | tf_op jit(solution)/shard_map/ppermute | solution.py:42
  46.0 21.2 %collective-permute-start.14 = (bf16[2,192,1024]{2,1,0:T(8,128)(2,1)S(1)}, bf16[2,192,1024]{2,1,0:T(8,128)(2,1)S(1)}, u32[]{:S(2)}, u32[]{:S(2)}) collective-permute-start(bf16[2,192,1024]{2,1,0:T(8,128)(2,1)S(1)} %get-tuple-element.60), channel_id=1, source_target_pairs={{3,2},{7,6},{11,10},{15,14},{19,18},{23,22},{27,26},{31,30}} | collective-permute-start | bytes 2359304 | tf_op jit(solution)/shard_map/ppermute | solution.py:46
  47.5 15.2 %collective-permute-start.10 = (bf16[1024,512]{1,0:T(8,128)(2,1)S(1)}, bf16[1024,512]{1,0:T(8,128)(2,1)S(1)}, u32[]{:S(2)}, u32[]{:S(2)}) collective-permute-start(bf16[1024,512]{1,0:T(8,128)(2,1)S(1)} %bitcast_convert_fusion.3), channel_id=1, source_target_pairs={{0,4},{4,0},{8,12},{12,8},{16,20},{20,16},{24,28},{28,24},{1,5},{5... | collective-permute-start | bytes 3145736 | tf_op jit(solution)/shard_map/ppermute | solution.py:14
  58.3 5.2 %collective-permute-start.12 = (bf16[1024,512]{1,0:T(8,128)(2,1)S(1)}, bf16[1024,512]{1,0:T(8,128)(2,1)S(1)}, u32[]{:S(2)}, u32[]{:S(2)}) collective-permute-start(bf16[1024,512]{1,0:T(8,128)(2,1)S(1)} %bitcast_convert_fusion.1), channel_id=1, source_target_pairs={{0,4},{4,0},{8,12},{12,8},{16,20},{20,16},{24,28},{28,24},{1,5},{5... | collective-permute-start | bytes 3145736 | tf_op jit(solution)/shard_map/ppermute | solution.py:14
  60.1 6.4 %collective-permute-start.11 = (bf16[1024,512]{1,0:T(8,128)(2,1)S(1)}, bf16[1024,512]{1,0:T(8,128)(2,1)S(1)}, u32[]{:S(2)}, u32[]{:S(2)}) collective-permute-start(bf16[1024,512]{1,0:T(8,128)(2,1)S(1)} %bitcast_convert_fusion.2), channel_id=1, source_target_pairs={{0,4},{4,0},{8,12},{12,8},{16,20},{20,16},{24,28},{28,24},{1,5},{5... | collective-permute-start | bytes 3145736 | tf_op jit(solution)/shard_map/ppermute | solution.py:14
  62.8 4.5 %collective-permute-start.8 = (bf16[2,192,1024]{2,1,0:T(8,128)(2,1)S(1)}, bf16[2,192,1024]{2,1,0:T(8,128)(2,1)S(1)}, u32[]{:S(2)}, u32[]{:S(2)}) collective-permute-start(bf16[2,192,1024]{2,1,0:T(8,128)(2,1)S(1)} %collective-permute-done.6), channel_id=1, source_target_pairs={{2,3},{6,7},{10,11},{14,15},{18,19},{22,23},{26,27},{30,31}} | collective-permute-start | bytes 2359304 | tf_op jit(solution)/shard_map/ppermute | solution.py:42
  63.5 21.4 %collective-permute-start.9 = (bf16[2,192,1024]{2,1,0:T(8,128)(2,1)S(1)}, bf16[2,192,1024]{2,1,0:T(8,128)(2,1)S(1)}, u32[]{:S(2)}, u32[]{:S(2)}) collective-permute-start(bf16[2,192,1024]{2,1,0:T(8,128)(2,1)S(1)} %collective-permute-done.7), channel_id=1, source_target_pairs={{1,0},{5,4},{9,8},{13,12},{17,16},{21,20},{25,24},{29,28}} | collective-permute-start | bytes 2359304 | tf_op jit(solution)/shard_map/ppermute | solution.py:46
  90.2 6.3 %collective-permute-start.18 = (bf16[1024,512]{1,0:T(8,128)(2,1)S(1)}, bf16[1024,512]{1,0:T(8,128)(2,1)S(1)}, u32[]{:S(2)}, u32[]{:S(2)}) collective-permute-start(bf16[1024,512]{1,0:T(8,128)(2,1)S(1)} %bitcast_convert_fusion), channel_id=1, source_target_pairs={{0,4},{4,0},{8,12},{12,8},{16,20},{20,16},{24,28},{28,24},{1,5},{5... | collective-permute-start | bytes 3145736 | tf_op jit(solution)/shard_map/ppermute | solution.py:14
  90.8 16.1 %collective-permute-start.26 = (bf16[2,192,1024]{2,1,0:T(8,128)(2,1)S(1)}, bf16[2,192,1024]{2,1,0:T(8,128)(2,1)S(1)}, u32[]{:S(2)}, u32[]{:S(2)}) collective-permute-start(bf16[2,192,1024]{2,1,0:T(8,128)(2,1)S(1)} %get-tuple-element.43), channel_id=1, source_target_pairs={{2,1},{3,2},{6,5},{7,6},{10,9},{11,10},{14,13},{15,14},{18,17},{19... | collective-permute-start | bytes 2359304 | tf_op jit(solution)/shard_map/ppermute | solution.py:46
  91.5 27.4 %collective-permute-start.24 = (bf16[2,192,1024]{2,1,0:T(8,128)(2,1)S(1)}, bf16[2,192,1024]{2,1,0:T(8,128)(2,1)S(1)}, u32[]{:S(2)}, u32[]{:S(2)}) collective-permute-start(bf16[2,192,1024]{2,1,0:T(8,128)(2,1)S(1)} %get-tuple-element.44), channel_id=1, source_target_pairs={{0,1},{1,2},{4,5},{5,6},{8,9},{9,10},{12,13},{13,14},{16,17},{17,1... | collective-permute-start | bytes 2359304 | tf_op jit(solution)/shard_map/ppermute | solution.py:42
  93.6 2.2 %collective-permute-start.15 = (bf16[2,8,128,128]{3,2,1,0:T(8,128)(2,1)S(1)}, bf16[2,8,128,128]{3,2,1,0:T(8,128)(2,1)S(1)}, u32[]{:S(2)}, u32[]{:S(2)}) collective-permute-start(bf16[2,8,128,128]{3,2,1,0:T(8,128)(2,1)S(1)} %get-tuple-element.62), channel_id=1, source_target_pairs={{0,4},{4,0},{8,12},{12,8},{16,20},{20,16},{24,28},{28,24},{1,5},{5... | collective-permute-start | bytes 1572872 | tf_op jit(solution)/shard_map/ppermute | solution.py:14
  96.0 9.2 %collective-permute-start.16 = (bf16[8,128,128]{2,1,0:T(8,128)(2,1)S(1)}, bf16[8,128,128]{2,1,0:T(8,128)(2,1)S(1)}, u32[]{:S(2)}, u32[]{:S(2)}) collective-permute-start(bf16[8,128,128]{2,1,0:T(8,128)(2,1)S(1)} %fusion.96), channel_id=1, source_target_pairs={{0,8},{4,12},{8,0},{12,4},{16,24},{20,28},{24,16},{28,20},{1,9},{5... | collective-permute-start | bytes 786440 | tf_op jit(solution)/shard_map/ppermute | solution.py:14
  98.1 18.3 %collective-permute-start.20 = (bf16[512,512]{1,0:T(8,128)(2,1)S(1)}, bf16[512,512]{1,0:T(8,128)(2,1)S(1)}, u32[]{:S(2)}, u32[]{:S(2)}) collective-permute-start(bf16[512,512]{1,0:T(8,128)(2,1)S(1)} %get-tuple-element.36), channel_id=1, source_target_pairs={{0,8},{4,12},{8,0},{12,4},{16,24},{20,28},{24,16},{28,20},{1,9},{5... | collective-permute-start | bytes 1572872 | tf_op jit(solution)/shard_map/ppermute | solution.py:14
  99.6 18.3 %collective-permute-start.22 = (bf16[512,512]{1,0:T(8,128)(2,1)S(1)}, bf16[512,512]{1,0:T(8,128)(2,1)S(1)}, u32[]{:S(2)}, u32[]{:S(2)}) collective-permute-start(bf16[512,512]{1,0:T(8,128)(2,1)S(1)} %get-tuple-element.38), channel_id=1, source_target_pairs={{0,16},{4,20},{8,24},{12,28},{16,0},{20,4},{24,8},{28,12},{1,17},{... | collective-permute-start | bytes 1572872 | tf_op jit(solution)/shard_map/ppermute | solution.py:14
  105.2 14.7 %collective-permute-start.17 = (bf16[8,128,128]{2,1,0:T(8,128)(2,1)S(1)}, bf16[8,128,128]{2,1,0:T(8,128)(2,1)S(1)}, u32[]{:S(2)}, u32[]{:S(2)}) collective-permute-start(bf16[8,128,128]{2,1,0:T(8,128)(2,1)S(1)} %fusion.70), channel_id=1, source_target_pairs={{0,16},{4,20},{8,24},{12,28},{16,0},{20,4},{24,8},{28,12},{1,17},{... | collective-permute-start | bytes 786440 | tf_op jit(solution)/shard_map/ppermute | solution.py:14
  107.1 20.5 %collective-permute-start.19 = (bf16[512,512]{1,0:T(8,128)(2,1)S(1)}, bf16[512,512]{1,0:T(8,128)(2,1)S(1)}, u32[]{:S(2)}, u32[]{:S(2)}) collective-permute-start(bf16[512,512]{1,0:T(8,128)(2,1)S(1)} %get-tuple-element.37), channel_id=1, source_target_pairs={{0,8},{4,12},{8,0},{12,4},{16,24},{20,28},{24,16},{28,20},{1,9},{5... | collective-permute-start | bytes 1572872 | tf_op jit(solution)/shard_map/ppermute | solution.py:14
  116.4 15.8 %collective-permute-start.21 = (bf16[512,512]{1,0:T(8,128)(2,1)S(1)}, bf16[512,512]{1,0:T(8,128)(2,1)S(1)}, u32[]{:S(2)}, u32[]{:S(2)}) collective-permute-start(bf16[512,512]{1,0:T(8,128)(2,1)S(1)} %get-tuple-element.35), channel_id=1, source_target_pairs={{0,16},{4,20},{8,24},{12,28},{16,0},{20,4},{24,8},{28,12},{1,17},{... | collective-permute-start | bytes 1572872 | tf_op jit(solution)/shard_map/ppermute | solution.py:14
  118.2 23.1 %collective-permute-start.28 = (bf16[512,512]{1,0:T(8,128)(2,1)S(1)}, bf16[512,512]{1,0:T(8,128)(2,1)S(1)}, u32[]{:S(2)}, u32[]{:S(2)}) collective-permute-start(bf16[512,512]{1,0:T(8,128)(2,1)S(1)} %get-tuple-element.40), channel_id=1, source_target_pairs={{0,16},{4,20},{8,24},{12,28},{16,0},{20,4},{24,8},{28,12},{1,17},{... | collective-permute-start | bytes 1572872 | tf_op jit(solution)/shard_map/ppermute | solution.py:14
  118.8 22.5 %collective-permute-start.29 = (bf16[512,512]{1,0:T(8,128)(2,1)S(1)}, bf16[512,512]{1,0:T(8,128)(2,1)S(1)}, u32[]{:S(2)}, u32[]{:S(2)}) collective-permute-start(bf16[512,512]{1,0:T(8,128)(2,1)S(1)} %get-tuple-element.39), channel_id=1, source_target_pairs={{0,8},{4,12},{8,0},{12,4},{16,24},{20,28},{24,16},{28,20},{1,9},{5... | collective-permute-start | bytes 1572872 | tf_op jit(solution)/shard_map/ppermute | solution.py:14
  120.0 25.3 %collective-permute-start.27 = (bf16[2,192,1024]{2,1,0:T(8,128)(2,1)S(1)}, bf16[2,192,1024]{2,1,0:T(8,128)(2,1)S(1)}, u32[]{:S(2)}, u32[]{:S(2)}) collective-permute-start(bf16[2,192,1024]{2,1,0:T(8,128)(2,1)S(1)} %add_convert_fusion.2), channel_id=1, source_target_pairs={{1,0},{2,1},{3,2},{5,4},{6,5},{7,6},{9,8},{10,9},{11,10},{13,12},{... | collective-permute-start | bytes 2359304 | tf_op jit(solution)/shard_map/ppermute | solution.py:46
  127.6 20.5 %collective-permute-start.25 = (bf16[2,192,1024]{2,1,0:T(8,128)(2,1)S(1)}, bf16[2,192,1024]{2,1,0:T(8,128)(2,1)S(1)}, u32[]{:S(2)}, u32[]{:S(2)}) collective-permute-start(bf16[2,192,1024]{2,1,0:T(8,128)(2,1)S(1)} %add_convert_fusion.4), channel_id=1, source_target_pairs={{0,1},{1,2},{2,3},{4,5},{5,6},{6,7},{8,9},{9,10},{10,11},{12,13},{... | collective-permute-start | bytes 2359304 | tf_op jit(solution)/shard_map/ppermute | solution.py:42
  141.8 3.2 %collective-permute-start.23 = (bf16[8,128,128]{2,1,0:T(8,128)(2,1)S(1)}, bf16[8,128,128]{2,1,0:T(8,128)(2,1)S(1)}, u32[]{:S(2)}, u32[]{:S(2)}) collective-permute-start(bf16[8,128,128]{2,1,0:T(8,128)(2,1)S(1)} %fusion.69), channel_id=1, source_target_pairs={{0,4},{4,0},{8,12},{12,8},{16,20},{20,16},{24,28},{28,24},{1,5},{5... | collective-permute-start | bytes 786440 | tf_op jit(solution)/shard_map/ppermute | solution.py:14
